TPU v7x, 512 devices: a whole 4x4x16 slice. The times are simulated.
512 devices in a mesh: seq: 256 (over x, y, z), head: 2 (over core).
Axes of the slice: x: 4, y: 4, z: 16, core: 2. Of those that a mesh axis runs over, the one named last changes fastest.
Arguments:
- queries: bfloat16 [65536, 1024], P('seq', 'head'), may hold values from -6 to 6
- key_rows: bfloat16 [65536, 1024], P('seq', 'head'), may hold values from -6 to 6
- value_rows: bfloat16 [65536, 1024], P('seq', 'head'), may hold values from -6 to 6
- out_weight: bfloat16 [1024, 1024], P('head'), may hold values from -0.1875 to 0.1875
Outputs:
- layer_output: bfloat16 [65536, 1024], P('seq', 'head')
All inputs are finite; a program needn't handle non-finite values.
Results may differ from a plain program's by a relative error of at most 0.015.
Values may be sent and summed in bfloat16 or wider, within the bound.
No kernel may reach another device: no remote copies, remote signals or barrier semaphores. Data moves between devices by JAX's collectives and lax.ppermute only.
A program may use at most 64 MiB of HBM per device.

v0:
```python
from functools import reduce

import jax
import jax.numpy as jnp
from jax import lax
from jax.sharding import PartitionSpec as P

HEAD_DIM = 64
BLOCK = 128
LEVELS = 5


def swapped(block, axis, apart):
    count = lax.axis_size(axis)
    route = []
    for low in range(count):
        high = low | 1 << apart
        if high != low and high < count:
            route += [(low, high), (high, low)]
    return lax.ppermute(block, axis, route)


def attend(query_blk, key_blk, value_blk, score_scale):
    scores = (
        jnp.einsum("nqhe,nkhe->nhqk", query_blk, key_blk, preferred_element_type=jnp.float32)
        * score_scale
    )
    row_max = jnp.max(scores, axis=-1)
    weights = jnp.exp(scores - row_max[..., None])
    row_total = jnp.sum(weights, axis=-1)
    weighted = jnp.einsum(
        "nhqk,nkhe->nqhe",
        weights.astype(jnp.bfloat16),
        value_blk,
        preferred_element_type=jnp.float32,
    )
    blocks_in, head_count, query_count = row_max.shape
    flat_rows = blocks_in * query_count
    return (
        jnp.transpose(row_max, (0, 2, 1)).reshape(flat_rows, head_count),
        jnp.transpose(row_total, (0, 2, 1)).reshape(flat_rows, head_count),
        weighted.reshape(flat_rows, head_count, value_blk.shape[-1]),
    )


def coarse(field, factor):
    if factor == 1:
        return field
    row_count, head_count, head_size = field.shape
    merged = field.astype(jnp.float32).reshape(row_count // factor, factor, head_count, head_size)
    return jnp.mean(merged, axis=1).astype(jnp.bfloat16)


def body(queries, key_rows, value_rows, out_weight):
    tok_rows, feat_width = queries.shape
    local_heads = feat_width // HEAD_DIM
    score_scale = HEAD_DIM ** (-0.5)
    cube_shape = (tok_rows, local_heads, HEAD_DIM)
    query_cube = queries.reshape(cube_shape)
    key_cube = key_rows.reshape(cube_shape)
    value_cube = value_rows.reshape(cube_shape)
    blocks_in = tok_rows // BLOCK
    block_shape = (blocks_in, BLOCK, local_heads, HEAD_DIM)
    terms = [
        (
            1,
            attend(
                query_cube.reshape(block_shape),
                key_cube.reshape(block_shape),
                value_cube.reshape(block_shape),
                score_scale,
            ),
        )
    ]
    remote = []
    for depth_no in range(1, LEVELS + 1):
        factor = 2 ** (depth_no - 1)
        coarse_q = coarse(query_cube, factor)
        coarse_k = coarse(key_cube, factor)
        coarse_v = coarse(value_cube, factor)
        if 2 * BLOCK * factor <= tok_rows:
            pair_count = coarse_q.shape[0] // BLOCK
            pair_shape = (pair_count // 2, 2, BLOCK, local_heads, HEAD_DIM)
            flat_shape = (pair_count, BLOCK, local_heads, HEAD_DIM)
            key_blk = coarse_k.reshape(pair_shape)[:, ::-1].reshape(flat_shape)
            value_blk = coarse_v.reshape(pair_shape)[:, ::-1].reshape(flat_shape)
            terms.append(
                (factor, attend(coarse_q.reshape(flat_shape), key_blk, value_blk, score_scale))
            )
        else:
            remote.append((factor, coarse_q, jnp.concatenate((coarse_k, coarse_v), axis=2)))
    remote_count = len(remote)
    fetched = []
    for level_no in range(remote_count):
        received = swapped(remote[level_no][2], "seq", level_no)
        for bit_no in range(level_no):
            received = jnp.concatenate((received, swapped(received, "seq", bit_no)), axis=0)
        fetched.append(received)
    for (factor, coarse_q, own_pairs), received in zip(remote, fetched):
        key_blk = received[:, :, :HEAD_DIM][None]
        value_blk = received[:, :, HEAD_DIM:][None]
        terms.append((factor, attend(coarse_q[None], key_blk, value_blk, score_scale)))
    spread = []
    for factor, (row_max, row_total, weighted) in terms:
        spread.append(
            (
                factor,
                jnp.repeat(row_max, factor, axis=0),
                jnp.repeat(row_total, factor, axis=0),
                jnp.repeat(weighted, factor, axis=0),
            )
        )
    highest = reduce(jnp.maximum, [entry[1] for entry in spread])
    denominator = jnp.zeros((tok_rows, local_heads), jnp.float32)
    numerator = jnp.zeros(cube_shape, jnp.float32)
    for factor, row_max, row_total, weighted in spread:
        rescale = factor * jnp.exp(row_max - highest)
        denominator = denominator + rescale * row_total
        numerator = numerator + rescale[..., None] * weighted
    attention = (
        (numerator / denominator[..., None]).astype(jnp.bfloat16).reshape(tok_rows, feat_width)
    )
    partial_value = jnp.dot(attention, out_weight, preferred_element_type=jnp.float32)
    return lax.psum_scatter(
        partial_value.astype(jnp.bfloat16), "head", scatter_dimension=1, tiled=True
    )


def solution(mesh):
    placed = (P("seq", "head"), P("seq", "head"), P("seq", "head"), P("head", None))
    return jax.shard_map(
        body, mesh=mesh, in_specs=placed, out_specs=P("seq", "head"), check_vma=False
    )
```

profile of v0, /device:TPU:1, one launch (start us, length us, event | category | flops | bytes accessed | tf_op | source)
XLA Modules:
  0.0 190.4 jit_solution(16794931403884500409)
XLA Ops:
  6.5 1.3 reshape.473
  8.1 0.8 copy-done.2
  9.5 0.8 pad_maximum_fusion.1
  10.3 5.7 %collective-permute-start.1 = (bf16[64,8,128]{0,2,1:T(8,128)(2,1)}, bf16[64,8,128]{0,2,1:T(8,128)(2,1)}, u32[]{:S(2)}, u32[]{:S(2)}) collective-permute-start(bf16[64,8,128]{0,2,1:T(8,128)(2,1)} %pad_maximum_fusion.1), channel_id=1, source_target_pairs={{0,4},{4,0},{2,6},{6,2},{8,12},{12,8},{10,14},{14,10},{16,20},{20,... | collective-permute-start | bytes 393224 | tf_op jit(solution)/shard_map/ppermute | solution.py:20
  16.0 1.2 reshape.476
  17.5 1.3 reduce_sum.177
  19.0 0.9 copy.150
  19.9 8.8 %collective-permute-start.3 = (bf16[32,8,128]{0,2,1:T(8,128)(2,1)}, bf16[32,8,128]{0,2,1:T(8,128)(2,1)}, u32[]{:S(2)}, u32[]{:S(2)}) collective-permute-start(bf16[32,8,128]{0,2,1:T(8,128)(2,1)} %copy.150), channel_id=1, source_target_pairs={{0,8},{8,0},{2,10},{10,2},{4,12},{12,4},{6,14},{14,6},{16,24},{24,... | collective-permute-start | bytes 196616 | tf_op jit(solution)/shard_map/ppermute | solution.py:20
  28.7 1.2 reshape.479
  30.1 1.3 reduce_sum.180
  31.6 0.9 copy.152
  32.5 8.8 %collective-permute-start.6 = (bf16[16,8,128]{0,2,1:T(8,128)(2,1)}, bf16[16,8,128]{0,2,1:T(8,128)(2,1)}, u32[]{:S(2)}, u32[]{:S(2)}) collective-permute-start(bf16[16,8,128]{0,2,1:T(8,128)(2,1)} %copy.152), channel_id=1, source_target_pairs={{0,16},{16,0},{2,18},{18,2},{4,20},{20,4},{6,22},{22,6},{8,24},{24... | collective-permute-start | bytes 98312 | tf_op jit(solution)/shard_map/ppermute | solution.py:20
  41.3 1.2 reshape.470
  42.8 1.4 reduce_sum.171
  44.8 0.7 pad_maximum_fusion
  45.6 2.6 %collective-permute-start = (bf16[128,8,128]{0,2,1:T(8,128)(2,1)}, bf16[128,8,128]{0,2,1:T(8,128)(2,1)}, u32[]{:S(2)}, u32[]{:S(2)}) collective-permute-start(bf16[128,8,128]{0,2,1:T(8,128)(2,1)} %pad_maximum_fusion), channel_id=1, source_target_pairs={{0,2},{2,0},{4,6},{6,4},{8,10},{10,8},{12,14},{14,12},{16,18},{18,... | collective-permute-start | bytes 786440 | tf_op jit(solution)/shard_map/ppermute | solution.py:20
  48.8 1.1 reshape.482
  50.1 1.2 reshape.475
  51.4 2.2 %rev.6 = bf16[1,2,128,8,64]{2,1,4,3,0:T(2,128)(2,1)} reverse(bf16[1,2,128,8,64]{2,1,4,3,0:T(2,128)(2,1)S(1)} %reshape_reshape.18), dimensions={1} | reverse | bytes 524288 | tf_op jit(solution)/shard_map/rev | solution.py:85
  53.7 2.1 %rev.7 = bf16[1,2,128,8,64]{2,1,4,3,0:T(2,128)(2,1)} reverse(bf16[1,2,128,8,64]{2,1,4,3,0:T(2,128)(2,1)S(1)} %reshape_reshape.20), dimensions={1} | reverse | bytes 524288 | tf_op jit(solution)/shard_map/rev | solution.py:86
  57.2 1.3 fusion.69
  58.5 1.3 reduce_sum.176
  59.9 2.2 %convolution_bitcast_fusion.1 = f32[2,128,8,64]{1,3,2,0:T(8,128)} fusion(f32[2,8,128,128]{2,3,1,0:T(8,128)S(1)} %get-tuple-element.23, bf16[2,128,8,64]{3,2,1,0:T(8,128)(2,1)} %reshape.482, f32[2,8,128]{2,1,0:T(8,128)S(1)} %get-tuple-element.22), kind=kOutput, calls=%fused_computation.5 | convolution fusion | flops 34078720 | bytes 1843200 | tf_op jit(solution)/shard_map/nhqk,nkhe->nqhe/dot_general | solution.py:31
  62.1 1.1 convolution_bitcast_fusion
  63.1 0.6 multiply_convert_fusion.10
  63.8 1.2 reshape.478
  65.0 1.3 reduce_sum.179
  66.3 2.6 %collective-permute-start.7 = (bf16[16,8,128]{0,2,1:T(8,128)(2,1)}, bf16[16,8,128]{0,2,1:T(8,128)(2,1)S(1)}, u32[]{:S(2)}, u32[]{:S(2)}) collective-permute-start(bf16[16,8,128]{0,2,1:T(8,128)(2,1)} %collective-permute-done.6), channel_id=1, source_target_pairs={{0,2},{2,0},{4,6},{6,4},{8,10},{10,8},{12,14},{14,12},{16,18},{18,... | collective-permute-start | bytes 98312 | tf_op jit(solution)/shard_map/ppermute | solution.py:20
  68.9 0.6 multiply_convert_fusion.13
  69.6 2.6 %collective-permute-start.4 = (bf16[32,8,128]{0,2,1:T(8,128)(2,1)}, bf16[32,8,128]{0,2,1:T(8,128)(2,1)S(1)}, u32[]{:S(2)}, u32[]{:S(2)}) collective-permute-start(bf16[32,8,128]{0,2,1:T(8,128)(2,1)} %collective-permute-done.3), channel_id=1, source_target_pairs={{0,2},{2,0},{4,6},{6,4},{8,10},{10,8},{12,14},{14,12},{16,18},{18,... | collective-permute-start | bytes 196616 | tf_op jit(solution)/shard_map/ppermute | solution.py:20
  72.2 8.4 %collective-permute-done.7 = bf16[16,8,128]{0,2,1:T(8,128)(2,1)S(1)} collective-permute-done((bf16[16,8,128]{0,2,1:T(8,128)(2,1)}, bf16[16,8,128]{0,2,1:T(8,128)(2,1)S(1)}, u32[]{:S(2)}, u32[]{:S(2)}) %collective-permute-start.7) | collective-permute-done | bytes 32800 | tf_op jit(solution)/shard_map/ppermute | solution.py:20
  80.6 1.9 pad_maximum_fusion.4
  82.5 14.5 %collective-permute-start.8 = (bf16[32,8,128]{0,2,1:T(8,128)(2,1)}, bf16[32,8,128]{0,2,1:T(8,128)(2,1)}, u32[]{:S(2)}, u32[]{:S(2)}) collective-permute-start(bf16[32,8,128]{0,2,1:T(8,128)(2,1)} %pad_maximum_fusion.4), channel_id=1, source_target_pairs={{0,4},{4,0},{2,6},{6,2},{8,12},{12,8},{10,14},{14,10},{16,20},{20,... | collective-permute-start | bytes 196616 | tf_op jit(solution)/shard_map/ppermute | solution.py:20
  97.0 1.9 pad_maximum_fusion.2
  98.9 3.7 %collective-permute-start.5 = (bf16[64,8,128]{0,2,1:T(8,128)(2,1)}, bf16[64,8,128]{0,2,1:T(8,128)(2,1)}, u32[]{:S(2)}, u32[]{:S(2)}) collective-permute-start(bf16[64,8,128]{0,2,1:T(8,128)(2,1)} %pad_maximum_fusion.2), channel_id=1, source_target_pairs={{0,4},{4,0},{2,6},{6,2},{8,12},{12,8},{10,14},{14,10},{16,20},{20,... | collective-permute-start | bytes 393224 | tf_op jit(solution)/shard_map/ppermute | solution.py:20
  102.6 1.0 fusion
  104.0 2.3 %copy.157 = f32[2,128,8,64]{1,0,3,2:T(2,128)} copy(f32[2,128,8,64]{1,3,2,0:T(8,128)} %convolution_bitcast_fusion.1) | data formatting | bytes 1048576 | tf_op jit(solution)/shard_map/nhqk,nkhe->nqhe/transpose | solution.py:31
  106.3 1.2 copy.161
  108.0 0.9 copy.139
  109.0 5.2 %collective-permute-done.8 = bf16[32,8,128]{0,2,1:T(8,128)(2,1)} collective-permute-done((bf16[32,8,128]{0,2,1:T(8,128)(2,1)}, bf16[32,8,128]{0,2,1:T(8,128)(2,1)}, u32[]{:S(2)}, u32[]{:S(2)}) %collective-permute-start.8) | collective-permute-done | bytes 65568 | tf_op jit(solution)/shard_map/ppermute | solution.py:20
  114.1 2.0 %pad_maximum_fusion.5 = bf16[64,8,128]{0,2,1:T(8,128)(2,1)} fusion(bf16[32,8,128]{0,2,1:T(8,128)(2,1)} %collective-permute-done.8, bf16[16,8,128]{0,2,1:T(8,128)(2,1)S(1)} %copy-done.5, bf16[16,8,128]{0,2,1:T(8,128)(2,1)} %collective-permute-done.6), kind=kLoop, calls=%fused_computation.46 | loop fusion | flops 393216 | bytes 262144 | tf_op jit(solution)/shard_map/concatenate | solution.py:97
  116.1 2.0 %collective-permute-start.9 = (bf16[64,8,128]{0,2,1:T(8,128)(2,1)}, bf16[64,8,128]{0,2,1:T(8,128)(2,1)}, u32[]{:S(2)}, u32[]{:S(2)}) collective-permute-start(bf16[64,8,128]{0,2,1:T(8,128)(2,1)} %pad_maximum_fusion.5), channel_id=1, source_target_pairs={{0,8},{8,0},{2,10},{10,2},{4,12},{12,4},{6,14},{14,6},{16,24},{24,... | collective-permute-start | bytes 393224 | tf_op jit(solution)/shard_map/ppermute | solution.py:20
  118.2 3.6 %collective-permute-start.2 = (bf16[64,8,128]{0,2,1:T(8,128)(2,1)}, bf16[64,8,128]{0,2,1:T(8,128)(2,1)S(1)}, u32[]{:S(2)}, u32[]{:S(2)}) collective-permute-start(bf16[64,8,128]{0,2,1:T(8,128)(2,1)} %collective-permute-done.1), channel_id=1, source_target_pairs={{0,2},{2,0},{4,6},{6,4},{8,10},{10,8},{12,14},{14,12},{16,18},{18,... | collective-permute-start | bytes 393224 | tf_op jit(solution)/shard_map/ppermute | solution.py:20
  121.8 1.3 pad_maximum_fusion.3
  123.3 0.9 convolution_bitcast_fusion.4
  124.2 3.8 %collective-permute-done.2 = bf16[64,8,128]{0,2,1:T(8,128)(2,1)S(1)} collective-permute-done((bf16[64,8,128]{0,2,1:T(8,128)(2,1)}, bf16[64,8,128]{0,2,1:T(8,128)(2,1)S(1)}, u32[]{:S(2)}, u32[]{:S(2)}) %collective-permute-start.2) | collective-permute-done | bytes 131104 | tf_op jit(solution)/shard_map/ppermute | solution.py:20
  128.0 1.3 fusion.67
  129.3 1.2 convolution_bitcast_fusion.3
  131.1 0.7 copy.176
  131.8 0.6 copy.149
  133.0 0.7 copy-done.15
  133.8 0.6 copy-done.19
  134.5 0.7 reshape.449
  135.9 1.0 copy.170
  137.0 9.5 %collective-permute-done.9 = bf16[64,8,128]{0,2,1:T(8,128)(2,1)} collective-permute-done((bf16[64,8,128]{0,2,1:T(8,128)(2,1)}, bf16[64,8,128]{0,2,1:T(8,128)(2,1)}, u32[]{:S(2)}, u32[]{:S(2)}) %collective-permute-start.9) | collective-permute-done | bytes 131104 | tf_op jit(solution)/shard_map/ppermute | solution.py:20
  146.4 1.5 pad_maximum_fusion.6
  149.3 1.0 copy.172
  150.3 1.2 fusion.68
  152.0 0.7 copy.143
  152.7 1.1 convolution_bitcast_fusion.2
  154.5 1.0 copy.165
  155.8 1.6 fusion.16
  157.5 1.3 convolution_convert_fusion
  158.8 24.8 %reduce-scatter.2.cloned.1.call-done = bf16[256,512]{1,0:T(8,128)(2,1)} async-done(((bf16[256,1024]{1,0:T(8,128)(2,1)}), bf16[256,512]{1,0:T(8,128)(2,1)}) %reduce-scatter.2.cloned.1.call-update) | async-done | bytes 262160 | tf_op jit(solution)/shard_map/reduce_scatter | solution.py:124
  (126 shorter events, 10.8 us)
Async XLA Ops:
  6.5 150.9 %copy-start = (bf16[512,1024]{1,0:T(8,128)(2,1)S(1)}, bf16[512,1024]{1,0:T(8,128)(2,1)}, u32[]{:S(2)}) copy-start(bf16[512,1024]{1,0:T(8,128)(2,1)} %param.7) | copy-start | bytes 3145732
  6.5 177.0 %reduce-scatter.2.cloned.1.call-start = ((), (), s32[]{:S(2)}) async-start(), calls=%async_computation.1 | async-start | bytes 786432 | tf_op jit(solution)/shard_map/reduce_scatter | solution.py:124
  8.0 1.0 copy-start.2
  9.5 6.5 %copy-start.1 = (bf16[256,512]{1,0:T(8,128)(2,1)S(1)}, bf16[256,512]{1,0:T(8,128)(2,1)}, u32[]{:S(2)}) copy-start(bf16[256,512]{1,0:T(8,128)(2,1)} %param.5) | copy-start | bytes 786436
  10.3 107.9 %collective-permute-start.1 = (bf16[64,8,128]{0,2,1:T(8,128)(2,1)}, bf16[64,8,128]{0,2,1:T(8,128)(2,1)}, u32[]{:S(2)}, u32[]{:S(2)}) collective-permute-start(bf16[64,8,128]{0,2,1:T(8,128)(2,1)} %pad_maximum_fusion.1), channel_id=1, source_target_pairs={{0,4},{4,0},{2,6},{6,2},{8,12},{12,8},{10,14},{14,10},{16,20},{20,... | collective-permute-start | bytes 393224 | tf_op jit(solution)/shard_map/ppermute | solution.py:20
  19.9 49.7 %collective-permute-start.3 = (bf16[32,8,128]{0,2,1:T(8,128)(2,1)}, bf16[32,8,128]{0,2,1:T(8,128)(2,1)}, u32[]{:S(2)}, u32[]{:S(2)}) collective-permute-start(bf16[32,8,128]{0,2,1:T(8,128)(2,1)} %copy.150), channel_id=1, source_target_pairs={{0,8},{8,0},{2,10},{10,2},{4,12},{12,4},{6,14},{14,6},{16,24},{24,... | collective-permute-start | bytes 196616 | tf_op jit(solution)/shard_map/ppermute | solution.py:20
  32.5 33.8 %collective-permute-start.6 = (bf16[16,8,128]{0,2,1:T(8,128)(2,1)}, bf16[16,8,128]{0,2,1:T(8,128)(2,1)}, u32[]{:S(2)}, u32[]{:S(2)}) collective-permute-start(bf16[16,8,128]{0,2,1:T(8,128)(2,1)} %copy.152), channel_id=1, source_target_pairs={{0,16},{16,0},{2,18},{18,2},{4,20},{20,4},{6,22},{22,6},{8,24},{24... | collective-permute-start | bytes 98312 | tf_op jit(solution)/shard_map/ppermute | solution.py:20
  45.6 104.8 %collective-permute-start = (bf16[128,8,128]{0,2,1:T(8,128)(2,1)}, bf16[128,8,128]{0,2,1:T(8,128)(2,1)}, u32[]{:S(2)}, u32[]{:S(2)}) collective-permute-start(bf16[128,8,128]{0,2,1:T(8,128)(2,1)} %pad_maximum_fusion), channel_id=1, source_target_pairs={{0,2},{2,0},{4,6},{6,4},{8,10},{10,8},{12,14},{14,12},{16,18},{18,... | collective-permute-start | bytes 786440 | tf_op jit(solution)/shard_map/ppermute | solution.py:20
  48.8 1.1 copy-start.3
  56.1 0.7 copy-start.6
  56.2 1.0 copy-start.14
  59.8 2.2 %copy-start.11 = (bf16[1,2,128,8,64]{2,1,4,3,0:T(2,128)(2,1)S(1)}, bf16[1,2,128,8,64]{2,1,4,3,0:T(2,128)(2,1)}, u32[]{:S(2)}) copy-start(bf16[1,2,128,8,64]{2,1,4,3,0:T(2,128)(2,1)} %rev.7) | copy-start | bytes 786436
  66.3 14.3 %collective-permute-start.7 = (bf16[16,8,128]{0,2,1:T(8,128)(2,1)}, bf16[16,8,128]{0,2,1:T(8,128)(2,1)S(1)}, u32[]{:S(2)}, u32[]{:S(2)}) collective-permute-start(bf16[16,8,128]{0,2,1:T(8,128)(2,1)} %collective-permute-done.6), channel_id=1, source_target_pairs={{0,2},{2,0},{4,6},{6,4},{8,10},{10,8},{12,14},{14,12},{16,18},{18,... | collective-permute-start | bytes 98312 | tf_op jit(solution)/shard_map/ppermute | solution.py:20
  69.6 27.4 %collective-permute-start.4 = (bf16[32,8,128]{0,2,1:T(8,128)(2,1)}, bf16[32,8,128]{0,2,1:T(8,128)(2,1)S(1)}, u32[]{:S(2)}, u32[]{:S(2)}) collective-permute-start(bf16[32,8,128]{0,2,1:T(8,128)(2,1)} %collective-permute-done.3), channel_id=1, source_target_pairs={{0,2},{2,0},{4,6},{6,4},{8,10},{10,8},{12,14},{14,12},{16,18},{18,... | collective-permute-start | bytes 196616 | tf_op jit(solution)/shard_map/ppermute | solution.py:20
  80.6 1.9 copy-start.4
  82.5 31.6 %collective-permute-start.8 = (bf16[32,8,128]{0,2,1:T(8,128)(2,1)}, bf16[32,8,128]{0,2,1:T(8,128)(2,1)}, u32[]{:S(2)}, u32[]{:S(2)}) collective-permute-start(bf16[32,8,128]{0,2,1:T(8,128)(2,1)} %pad_maximum_fusion.4), channel_id=1, source_target_pairs={{0,4},{4,0},{2,6},{6,2},{8,12},{12,8},{10,14},{14,10},{16,20},{20,... | collective-permute-start | bytes 196616 | tf_op jit(solution)/shard_map/ppermute | solution.py:20
  97.0 1.9 %copy-start.12 = (bf16[32,8,128]{0,2,1:T(8,128)(2,1)}, bf16[32,8,128]{0,2,1:T(8,128)(2,1)S(1)}, u32[]{:S(2)}) copy-start(bf16[32,8,128]{0,2,1:T(8,128)(2,1)S(1)} %collective-permute-done.4) | copy-start | bytes 196612
  98.9 22.9 %collective-permute-start.5 = (bf16[64,8,128]{0,2,1:T(8,128)(2,1)}, bf16[64,8,128]{0,2,1:T(8,128)(2,1)}, u32[]{:S(2)}, u32[]{:S(2)}) collective-permute-start(bf16[64,8,128]{0,2,1:T(8,128)(2,1)} %pad_maximum_fusion.2), channel_id=1, source_target_pairs={{0,4},{4,0},{2,6},{6,2},{8,12},{12,8},{10,14},{14,10},{16,20},{20,... | collective-permute-start | bytes 393224 | tf_op jit(solution)/shard_map/ppermute | solution.py:20
  104.0 2.3 %copy-start.7 = (f32[2,128,8,64]{1,3,2,0:T(8,128)S(1)}, f32[2,128,8,64]{1,3,2,0:T(8,128)}, u32[]{:S(2)}) copy-start(f32[2,128,8,64]{1,3,2,0:T(8,128)} %convolution_bitcast_fusion) | copy-start | bytes 1572868
  108.0 6.1 %copy-start.5 = (bf16[16,8,128]{0,2,1:T(8,128)(2,1)S(1)}, bf16[16,8,128]{0,2,1:T(8,128)(2,1)}, u32[]{:S(2)}) copy-start(bf16[16,8,128]{0,2,1:T(8,128)(2,1)} %copy-done.4) | copy-start | bytes 98308
  109.0 12.8 %copy-start.13 = (bf16[32,8,128]{0,2,1:T(8,128)(2,1)S(1)}, bf16[32,8,128]{0,2,1:T(8,128)(2,1)}, u32[]{:S(2)}) copy-start(bf16[32,8,128]{0,2,1:T(8,128)(2,1)} %copy-done.12) | copy-start | bytes 196612
  116.1 7.0 %copy-start.16 = (bf16[32,8,64]{2,1,0:T(8,128)(2,1)S(1)}, bf16[32,8,64]{2,1,0:T(8,128)(2,1)}, u32[]{:S(2)}) copy-start(bf16[32,8,64]{2,1,0:T(8,128)(2,1)} %multiply_convert_fusion.10) | copy-start | bytes 98308
  116.1 30.3 %collective-permute-start.9 = (bf16[64,8,128]{0,2,1:T(8,128)(2,1)}, bf16[64,8,128]{0,2,1:T(8,128)(2,1)}, u32[]{:S(2)}, u32[]{:S(2)}) collective-permute-start(bf16[64,8,128]{0,2,1:T(8,128)(2,1)} %pad_maximum_fusion.5), channel_id=1, source_target_pairs={{0,8},{8,0},{2,10},{10,2},{4,12},{12,4},{6,14},{14,6},{16,24},{24,... | collective-permute-start | bytes 393224 | tf_op jit(solution)/shard_map/ppermute | solution.py:20
  118.2 9.8 %collective-permute-start.2 = (bf16[64,8,128]{0,2,1:T(8,128)(2,1)}, bf16[64,8,128]{0,2,1:T(8,128)(2,1)S(1)}, u32[]{:S(2)}, u32[]{:S(2)}) collective-permute-start(bf16[64,8,128]{0,2,1:T(8,128)(2,1)} %collective-permute-done.1), channel_id=1, source_target_pairs={{0,2},{2,0},{4,6},{6,4},{8,10},{10,8},{12,14},{14,12},{16,18},{18,... | collective-permute-start | bytes 393224 | tf_op jit(solution)/shard_map/ppermute | solution.py:20
  123.3 0.9 copy-start.18
  132.8 0.9 copy-start.15
  133.7 0.7 copy-start.19
  137.0 11.0 %copy-start.17 = (bf16[16,8,64]{2,1,0:T(8,128)(2,1)S(1)}, bf16[16,8,64]{2,1,0:T(8,128)(2,1)}, u32[]{:S(2)}) copy-start(bf16[16,8,64]{2,1,0:T(8,128)(2,1)} %multiply_convert_fusion.13) | copy-start | bytes 49156
  149.3 1.0 copy-start.10
  154.1 1.4 copy-start.20
  154.1 1.4 copy-start.21
  154.1 1.4 copy-start.22
  154.1 1.4 copy-start.23
  154.1 1.3 copy-start.24
  154.2 1.3 copy-start.25
  154.4 1.1 copy-start.8
  154.4 1.4 copy-start.9
Sparse Core Ops, SparseCore 0:
  158.9 24.6 reduce-scatter.1
where the time goes:
time: 191 us; the launch traced here: 190 us
  starting transfers between devices  55.1 us (29%)
  waiting for transfers between devices  51.7 us (27%)
  local copies, waits for them, and re-layouts  34.5 us (18%)
  other arithmetic  22.5 us (12%)
  between operations  14.2 us (7%)
  matrix products  12.5 us (7%)
    ppermute x10, starting transfers between devices, swapped(): return lax.ppermute(block, axis, route)  55 us
    ppermute x10, waiting for transfers between devices, swapped(): return lax.ppermute(block, axis, route)  26.8 us
    reduce_scatter x1, waiting for transfers between devices, body(): lax.psum_scatter(partial_value.astype(jnp.bfloat16), 'head', scatter_dime...  24.8 us
    convert_element_type x12, local copies, waits for them, and re-layouts, coarse(): field.astype(jnp.float32)  8.64 us
    concatenate x5, other arithmetic, body(): jnp.concatenate((received, swapped(received, 'seq', bit_no)), axis=0)  8.52 us
    reduce_sum x12, other arithmetic, coarse(): return jnp.mean(merged, axis=1).astype(jnp.bfloat16)  7.59 us
    dot_general x6, matrix products, attend(): jnp.einsum('nhqk,nkhe->nqhe', weights.astype(jnp.bfloat16), value_blk, pr...  6.73 us
    dot_general x6, matrix products, attend(): jnp.einsum('nqhe,nkhe->nhqk', query_blk, key_blk, preferred_element_type=...  4.51 us
  transfers between devices with their start and end apart: 11, of which 5 were waited for; matrix products, arithmetic and copies ran while one was open for 29% of the time, Pallas kernels for 0%

commit v1 on v0

v1 whole, which is shorter than its diff:
```python
import jax
import jax.numpy as jnp
from jax import lax
from jax.experimental import pallas as pl
from jax.experimental.pallas import tpu as pltpu
from jax.sharding import PartitionSpec as P

HEAD_DIM = 64
SCALE = 0.125
LANES = 128
RING = 16
VMEM_LIMIT = 16 * 1024 * 1024


def params(limit=VMEM_LIMIT):
    return pltpu.CompilerParams(vmem_limit_bytes=limit)


def half_lanes(shape):
    return lax.broadcasted_iota(jnp.int32, shape, 1) < HEAD_DIM


def attend_pair(query, key, value):
    rows = query.shape[0]
    scaled = query * jnp.bfloat16(SCALE)
    left = half_lanes(scaled.shape)
    zero = jnp.zeros_like(scaled)
    both = jnp.concatenate((jnp.where(left, scaled, zero), jnp.where(left, zero, scaled)), axis=0)
    scores = lax.dot_general(both, key, (((1,), (1,)), ((), ())), preferred_element_type=jnp.float32)
    row_max = jnp.max(scores, axis=1, keepdims=True)
    weights = jnp.exp(scores - row_max).astype(jnp.bfloat16)
    wide = jnp.concatenate((value, jnp.ones_like(value)), axis=1)
    sums = jnp.dot(weights, wide, preferred_element_type=jnp.float32)
    left = half_lanes((rows, LANES))
    highest = jnp.where(left, row_max[:rows], row_max[rows:])
    total = jnp.where(left, sums[:rows, LANES:], sums[rows:, LANES:])
    weighted = jnp.where(left, sums[:rows, :LANES], sums[rows:, :LANES])
    return highest, total, weighted


def merge(one, two, factor):
    highest = jnp.maximum(one[0], two[0])
    keep = jnp.exp(one[0] - highest)
    add = factor * jnp.exp(two[0] - highest)
    return highest, keep * one[1] + add * two[1], keep * one[2] + add * two[2]


def spread(ref, rows, factor):
    def run(value):
        for turn in range(factor):
            ref[pl.ds(turn, rows, stride=factor), :] = value
        return ref[pl.ds(0, rows * factor), :]

    return run


def mean_matrix(rows, shift):
    row = lax.broadcasted_iota(jnp.int32, (rows, rows << shift), 0)
    col = lax.broadcasted_iota(jnp.int32, (rows, rows << shift), 1)
    return jnp.where((col >> shift) == row, 1.0 / (1 << shift), 0.0).astype(jnp.bfloat16)


def coarse_kernel(q_hbm, k_hbm, v_hbm, q_ref, kv2_ref, kv3_ref, kv4_ref, kv5_ref, q_in, k_in, v_in, sems):
    copies = [
        pltpu.make_async_copy(hbm, vmem, sems.at[turn])
        for turn, (hbm, vmem) in enumerate(((k_hbm, k_in), (v_hbm, v_in), (q_hbm, q_in)))
    ]
    for copy in copies:
        copy.start()
    means = jnp.concatenate([mean_matrix(256 >> shift, shift) for shift in (1, 2, 3, 4)], axis=0)
    width = q_in.shape[1]
    for turn, field in enumerate((k_in, v_in)):
        copies[turn].wait()
        means_of = jnp.dot(means, field[...], preferred_element_type=jnp.float32).astype(jnp.bfloat16)
        cols = slice(turn * width, (turn + 1) * width)
        kv2_ref[:, cols] = means_of[:128]
        kv3_ref[:, cols] = means_of[128:192]
        kv4_ref[:, cols] = means_of[192:224]
        kv5_ref[:, cols] = means_of[224:240]
    copies[2].wait()
    q_ref[...] = jnp.dot(means, q_in[...], preferred_element_type=jnp.float32).astype(jnp.bfloat16)


def pack_kernel(kv4_ref, far5_ref, near5_ref, out_ref):
    out_ref[0:32, :] = kv4_ref[...]
    out_ref[32:48, :] = far5_ref[...]
    out_ref[48:64, :] = near5_ref[...]


def near_kernel(q_ref, k_ref, v_ref, top_ref, total_ref, sum_ref):
    for pair in range(4):
        cols = slice(pair * LANES, (pair + 1) * LANES)
        highest, total, weighted = attend_pair(q_ref[:, cols], k_ref[:, cols], v_ref[:, cols])
        top_ref[:, cols] = highest
        total_ref[:, cols] = total
        sum_ref[:, cols] = weighted


def middle_kernel(
    q_ref, kv2_ref, kv3a_ref, kv3b_ref, top_in, total_in, sum_in, top_ref, total_ref, sum_ref, scratch_ref
):
    width = q_ref.shape[1]
    for pair in range(4):
        cols = slice(pair * LANES, (pair + 1) * LANES)
        vcols = slice(width + pair * LANES, width + (pair + 1) * LANES)
        level2 = attend_pair(q_ref[:128, cols], kv2_ref[:, cols], kv2_ref[:, vcols])
        key3 = jnp.concatenate((kv3a_ref[:, cols], kv3b_ref[:, cols]), axis=0)
        value3 = jnp.concatenate((kv3a_ref[:, vcols], kv3b_ref[:, vcols]), axis=0)
        level3 = attend_pair(q_ref[128:192, cols], key3, value3)
        double = spread(scratch_ref, 64, 2)
        level2 = merge(level2, [double(part) for part in level3], 2.0)
        double = spread(scratch_ref, 128, 2)
        near = (top_in[:, cols], total_in[:, cols], sum_in[:, cols])
        top_ref[:, cols], total_ref[:, cols], sum_ref[:, cols] = merge(
            near, [double(part) for part in level2], 2.0
        )


def last_kernel(
    q_ref, one_ref, two_ref, three_ref, four_ref, top_ref, total_ref, sum_ref, w_ref, mine_ref, send_ref, scratch_ref
):
    core = lax.axis_index("head")
    width = q_ref.shape[1]
    parts = (one_ref, two_ref, three_ref, four_ref)
    pieces = []
    for pair in range(4):
        cols = slice(pair * LANES, (pair + 1) * LANES)
        vcols = slice(width + pair * LANES, width + (pair + 1) * LANES)
        key4, value4, key5, value5 = [
            jnp.concatenate([part[rows, lanes] for part in parts], axis=0)
            for rows in (slice(0, 32), slice(32, 64))
            for lanes in (cols, vcols)
        ]
        level4 = attend_pair(q_ref[192:224, cols], key4, value4)
        level5 = attend_pair(q_ref[224:240, cols], key5, value5)
        double = spread(scratch_ref, 16, 2)
        far = merge(level4, [double(part) for part in level5], 2.0)
        eight = spread(scratch_ref, 32, 8)
        near = (top_ref[:, cols], total_ref[:, cols], sum_ref[:, cols])
        near = merge(near, [eight(part) for part in far], 8.0)
        pieces.append((near[2] / near[1]).astype(jnp.bfloat16))
    attention = jnp.concatenate(pieces, axis=1)
    half = w_ref.shape[1] // 2
    away = pl.multiple_of((1 - core) * half, half)
    home = pl.multiple_of(core * half, half)
    send_ref[...] = jnp.dot(attention, w_ref[:, pl.ds(away, half)], preferred_element_type=jnp.float32).astype(
        jnp.bfloat16
    )
    mine_ref[...] = jnp.dot(attention, w_ref[:, pl.ds(home, half)], preferred_element_type=jnp.float32).astype(
        jnp.bfloat16
    )


def moved(block, partner):
    count = lax.axis_size("seq")
    return lax.ppermute(block, "seq", [(i, i - i % RING + partner(i % RING)) for i in range(count)])


def flip(mask):
    return lambda place: place ^ mask


def far_partner(place):
    return 11 - place if place // 4 in (0, 2) else 19 - place


def call(kernel, name, outs, scratch=(), flops=0, moved_bytes=1_000_000, exps=0, in_specs=None, limit=VMEM_LIMIT):
    given = {} if in_specs is None else {"in_specs": in_specs}
    return pl.pallas_call(
        kernel,
        out_shape=outs,
        scratch_shapes=list(scratch),
        compiler_params=params(limit),
        cost_estimate=pl.CostEstimate(flops=flops, bytes_accessed=moved_bytes, transcendentals=exps),
        name=name,
        **given,
    )


def body(queries, key_rows, value_rows, out_weight):
    rows, width = queries.shape
    f32, bf16 = jnp.float32, jnp.bfloat16
    shape = jax.ShapeDtypeStruct
    fields = (shape((rows, width), f32),) * 3
    coarse_q, kv2, kv3, kv4, kv5 = call(
        coarse_kernel,
        "coarse",
        (shape((240, width), bf16),) + tuple(shape((size, 2 * width), bf16) for size in (128, 64, 32, 16)),
        [pltpu.VMEM((rows, width), bf16)] * 3 + [pltpu.SemaphoreType.DMA((3,))],
        flops=2 * 240 * 256 * 1536,
        in_specs=[pl.BlockSpec(memory_space=pltpu.HBM)] * 3,
        limit=63 * 1024 * 1024,
    )(queries, key_rows, value_rows)
    far5 = moved(kv5, far_partner)
    far4 = moved(kv4, flip(4))
    near5 = moved(kv5, flip(12))
    kv3a = moved(kv3, flip(2))
    kv2_got = moved(kv2, flip(1))
    near = call(near_kernel, "near", fields, flops=8 * 256 * 256 * 64 * 4, exps=8 * 256 * 256)(
        queries, key_rows, value_rows
    )
    own = call(pack_kernel, "pack", shape((64, 2 * width), bf16))(far4, far5, near5)
    two = moved(own, flip(2))
    one = moved(own, flip(1))
    kv3b = moved(kv3a, flip(1))
    three = moved(two, flip(1))
    near = call(
        middle_kernel, "middle", fields, [pltpu.VMEM((256, LANES), f32)], flops=300_000_000, exps=8 * 256 * 200
    )(coarse_q, kv2_got, kv3a, kv3b, *near)
    mine, send = call(
        last_kernel,
        "last",
        (shape((rows, width), bf16),) * 2,
        [pltpu.VMEM((256, LANES), f32)],
        flops=600_000_000,
        exps=8 * 256 * 100,
    )(coarse_q, own, one, two, three, *near, out_weight)
    fetched = lax.ppermute(send, "head", [(0, 1), (1, 0)])
    return (mine.astype(f32) + fetched.astype(f32)).astype(bf16)


def solution(mesh):
    placed = (P("seq", "head"), P("seq", "head"), P("seq", "head"), P("head", None))
    return jax.shard_map(
        body, mesh=mesh, in_specs=placed, out_specs=P("seq", "head"), check_vma=False
    )
```

time: 191 us -> 58.8 us (0.31)
  waiting for transfers between devices: 51.7 us -> 5.28 us
  local copies, waits for them, and re-layouts: 34.5 us -> 0.02 us
  other arithmetic: 22.5 us -> 0.77 us
  between operations: 14.2 us -> 0.22 us
  matrix products: 12.5 us -> 0 us
  starting transfers between devices: 55.1 us -> 44.7 us
  Pallas kernels: 0 us -> 7.46 us
    reduce_scatter x1 -> x0, waiting for transfers between devices: 24.8 us -> none  [body(): lax.psum_scatter(partial_value.astype(jnp.bfloat16), 'head', scatter_dime...]
    ppermute x10, waiting for transfers between devices: 26.8 us -> 5.28 us  [the longest x9 4.14 us: moved(): lax.ppermute(block, 'seq', [(i, i - i % RING + partner(i % RING)) for i i...]
    dot_general x13 -> x0, matrix products: 12.5 us -> none  [the longest x6 6.73 us: attend(): jnp.einsum('nhqk,nkhe->nqhe', weights.astype(jnp.bfloat16), value_blk, pr...]
    ppermute x10, starting transfers between devices: 55 us -> 44.7 us  [the longest x9 39.4 us: moved(): lax.ppermute(block, 'seq', [(i, i - i % RING + partner(i % RING)) for i i...]
    concatenate x9 -> x0, other arithmetic: 10.2 us -> none  [the longest x5 8.52 us: body(): jnp.concatenate((received, swapped(received, 'seq', bit_no)), axis=0)]
    reduce_sum x17 -> x0, other arithmetic: 9.25 us -> none  [the longest x12 7.59 us: coarse(): return jnp.mean(merged, axis=1).astype(jnp.bfloat16)]
    convert_element_type x12 -> x0, local copies, waits for them, and re-layouts: 8.64 us -> none  [coarse(): field.astype(jnp.float32)]
    reshape x24 -> x0, local copies, waits for them, and re-layouts: 8.21 us -> none  [the longest x8 4.28 us: body(): jnp.repeat(weighted, factor, axis=0)]
  transfers between devices with their start and end apart: 11 -> 10, of which waited for: 5 -> 4; matrix products, arithmetic and copies ran while one was open for 29% -> 0% of each run, Pallas kernels for 0% -> 4%
where the time goes in v1:
time: 58.8 us; the launch traced here: 58.4 us
  starting transfers between devices  44.7 us (76%)
  Pallas kernels  7.46 us (13%)
  waiting for transfers between devices  5.28 us (9%)
  other arithmetic  0.77 us (1%)
    ppermute x9, starting transfers between devices, moved(): lax.ppermute(block, 'seq', [(i, i - i % RING + partner(i % RING)) for i i...  39.4 us
    ppermute x1, starting transfers between devices, body(): fetched = lax.ppermute(send, 'head', [(0, 1), (1, 0)])  5.23 us
    ppermute x9, waiting for transfers between devices, moved(): lax.ppermute(block, 'seq', [(i, i - i % RING + partner(i % RING)) for i i...  4.14 us
    pallas_call x1, Pallas kernels, body(): call(last_kernel, 'last', (shape((rows, width), bf16),) * 2, [pltpu.VMEM(...  2.56 us
    pallas_call x1, Pallas kernels, body(): call(coarse_kernel, 'coarse', (shape((240, width), bf16),) + tuple((shape...  2.41 us
    pallas_call x1, Pallas kernels, body(): call(middle_kernel, 'middle', fields, [pltpu.VMEM((256, LANES), f32)], fl...  1.59 us
  transfers between devices with their start and end apart: 10, of which 4 were waited for; matrix products, arithmetic and copies ran while one was open for 0% of the time, Pallas kernels for 4%

profile of v1, /device:TPU:1, one launch (start us, length us, event | category | flops | bytes accessed | tf_op | source)
XLA Modules:
  0.0 58.4 jit_solution(13974396828820890767)
XLA Ops:
  0.0 0.0 copy-start.3
  0.0 0.0 copy-start.4
  0.0 2.4 %coarse.1 = (bf16[240,512]{1,0:T(8,128)(2,1)}, bf16[128,1024]{1,0:T(8,128)(2,1)}, bf16[64,1024]{1,0:T(8,128)(2,1)}, bf16[32,1024]{1,0:T(8,128)(2,1)}, bf16[16,1024]{1,0:T(8,128)(2,1)}) custom-call(bf16[256,512]{1,0:T(8,128)(2,1)} %q_ref.1, bf16[256,512]{1,0:T(8,128)(2,1)} %k_ref.1, bf16[256,512]{1,0:T(8,128)(2,1)} %v_ref.1), custom_call_target="tpu_custom_call" | custom-call | flops 188743680 | bytes 1000000 | tf_op jit(solution)/shard_map/coarse/pallas_call | solution.py:185
  2.4 0.0 copy-start.2
  2.4 9.8 %collective-permute-start = (bf16[32,1024]{1,0:T(8,128)(2,1)}, bf16[32,1024]{1,0:T(8,128)(2,1)S(1)}, u32[]{:S(2)}, u32[]{:S(2)}) collective-permute-start(bf16[32,1024]{1,0:T(8,128)(2,1)} %get-tuple-element.19), channel_id=1, source_target_pairs={{0,8},{2,10},{4,12},{6,14},{8,0},{10,2},{12,4},{14,6},{16,24},{18,... | collective-permute-start | bytes 196616 | tf_op jit(solution)/shard_map/ppermute | solution.py:156
  12.2 9.3 %collective-permute-start.1 = (bf16[16,1024]{1,0:T(8,128)(2,1)}, bf16[16,1024]{1,0:T(8,128)(2,1)S(1)}, u32[]{:S(2)}, u32[]{:S(2)}) collective-permute-start(bf16[16,1024]{1,0:T(8,128)(2,1)} %get-tuple-element.20), channel_id=1, source_target_pairs={{0,22},{2,20},{4,18},{6,16},{8,30},{10,28},{12,26},{14,24},{16,6},... | collective-permute-start | bytes 98312 | tf_op jit(solution)/shard_map/ppermute | solution.py:156
  21.5 1.9 %collective-permute-start.2 = (bf16[16,1024]{1,0:T(8,128)(2,1)}, bf16[16,1024]{1,0:T(8,128)(2,1)S(1)}, u32[]{:S(2)}, u32[]{:S(2)}) collective-permute-start(bf16[16,1024]{1,0:T(8,128)(2,1)} %get-tuple-element.20), channel_id=1, source_target_pairs={{0,24},{2,26},{4,28},{6,30},{8,16},{10,18},{12,20},{14,22},{16,8},... | collective-permute-start | bytes 98312 | tf_op jit(solution)/shard_map/ppermute | solution.py:156
  23.5 4.0 %collective-permute-start.7 = (bf16[64,1024]{1,0:T(8,128)(2,1)}, bf16[64,1024]{1,0:T(8,128)(2,1)S(1)}, u32[]{:S(2)}, u32[]{:S(2)}) collective-permute-start(bf16[64,1024]{1,0:T(8,128)(2,1)} %get-tuple-element.22), channel_id=1, source_target_pairs={{0,4},{2,6},{4,0},{6,2},{8,12},{10,14},{12,8},{14,10},{16,20},{18,... | collective-permute-start | bytes 393224 | tf_op jit(solution)/shard_map/ppermute | solution.py:156
  27.4 1.9 %collective-permute-start.6 = (bf16[128,1024]{1,0:T(8,128)(2,1)}, bf16[128,1024]{1,0:T(8,128)(2,1)S(1)}, u32[]{:S(2)}, u32[]{:S(2)}) collective-permute-start(bf16[128,1024]{1,0:T(8,128)(2,1)} %get-tuple-element.21), channel_id=1, source_target_pairs={{0,2},{2,0},{4,6},{6,4},{8,10},{10,8},{12,14},{14,12},{16,18},{18,... | collective-permute-start | bytes 786440 | tf_op jit(solution)/shard_map/ppermute | solution.py:156
  29.4 0.0 collective-permute-done.1.far5_ref
  29.4 1.0 %collective-permute-done.2.near5_ref = bf16[16,1024]{1,0:T(8,128)(2,1)S(1)} collective-permute-done((bf16[16,1024]{1,0:T(8,128)(2,1)}, bf16[16,1024]{1,0:T(8,128)(2,1)S(1)}, u32[]{:S(2)}, u32[]{:S(2)}) %collective-permute-start.2) | collective-permute-done | bytes 32800 | tf_op jit(solution)/shard_map/ppermute | solution.py:156
  30.4 0.0 collective-permute-done.kv4_ref
  30.4 0.0 copy-start.1
  30.5 4.8 %collective-permute-start.4 = (bf16[64,1024]{1,0:T(8,128)(2,1)S(1)}, bf16[64,1024]{1,0:T(8,128)(2,1)S(1)}, u32[]{:S(2)}, u32[]{:S(2)}) collective-permute-start(bf16[64,1024]{1,0:T(8,128)(2,1)S(1)} %pack.1.one_ref), channel_id=1, source_target_pairs={{0,4},{2,6},{4,0},{6,2},{8,12},{10,14},{12,8},{14,10},{16,20},{18,... | collective-permute-start | bytes 393224 | tf_op jit(solution)/shard_map/ppermute | solution.py:156
  35.2 0.0 collective-permute-done.7.kv3a_ref
  35.2 1.9 %collective-permute-start.8 = (bf16[64,1024]{1,0:T(8,128)(2,1)S(1)}, bf16[64,1024]{1,0:T(8,128)(2,1)S(1)}, u32[]{:S(2)}, u32[]{:S(2)}) collective-permute-start(bf16[64,1024]{1,0:T(8,128)(2,1)S(1)} %collective-permute-done.7.kv3a_ref), channel_id=1, source_target_pairs={{0,2},{2,0},{4,6},{6,4},{8,10},{10,8},{12,14},{14,12},{16,18},{18,... | collective-permute-start | bytes 393224 | tf_op jit(solution)/shard_map/ppermute | solution.py:156
  37.2 3.4 %collective-permute-start.3 = (bf16[64,1024]{1,0:T(8,128)(2,1)S(1)}, bf16[64,1024]{1,0:T(8,128)(2,1)S(1)}, u32[]{:S(2)}, u32[]{:S(2)}) collective-permute-start(bf16[64,1024]{1,0:T(8,128)(2,1)S(1)} %pack.1.one_ref), channel_id=1, source_target_pairs={{0,2},{2,0},{4,6},{6,4},{8,10},{10,8},{12,14},{14,12},{16,18},{18,... | collective-permute-start | bytes 393224 | tf_op jit(solution)/shard_map/ppermute | solution.py:156
  40.5 0.0 collective-permute-done.4.three_ref
  40.6 2.5 %collective-permute-start.5 = (bf16[64,1024]{1,0:T(8,128)(2,1)S(1)}, bf16[64,1024]{1,0:T(8,128)(2,1)S(1)}, u32[]{:S(2)}, u32[]{:S(2)}) collective-permute-start(bf16[64,1024]{1,0:T(8,128)(2,1)S(1)} %collective-permute-done.4.three_ref), channel_id=1, source_target_pairs={{0,2},{2,0},{4,6},{6,4},{8,10},{10,8},{12,14},{14,12},{16,18},{18,... | collective-permute-start | bytes 393224 | tf_op jit(solution)/shard_map/ppermute | solution.py:156
  43.1 0.0 copy-done.3
  43.1 0.0 copy-done.4
  43.1 0.0 copy-done.2
  43.1 0.9 %near.1 = (f32[256,512]{1,0:T(8,128)S(1)}, f32[256,512]{1,0:T(8,128)S(1)}, f32[256,512]{1,0:T(8,128)S(1)}) custom-call(bf16[256,512]{1,0:T(8,128)(2,1)S(1)} %copy-done.2, bf16[256,512]{1,0:T(8,128)(2,1)S(1)} %copy-done.3, bf16[256,512]{1,0:T(8,128)(2,1)S(1)} %copy-done.4), custom_call_target="tpu_custom_call" | custom-call | flops 134217728 | bytes 1000000 | tf_op jit(solution)/shard_map/near/pallas_call | solution.py:199
  44.0 0.0 collective-permute-done.8.kv3b_ref
  44.0 0.0 collective-permute-done.6.kv2_ref
  44.0 0.0 copy-done.1
  44.0 0.0 copy-start
  44.0 1.6 %middle.1 = (f32[256,512]{1,0:T(8,128)S(1)}, f32[256,512]{1,0:T(8,128)S(1)}, f32[256,512]{1,0:T(8,128)S(1)}) custom-call(bf16[240,512]{1,0:T(8,128)(2,1)S(1)} %copy-done.1, bf16[128,1024]{1,0:T(8,128)(2,1)S(1)} %collective-permute-done.6.kv2_ref, bf16[64,1024]{1,0:T(8,128)(2,1)S(1)} %collective-permute-done.7.kv3a_ref, ...), custom_call_target="tpu_custom_call" | custom-call | flops 300000000 | bytes 1000000 | tf_op jit(solution)/shard_map/middle/pallas_call | solution.py:207
  45.6 0.3 collective-permute-done.3.two_ref
  45.9 2.8 %collective-permute-done.5.four_ref = bf16[64,1024]{1,0:T(8,128)(2,1)S(1)} collective-permute-done((bf16[64,1024]{1,0:T(8,128)(2,1)S(1)}, bf16[64,1024]{1,0:T(8,128)(2,1)S(1)}, u32[]{:S(2)}, u32[]{:S(2)}) %collective-permute-start.5) | collective-permute-done | bytes 131104 | tf_op jit(solution)/shard_map/ppermute | solution.py:156
  48.7 0.0 copy-done
  48.7 2.6 %last.1 = (bf16[256,512]{1,0:T(8,128)(2,1)S(1)}, bf16[256,512]{1,0:T(8,128)(2,1)S(1)}) custom-call(bf16[240,512]{1,0:T(8,128)(2,1)S(1)} %copy-done.1, bf16[64,1024]{1,0:T(8,128)(2,1)S(1)} %pack.1.one_ref, bf16[64,1024]{1,0:T(8,128)(2,1)S(1)} %collective-permute-done.3.two_ref, bf16[64,1024]{1,0:T(8,128)(2,1)S(1)} %collective-permute-done.4.three_ref, ...), custom_call_target="tpu_custom_call" | custom-call | flops 600000000 | bytes 1000000 | tf_op jit(solution)/shard_map/last/pallas_call | solution.py:210
  51.3 5.2 %collective-permute-start.9 = (bf16[256,512]{1,0:T(8,128)(2,1)S(1)}, bf16[256,512]{1,0:T(8,128)(2,1)S(1)}, u32[]{:S(2)}, u32[]{:S(2)}) collective-permute-start(bf16[256,512]{1,0:T(8,128)(2,1)S(1)} %get-tuple-element.30), channel_id=1, source_target_pairs={{0,1},{1,0},{2,3},{3,2},{4,5},{5,4},{6,7},{7,6},{8,9},{9,8},{10,11... | collective-permute-start | bytes 786440 | tf_op jit(solution)/shard_map/ppermute | solution.py:218
  56.5 1.1 %collective-permute-done.9 = bf16[256,512]{1,0:T(8,128)(2,1)S(1)} collective-permute-done((bf16[256,512]{1,0:T(8,128)(2,1)S(1)}, bf16[256,512]{1,0:T(8,128)(2,1)S(1)}, u32[]{:S(2)}, u32[]{:S(2)}) %collective-permute-start.9) | collective-permute-done | bytes 262176 | tf_op jit(solution)/shard_map/ppermute | solution.py:218
  57.7 0.8 %add_convert_fusion = bf16[256,512]{1,0:T(8,128)(2,1)} fusion(bf16[256,512]{1,0:T(8,128)(2,1)S(1)} %collective-permute-done.9, bf16[256,512]{1,0:T(8,128)(2,1)S(1)} %get-tuple-element.29), kind=kLoop, calls=%fused_computation | loop fusion | flops 524288 | bytes 786432 | tf_op jit(solution)/shard_map/convert_element_type | solution.py:219
  (1 shorter events, 0.0 us)
Async XLA Ops:
  0.0 43.1 %copy-start.3 = (bf16[256,512]{1,0:T(8,128)(2,1)S(1)}, bf16[256,512]{1,0:T(8,128)(2,1)}, u32[]{:S(2)}) copy-start(bf16[256,512]{1,0:T(8,128)(2,1)} %k_ref.1) | copy-start | bytes 786436
  0.0 43.1 %copy-start.4 = (bf16[256,512]{1,0:T(8,128)(2,1)S(1)}, bf16[256,512]{1,0:T(8,128)(2,1)}, u32[]{:S(2)}) copy-start(bf16[256,512]{1,0:T(8,128)(2,1)} %v_ref.1) | copy-start | bytes 786436
  2.4 40.7 %copy-start.2 = (bf16[256,512]{1,0:T(8,128)(2,1)S(1)}, bf16[256,512]{1,0:T(8,128)(2,1)}, u32[]{:S(2)}) copy-start(bf16[256,512]{1,0:T(8,128)(2,1)} %q_ref.1) | copy-start | bytes 786436
  2.4 28.0 %collective-permute-start = (bf16[32,1024]{1,0:T(8,128)(2,1)}, bf16[32,1024]{1,0:T(8,128)(2,1)S(1)}, u32[]{:S(2)}, u32[]{:S(2)}) collective-permute-start(bf16[32,1024]{1,0:T(8,128)(2,1)} %get-tuple-element.19), channel_id=1, source_target_pairs={{0,8},{2,10},{4,12},{6,14},{8,0},{10,2},{12,4},{14,6},{16,24},{18,... | collective-permute-start | bytes 196616 | tf_op jit(solution)/shard_map/ppermute | solution.py:156
  12.2 17.1 %collective-permute-start.1 = (bf16[16,1024]{1,0:T(8,128)(2,1)}, bf16[16,1024]{1,0:T(8,128)(2,1)S(1)}, u32[]{:S(2)}, u32[]{:S(2)}) collective-permute-start(bf16[16,1024]{1,0:T(8,128)(2,1)} %get-tuple-element.20), channel_id=1, source_target_pairs={{0,22},{2,20},{4,18},{6,16},{8,30},{10,28},{12,26},{14,24},{16,6},... | collective-permute-start | bytes 98312 | tf_op jit(solution)/shard_map/ppermute | solution.py:156
  21.5 8.9 %collective-permute-start.2 = (bf16[16,1024]{1,0:T(8,128)(2,1)}, bf16[16,1024]{1,0:T(8,128)(2,1)S(1)}, u32[]{:S(2)}, u32[]{:S(2)}) collective-permute-start(bf16[16,1024]{1,0:T(8,128)(2,1)} %get-tuple-element.20), channel_id=1, source_target_pairs={{0,24},{2,26},{4,28},{6,30},{8,16},{10,18},{12,20},{14,22},{16,8},... | collective-permute-start | bytes 98312 | tf_op jit(solution)/shard_map/ppermute | solution.py:156
  23.5 11.8 %collective-permute-start.7 = (bf16[64,1024]{1,0:T(8,128)(2,1)}, bf16[64,1024]{1,0:T(8,128)(2,1)S(1)}, u32[]{:S(2)}, u32[]{:S(2)}) collective-permute-start(bf16[64,1024]{1,0:T(8,128)(2,1)} %get-tuple-element.22), channel_id=1, source_target_pairs={{0,4},{2,6},{4,0},{6,2},{8,12},{10,14},{12,8},{14,10},{16,20},{18,... | collective-permute-start | bytes 393224 | tf_op jit(solution)/shard_map/ppermute | solution.py:156
  27.4 16.6 %collective-permute-start.6 = (bf16[128,1024]{1,0:T(8,128)(2,1)}, bf16[128,1024]{1,0:T(8,128)(2,1)S(1)}, u32[]{:S(2)}, u32[]{:S(2)}) collective-permute-start(bf16[128,1024]{1,0:T(8,128)(2,1)} %get-tuple-element.21), channel_id=1, source_target_pairs={{0,2},{2,0},{4,6},{6,4},{8,10},{10,8},{12,14},{14,12},{16,18},{18,... | collective-permute-start | bytes 786440 | tf_op jit(solution)/shard_map/ppermute | solution.py:156
  30.4 13.6 %copy-start.1 = (bf16[240,512]{1,0:T(8,128)(2,1)S(1)}, bf16[240,512]{1,0:T(8,128)(2,1)}, u32[]{:S(2)}) copy-start(bf16[240,512]{1,0:T(8,128)(2,1)} %get-tuple-element.18.q_ref) | copy-start | bytes 737284
  30.5 10.1 %collective-permute-start.4 = (bf16[64,1024]{1,0:T(8,128)(2,1)S(1)}, bf16[64,1024]{1,0:T(8,128)(2,1)S(1)}, u32[]{:S(2)}, u32[]{:S(2)}) collective-permute-start(bf16[64,1024]{1,0:T(8,128)(2,1)S(1)} %pack.1.one_ref), channel_id=1, source_target_pairs={{0,4},{2,6},{4,0},{6,2},{8,12},{10,14},{12,8},{14,10},{16,20},{18,... | collective-permute-start | bytes 393224 | tf_op jit(solution)/shard_map/ppermute | solution.py:156
  35.2 8.7 %collective-permute-start.8 = (bf16[64,1024]{1,0:T(8,128)(2,1)S(1)}, bf16[64,1024]{1,0:T(8,128)(2,1)S(1)}, u32[]{:S(2)}, u32[]{:S(2)}) collective-permute-start(bf16[64,1024]{1,0:T(8,128)(2,1)S(1)} %collective-permute-done.7.kv3a_ref), channel_id=1, source_target_pairs={{0,2},{2,0},{4,6},{6,4},{8,10},{10,8},{12,14},{14,12},{16,18},{18,... | collective-permute-start | bytes 393224 | tf_op jit(solution)/shard_map/ppermute | solution.py:156
  37.2 8.7 %collective-permute-start.3 = (bf16[64,1024]{1,0:T(8,128)(2,1)S(1)}, bf16[64,1024]{1,0:T(8,128)(2,1)S(1)}, u32[]{:S(2)}, u32[]{:S(2)}) collective-permute-start(bf16[64,1024]{1,0:T(8,128)(2,1)S(1)} %pack.1.one_ref), channel_id=1, source_target_pairs={{0,2},{2,0},{4,6},{6,4},{8,10},{10,8},{12,14},{14,12},{16,18},{18,... | collective-permute-start | bytes 393224 | tf_op jit(solution)/shard_map/ppermute | solution.py:156
  40.6 8.1 %collective-permute-start.5 = (bf16[64,1024]{1,0:T(8,128)(2,1)S(1)}, bf16[64,1024]{1,0:T(8,128)(2,1)S(1)}, u32[]{:S(2)}, u32[]{:S(2)}) collective-permute-start(bf16[64,1024]{1,0:T(8,128)(2,1)S(1)} %collective-permute-done.4.three_ref), channel_id=1, source_target_pairs={{0,2},{2,0},{4,6},{6,4},{8,10},{10,8},{12,14},{14,12},{16,18},{18,... | collective-permute-start | bytes 393224 | tf_op jit(solution)/shard_map/ppermute | solution.py:156
  44.0 4.7 %copy-start = (bf16[512,1024]{1,0:T(8,128)(2,1)S(1)}, bf16[512,1024]{1,0:T(8,128)(2,1)}, u32[]{:S(2)}) copy-start(bf16[512,1024]{1,0:T(8,128)(2,1)} %w_ref.1) | copy-start | bytes 3145732
  51.3 6.4 %collective-permute-start.9 = (bf16[256,512]{1,0:T(8,128)(2,1)S(1)}, bf16[256,512]{1,0:T(8,128)(2,1)S(1)}, u32[]{:S(2)}, u32[]{:S(2)}) collective-permute-start(bf16[256,512]{1,0:T(8,128)(2,1)S(1)} %get-tuple-element.30), channel_id=1, source_target_pairs={{0,1},{1,0},{2,3},{3,2},{4,5},{5,4},{6,7},{7,6},{8,9},{9,8},{10,11... | collective-permute-start | bytes 786440 | tf_op jit(solution)/shard_map/ppermute | solution.py:218

commit v2 on v1

--- a/solution.py
+++ b/solution.py
@@ -9,6 +9,7 @@
 SCALE = 0.125
 LANES = 128
 RING = 16
+NEVER = -1e30
 VMEM_LIMIT = 16 * 1024 * 1024
 
 
@@ -20,13 +21,18 @@
     return lax.broadcasted_iota(jnp.int32, shape, 1) < HEAD_DIM
 
 
-def attend_pair(query, key, value):
+def attend_pair(query, key, value, pieces=False):
     rows = query.shape[0]
     scaled = query * jnp.bfloat16(SCALE)
     left = half_lanes(scaled.shape)
     zero = jnp.zeros_like(scaled)
     both = jnp.concatenate((jnp.where(left, scaled, zero), jnp.where(left, zero, scaled)), axis=0)
     scores = lax.dot_general(both, key, (((1,), (1,)), ((), ())), preferred_element_type=jnp.float32)
+    if pieces:
+        row = lax.broadcasted_iota(jnp.int32, scores.shape, 0)
+        row = jnp.where(row >= rows, row - rows, row)
+        col = lax.broadcasted_iota(jnp.int32, scores.shape, 1)
+        scores = jnp.where((row < 32) == ((col & 63) < 32), scores, NEVER)
     row_max = jnp.max(scores, axis=1, keepdims=True)
     weights = jnp.exp(scores - row_max).astype(jnp.bfloat16)
     wide = jnp.concatenate((value, jnp.ones_like(value)), axis=1)
@@ -81,10 +87,10 @@
     q_ref[...] = jnp.dot(means, q_in[...], preferred_element_type=jnp.float32).astype(jnp.bfloat16)
 
 
-def pack_kernel(kv4_ref, far5_ref, near5_ref, out_ref):
-    out_ref[0:32, :] = kv4_ref[...]
-    out_ref[32:48, :] = far5_ref[...]
-    out_ref[48:64, :] = near5_ref[...]
+def pack_kernel(kv4_ref, near5_ref, far5_ref, after3_ref, after2_ref, own_ref):
+    own_ref[0:32, :] = kv4_ref[...]
+    own_ref[32:48, :] = near5_ref[...]
+    own_ref[48:64, :] = far5_ref[...]
 
 
 def near_kernel(q_ref, k_ref, v_ref, top_ref, total_ref, sum_ref):
@@ -116,28 +122,32 @@
         )
 
 
+def partial_kernel(q_ref, own_ref, one_ref, two_ref, top_ref, total_ref, sum_ref):
+    width = q_ref.shape[1]
+    parts = (own_ref, one_ref, two_ref)
+    for pair in range(4):
+        cols = slice(pair * LANES, (pair + 1) * LANES)
+        vcols = slice(width + pair * LANES, width + (pair + 1) * LANES)
+        key = jnp.concatenate([part[0:64, cols] for part in parts], axis=0)
+        value = jnp.concatenate([part[0:64, vcols] for part in parts], axis=0)
+        top_ref[:, cols], total_ref[:, cols], sum_ref[:, cols] = attend_pair(q_ref[192:240, cols], key, value, True)
+
+
 def last_kernel(
-    q_ref, one_ref, two_ref, three_ref, four_ref, top_ref, total_ref, sum_ref, w_ref, mine_ref, send_ref, scratch_ref
+    q_ref, part_ref, far_top, far_total, far_sum, top_ref, total_ref, sum_ref, w_ref, mine_ref, send_ref, *scratch
 ):
     core = lax.axis_index("head")
     width = q_ref.shape[1]
-    parts = (one_ref, two_ref, three_ref, four_ref)
     pieces = []
     for pair in range(4):
         cols = slice(pair * LANES, (pair + 1) * LANES)
         vcols = slice(width + pair * LANES, width + (pair + 1) * LANES)
-        key4, value4, key5, value5 = [
-            jnp.concatenate([part[rows, lanes] for part in parts], axis=0)
-            for rows in (slice(0, 32), slice(32, 64))
-            for lanes in (cols, vcols)
-        ]
-        level4 = attend_pair(q_ref[192:224, cols], key4, value4)
-        level5 = attend_pair(q_ref[224:240, cols], key5, value5)
-        double = spread(scratch_ref, 16, 2)
-        far = merge(level4, [double(part) for part in level5], 2.0)
-        eight = spread(scratch_ref, 32, 8)
-        near = (top_ref[:, cols], total_ref[:, cols], sum_ref[:, cols])
-        near = merge(near, [eight(part) for part in far], 8.0)
+        piece = attend_pair(q_ref[192:240, cols], part_ref[:, cols], part_ref[:, vcols], True)
+        far = merge((far_top[:, cols], far_total[:, cols], far_sum[:, cols]), piece, 1.0)
+        level5 = [spread(ref, 16, 2)(part[32:48]) for ref, part in zip(scratch[6 * pair :], far)]
+        level4 = merge([part[0:32] for part in far], level5, 2.0)
+        far = [spread(ref, 32, 8)(part) for ref, part in zip(scratch[6 * pair + 3 :], level4)]
+        near = merge((top_ref[:, cols], total_ref[:, cols], sum_ref[:, cols]), far, 8.0)
         pieces.append((near[2] / near[1]).astype(jnp.bfloat16))
     attention = jnp.concatenate(pieces, axis=1)
     half = w_ref.shape[1] // 2
@@ -164,8 +174,7 @@
     return 11 - place if place // 4 in (0, 2) else 19 - place
 
 
-def call(kernel, name, outs, scratch=(), flops=0, moved_bytes=1_000_000, exps=0, in_specs=None, limit=VMEM_LIMIT):
-    given = {} if in_specs is None else {"in_specs": in_specs}
+def call(kernel, name, outs, scratch=(), flops=0, moved_bytes=1_000_000, exps=0, limit=VMEM_LIMIT, **more):
     return pl.pallas_call(
         kernel,
         out_shape=outs,
@@ -173,7 +182,7 @@
         compiler_params=params(limit),
         cost_estimate=pl.CostEstimate(flops=flops, bytes_accessed=moved_bytes, transcendentals=exps),
         name=name,
-        **given,
+        **more,
     )
 
 
@@ -191,15 +200,21 @@
         in_specs=[pl.BlockSpec(memory_space=pltpu.HBM)] * 3,
         limit=63 * 1024 * 1024,
     )(queries, key_rows, value_rows)
-    far5 = moved(kv5, far_partner)
     far4 = moved(kv4, flip(4))
     near5 = moved(kv5, flip(12))
+    far5 = moved(kv5, far_partner)
     kv3a = moved(kv3, flip(2))
     kv2_got = moved(kv2, flip(1))
     near = call(near_kernel, "near", fields, flops=8 * 256 * 256 * 64 * 4, exps=8 * 256 * 256)(
         queries, key_rows, value_rows
     )
-    own = call(pack_kernel, "pack", shape((64, 2 * width), bf16))(far4, far5, near5)
+    whole, anywhere = pl.BlockSpec(memory_space=pltpu.VMEM), pl.BlockSpec(memory_space=pl.ANY)
+    own = call(
+        pack_kernel,
+        "pack",
+        shape((64, 2 * width), bf16),
+        in_specs=(whole, whole, whole, anywhere, anywhere),
+    )(far4, near5, far5, kv3a, kv2_got)
     two = moved(own, flip(2))
     one = moved(own, flip(1))
     kv3b = moved(kv3a, flip(1))
@@ -207,14 +222,17 @@
     near = call(
         middle_kernel, "middle", fields, [pltpu.VMEM((256, LANES), f32)], flops=300_000_000, exps=8 * 256 * 200
     )(coarse_q, kv2_got, kv3a, kv3b, *near)
+    far = call(partial_kernel, "partial", (shape((48, width), f32),) * 3, flops=60_000_000, exps=8 * 48 * 192)(
+        coarse_q, own, one, two
+    )
     mine, send = call(
         last_kernel,
         "last",
         (shape((rows, width), bf16),) * 2,
-        [pltpu.VMEM((256, LANES), f32)],
+        ([pltpu.VMEM((32, LANES), f32)] * 3 + [pltpu.VMEM((256, LANES), f32)] * 3) * 4,
         flops=600_000_000,
         exps=8 * 256 * 100,
-    )(coarse_q, own, one, two, three, *near, out_weight)
+    )(coarse_q, three, *far, *near, out_weight)
     fetched = lax.ppermute(send, "head", [(0, 1), (1, 0)])
     return (mine.astype(f32) + fetched.astype(f32)).astype(bf16)
 

time: 58.8 us -> 62.4 us (1.061)
  waiting for transfers between devices: 5.28 us -> 9.59 us
    ppermute x9, waiting for transfers between devices: 4.14 us -> 8.45 us  [moved(): lax.ppermute(block, 'seq', [(i, i - i % RING + partner(i % RING)) for i i...]
    ppermute x9, starting transfers between devices: 39.4 us -> 38.7 us  [moved(): lax.ppermute(block, 'seq', [(i, i - i % RING + partner(i % RING)) for i i...]
    pallas_call x2 -> x3, Pallas kernels: 2.57 us -> 2.49 us  [the longest x1 1.32 us: body(): call(last_kernel, 'last', (shape((rows, width), bf16),) * 2, ([pltpu.VMEM...]
  transfers between devices with their start and end apart: 10 -> 10, of which waited for: 4 -> 4; matrix products, arithmetic and copies ran while one was open for 0% -> 0% of each run, Pallas kernels for 4% -> 6%
where the time goes in v2:
time: 62.4 us; the launch traced here: 62 us
  starting transfers between devices  44.1 us (71%)
  waiting for transfers between devices  9.59 us (15%)
  Pallas kernels  7.37 us (12%)
  other arithmetic  0.77 us (1%)
    ppermute x9, starting transfers between devices, moved(): lax.ppermute(block, 'seq', [(i, i - i % RING + partner(i % RING)) for i i...  38.7 us
    ppermute x9, waiting for transfers between devices, moved(): lax.ppermute(block, 'seq', [(i, i - i % RING + partner(i % RING)) for i i...  8.45 us
    ppermute x1, starting transfers between devices, body(): fetched = lax.ppermute(send, 'head', [(0, 1), (1, 0)])  5.33 us
    pallas_call x1, Pallas kernels, body(): call(coarse_kernel, 'coarse', (shape((240, width), bf16),) + tuple((shape...  2.4 us
    pallas_call x1, Pallas kernels, body(): call(middle_kernel, 'middle', fields, [pltpu.VMEM((256, LANES), f32)], fl...  1.59 us
    pallas_call x1, Pallas kernels, body(): call(last_kernel, 'last', (shape((rows, width), bf16),) * 2, ([pltpu.VMEM...  1.32 us
  transfers between devices with their start and end apart: 10, of which 4 were waited for; matrix products, arithmetic and copies ran while one was open for 0% of the time, Pallas kernels for 6%

profile of v2, /device:TPU:1, one launch (start us, length us, event | category | flops | bytes accessed | tf_op | source)
XLA Modules:
  0.0 62.0 jit_solution(11614782464791685739)
XLA Ops:
  0.0 0.0 copy-start.4
  0.0 2.4 %coarse.1 = (bf16[240,512]{1,0:T(8,128)(2,1)}, bf16[128,1024]{1,0:T(8,128)(2,1)}, bf16[64,1024]{1,0:T(8,128)(2,1)}, bf16[32,1024]{1,0:T(8,128)(2,1)}, bf16[16,1024]{1,0:T(8,128)(2,1)}) custom-call(bf16[256,512]{1,0:T(8,128)(2,1)} %q_ref.1, bf16[256,512]{1,0:T(8,128)(2,1)} %k_ref.1, bf16[256,512]{1,0:T(8,128)(2,1)} %v_ref.1), custom_call_target="tpu_custom_call" | custom-call | flops 188743680 | bytes 1000000 | tf_op jit(solution)/shard_map/coarse/pallas_call | solution.py:194
  2.4 4.4 %collective-permute-start.4 = (bf16[128,1024]{1,0:T(8,128)(2,1)}, bf16[128,1024]{1,0:T(8,128)(2,1)S(1)}, u32[]{:S(2)}, u32[]{:S(2)}) collective-permute-start(bf16[128,1024]{1,0:T(8,128)(2,1)} %get-tuple-element.25), channel_id=1, source_target_pairs={{0,2},{2,0},{4,6},{6,4},{8,10},{10,8},{12,14},{14,12},{16,18},{18,... | collective-permute-start | bytes 786440 | tf_op jit(solution)/shard_map/ppermute | solution.py:166
  6.8 4.9 %collective-permute-start.3 = (bf16[64,1024]{1,0:T(8,128)(2,1)}, bf16[64,1024]{1,0:T(8,128)(2,1)S(1)}, u32[]{:S(2)}, u32[]{:S(2)}) collective-permute-start(bf16[64,1024]{1,0:T(8,128)(2,1)} %get-tuple-element.24), channel_id=1, source_target_pairs={{0,4},{2,6},{4,0},{6,2},{8,12},{10,14},{12,8},{14,10},{16,20},{18,... | collective-permute-start | bytes 393224 | tf_op jit(solution)/shard_map/ppermute | solution.py:166
  11.7 8.8 %collective-permute-start = (bf16[32,1024]{1,0:T(8,128)(2,1)}, bf16[32,1024]{1,0:T(8,128)(2,1)S(1)}, u32[]{:S(2)}, u32[]{:S(2)}) collective-permute-start(bf16[32,1024]{1,0:T(8,128)(2,1)} %get-tuple-element.22), channel_id=1, source_target_pairs={{0,8},{2,10},{4,12},{6,14},{8,0},{10,2},{12,4},{14,6},{16,24},{18,... | collective-permute-start | bytes 196616 | tf_op jit(solution)/shard_map/ppermute | solution.py:166
  20.5 0.0 copy-start.2
  20.5 0.0 copy-start.3
  20.5 6.7 %collective-permute-start.2 = (bf16[16,1024]{1,0:T(8,128)(2,1)}, bf16[16,1024]{1,0:T(8,128)(2,1)S(1)}, u32[]{:S(2)}, u32[]{:S(2)}) collective-permute-start(bf16[16,1024]{1,0:T(8,128)(2,1)} %get-tuple-element.23), channel_id=1, source_target_pairs={{0,22},{2,20},{4,18},{6,16},{8,30},{10,28},{12,26},{14,24},{16,6},... | collective-permute-start | bytes 98312 | tf_op jit(solution)/shard_map/ppermute | solution.py:166
  27.3 1.9 %collective-permute-start.1 = (bf16[16,1024]{1,0:T(8,128)(2,1)}, bf16[16,1024]{1,0:T(8,128)(2,1)S(1)}, u32[]{:S(2)}, u32[]{:S(2)}) collective-permute-start(bf16[16,1024]{1,0:T(8,128)(2,1)} %get-tuple-element.23), channel_id=1, source_target_pairs={{0,24},{2,26},{4,28},{6,30},{8,16},{10,18},{12,20},{14,22},{16,8},... | collective-permute-start | bytes 98312 | tf_op jit(solution)/shard_map/ppermute | solution.py:166
  29.2 3.8 %collective-permute-done.2.far5_ref = bf16[16,1024]{1,0:T(8,128)(2,1)S(1)} collective-permute-done((bf16[16,1024]{1,0:T(8,128)(2,1)}, bf16[16,1024]{1,0:T(8,128)(2,1)S(1)}, u32[]{:S(2)}, u32[]{:S(2)}) %collective-permute-start.2) | collective-permute-done | bytes 32800 | tf_op jit(solution)/shard_map/ppermute | solution.py:166
  33.0 3.1 %collective-permute-done.1.near5_ref = bf16[16,1024]{1,0:T(8,128)(2,1)S(1)} collective-permute-done((bf16[16,1024]{1,0:T(8,128)(2,1)}, bf16[16,1024]{1,0:T(8,128)(2,1)S(1)}, u32[]{:S(2)}, u32[]{:S(2)}) %collective-permute-start.1) | collective-permute-done | bytes 32800 | tf_op jit(solution)/shard_map/ppermute | solution.py:166
  36.1 0.0 collective-permute-done.kv4_ref
  36.1 0.0 collective-permute-done.3.after3_ref.kv3a_ref
  36.1 0.0 collective-permute-done.4.after2_ref.kv2_ref
  36.1 0.0 copy-start
  36.1 4.8 %collective-permute-start.5 = (bf16[64,1024]{1,0:T(8,128)(2,1)S(1)}, bf16[64,1024]{1,0:T(8,128)(2,1)S(1)}, u32[]{:S(2)}, u32[]{:S(2)}) collective-permute-start(bf16[64,1024]{1,0:T(8,128)(2,1)S(1)} %pack.1.own_ref), channel_id=1, source_target_pairs={{0,4},{2,6},{4,0},{6,2},{8,12},{10,14},{12,8},{14,10},{16,20},{18,... | collective-permute-start | bytes 393224 | tf_op jit(solution)/shard_map/ppermute | solution.py:166
  40.9 1.9 %collective-permute-start.8 = (bf16[64,1024]{1,0:T(8,128)(2,1)S(1)}, bf16[64,1024]{1,0:T(8,128)(2,1)S(1)}, u32[]{:S(2)}, u32[]{:S(2)}) collective-permute-start(bf16[64,1024]{1,0:T(8,128)(2,1)S(1)} %collective-permute-done.3.after3_ref.kv3a_ref), channel_id=1, source_target_pairs={{0,2},{2,0},{4,6},{6,4},{8,10},{10,8},{12,14},{14,12},{16,18},{18,... | collective-permute-start | bytes 393224 | tf_op jit(solution)/shard_map/ppermute | solution.py:166
  42.9 3.4 %collective-permute-start.7 = (bf16[64,1024]{1,0:T(8,128)(2,1)S(1)}, bf16[64,1024]{1,0:T(8,128)(2,1)S(1)}, u32[]{:S(2)}, u32[]{:S(2)}) collective-permute-start(bf16[64,1024]{1,0:T(8,128)(2,1)S(1)} %pack.1.own_ref), channel_id=1, source_target_pairs={{0,2},{2,0},{4,6},{6,4},{8,10},{10,8},{12,14},{14,12},{16,18},{18,... | collective-permute-start | bytes 393224 | tf_op jit(solution)/shard_map/ppermute | solution.py:166
  46.2 0.0 collective-permute-done.5.two_ref
  46.2 1.9 %collective-permute-start.6 = (bf16[64,1024]{1,0:T(8,128)(2,1)S(1)}, bf16[64,1024]{1,0:T(8,128)(2,1)S(1)}, u32[]{:S(2)}, u32[]{:S(2)}) collective-permute-start(bf16[64,1024]{1,0:T(8,128)(2,1)S(1)} %collective-permute-done.5.two_ref), channel_id=1, source_target_pairs={{0,2},{2,0},{4,6},{6,4},{8,10},{10,8},{12,14},{14,12},{16,18},{18,... | collective-permute-start | bytes 393224 | tf_op jit(solution)/shard_map/ppermute | solution.py:166
  48.2 0.0 copy-done.4
  48.2 0.0 copy-done.2
  48.2 0.0 copy-done.3
  48.2 0.9 %near.1 = (f32[256,512]{1,0:T(8,128)S(1)}, f32[256,512]{1,0:T(8,128)S(1)}, f32[256,512]{1,0:T(8,128)S(1)}) custom-call(bf16[256,512]{1,0:T(8,128)(2,1)S(1)} %copy-done.2, bf16[256,512]{1,0:T(8,128)(2,1)S(1)} %copy-done.3, bf16[256,512]{1,0:T(8,128)(2,1)S(1)} %copy-done.4), custom_call_target="tpu_custom_call" | custom-call | flops 134217728 | bytes 1000000 | tf_op jit(solution)/shard_map/near/pallas_call | solution.py:208
  49.1 0.0 collective-permute-done.8.kv3b_ref
  49.1 0.0 copy-done
  49.1 0.0 copy-start.1
  49.1 1.6 %middle.1 = (f32[256,512]{1,0:T(8,128)S(1)}, f32[256,512]{1,0:T(8,128)S(1)}, f32[256,512]{1,0:T(8,128)S(1)}) custom-call(bf16[240,512]{1,0:T(8,128)(2,1)S(1)} %copy-done, bf16[128,1024]{1,0:T(8,128)(2,1)S(1)} %collective-permute-done.4.after2_ref.kv2_ref, bf16[64,1024]{1,0:T(8,128)(2,1)S(1)} %collective-permute-done.3.after3_ref.kv3a_ref, ...), custom_call_target="tpu_custom_call" | custom-call | flops 300000000 | bytes 1000000 | tf_op jit(solution)/shard_map/middle/pallas_call | solution.py:222
  50.7 0.0 collective-permute-done.7.one_ref
  50.7 1.2 %partial.1 = (f32[48,512]{1,0:T(8,128)S(1)}, f32[48,512]{1,0:T(8,128)S(1)}, f32[48,512]{1,0:T(8,128)S(1)}) custom-call(bf16[240,512]{1,0:T(8,128)(2,1)S(1)} %copy-done, bf16[64,1024]{1,0:T(8,128)(2,1)S(1)} %pack.1.own_ref, bf16[64,1024]{1,0:T(8,128)(2,1)S(1)} %collective-permute-done.7.one_ref, bf16[64,1024]{1,0:T(8,128)(2,1)S(1)} %collective-permute-done.5.two_ref), custom_call_target="tpu_custom_call" | custom-call | flops 60000000 | bytes 1000000 | tf_op jit(solution)/shard_map/partial/pallas_call | solution.py:225
  51.9 1.6 %collective-permute-done.6.part_ref = bf16[64,1024]{1,0:T(8,128)(2,1)S(1)} collective-permute-done((bf16[64,1024]{1,0:T(8,128)(2,1)S(1)}, bf16[64,1024]{1,0:T(8,128)(2,1)S(1)}, u32[]{:S(2)}, u32[]{:S(2)}) %collective-permute-start.6) | collective-permute-done | bytes 131104 | tf_op jit(solution)/shard_map/ppermute | solution.py:166
  53.5 0.0 copy-done.1
  53.5 1.3 %last.1 = (bf16[256,512]{1,0:T(8,128)(2,1)S(1)}, bf16[256,512]{1,0:T(8,128)(2,1)S(1)}) custom-call(bf16[240,512]{1,0:T(8,128)(2,1)S(1)} %copy-done, bf16[64,1024]{1,0:T(8,128)(2,1)S(1)} %collective-permute-done.6.part_ref, f32[48,512]{1,0:T(8,128)S(1)} %get-tuple-element.26.far_top, f32[48,512]{1,0:T(8,128)S(1)} %get-tuple-element.27.far_total, ...), custom_call_target="tpu_custom_call" | custom-call | flops 600000000 | bytes 1000000 | tf_op jit(solution)/shard_map/last/pallas_call | solution.py:228
  54.8 5.3 %collective-permute-start.9 = (bf16[256,512]{1,0:T(8,128)(2,1)S(1)}, bf16[256,512]{1,0:T(8,128)(2,1)S(1)}, u32[]{:S(2)}, u32[]{:S(2)}) collective-permute-start(bf16[256,512]{1,0:T(8,128)(2,1)S(1)} %get-tuple-element.36), channel_id=1, source_target_pairs={{0,1},{1,0},{2,3},{3,2},{4,5},{5,4},{6,7},{7,6},{8,9},{9,8},{10,11... | collective-permute-start | bytes 786440 | tf_op jit(solution)/shard_map/ppermute | solution.py:236
  60.1 1.1 %collective-permute-done.9 = bf16[256,512]{1,0:T(8,128)(2,1)S(1)} collective-permute-done((bf16[256,512]{1,0:T(8,128)(2,1)S(1)}, bf16[256,512]{1,0:T(8,128)(2,1)S(1)}, u32[]{:S(2)}, u32[]{:S(2)}) %collective-permute-start.9) | collective-permute-done | bytes 262176 | tf_op jit(solution)/shard_map/ppermute | solution.py:236
  61.3 0.8 %add_convert_fusion = bf16[256,512]{1,0:T(8,128)(2,1)} fusion(bf16[256,512]{1,0:T(8,128)(2,1)S(1)} %collective-permute-done.9, bf16[256,512]{1,0:T(8,128)(2,1)S(1)} %get-tuple-element.35), kind=kLoop, calls=%fused_computation | loop fusion | flops 524288 | bytes 786432 | tf_op jit(solution)/shard_map/convert_element_type | solution.py:237
  (1 shorter events, 0.0 us)
Async XLA Ops:
  0.0 48.2 %copy-start.4 = (bf16[256,512]{1,0:T(8,128)(2,1)S(1)}, bf16[256,512]{1,0:T(8,128)(2,1)}, u32[]{:S(2)}) copy-start(bf16[256,512]{1,0:T(8,128)(2,1)} %v_ref.1) | copy-start | bytes 786436
  2.4 33.7 %collective-permute-start.4 = (bf16[128,1024]{1,0:T(8,128)(2,1)}, bf16[128,1024]{1,0:T(8,128)(2,1)S(1)}, u32[]{:S(2)}, u32[]{:S(2)}) collective-permute-start(bf16[128,1024]{1,0:T(8,128)(2,1)} %get-tuple-element.25), channel_id=1, source_target_pairs={{0,2},{2,0},{4,6},{6,4},{8,10},{10,8},{12,14},{14,12},{16,18},{18,... | collective-permute-start | bytes 786440 | tf_op jit(solution)/shard_map/ppermute | solution.py:166
  6.8 29.3 %collective-permute-start.3 = (bf16[64,1024]{1,0:T(8,128)(2,1)}, bf16[64,1024]{1,0:T(8,128)(2,1)S(1)}, u32[]{:S(2)}, u32[]{:S(2)}) collective-permute-start(bf16[64,1024]{1,0:T(8,128)(2,1)} %get-tuple-element.24), channel_id=1, source_target_pairs={{0,4},{2,6},{4,0},{6,2},{8,12},{10,14},{12,8},{14,10},{16,20},{18,... | collective-permute-start | bytes 393224 | tf_op jit(solution)/shard_map/ppermute | solution.py:166
  11.7 24.4 %collective-permute-start = (bf16[32,1024]{1,0:T(8,128)(2,1)}, bf16[32,1024]{1,0:T(8,128)(2,1)S(1)}, u32[]{:S(2)}, u32[]{:S(2)}) collective-permute-start(bf16[32,1024]{1,0:T(8,128)(2,1)} %get-tuple-element.22), channel_id=1, source_target_pairs={{0,8},{2,10},{4,12},{6,14},{8,0},{10,2},{12,4},{14,6},{16,24},{18,... | collective-permute-start | bytes 196616 | tf_op jit(solution)/shard_map/ppermute | solution.py:166
  20.5 27.7 %copy-start.2 = (bf16[256,512]{1,0:T(8,128)(2,1)S(1)}, bf16[256,512]{1,0:T(8,128)(2,1)}, u32[]{:S(2)}) copy-start(bf16[256,512]{1,0:T(8,128)(2,1)} %q_ref.1) | copy-start | bytes 786436
  20.5 27.6 %copy-start.3 = (bf16[256,512]{1,0:T(8,128)(2,1)S(1)}, bf16[256,512]{1,0:T(8,128)(2,1)}, u32[]{:S(2)}) copy-start(bf16[256,512]{1,0:T(8,128)(2,1)} %k_ref.1) | copy-start | bytes 786436
  20.5 12.5 %collective-permute-start.2 = (bf16[16,1024]{1,0:T(8,128)(2,1)}, bf16[16,1024]{1,0:T(8,128)(2,1)S(1)}, u32[]{:S(2)}, u32[]{:S(2)}) collective-permute-start(bf16[16,1024]{1,0:T(8,128)(2,1)} %get-tuple-element.23), channel_id=1, source_target_pairs={{0,22},{2,20},{4,18},{6,16},{8,30},{10,28},{12,26},{14,24},{16,6},... | collective-permute-start | bytes 98312 | tf_op jit(solution)/shard_map/ppermute | solution.py:166
  27.3 8.8 %collective-permute-start.1 = (bf16[16,1024]{1,0:T(8,128)(2,1)}, bf16[16,1024]{1,0:T(8,128)(2,1)S(1)}, u32[]{:S(2)}, u32[]{:S(2)}) collective-permute-start(bf16[16,1024]{1,0:T(8,128)(2,1)} %get-tuple-element.23), channel_id=1, source_target_pairs={{0,24},{2,26},{4,28},{6,30},{8,16},{10,18},{12,20},{14,22},{16,8},... | collective-permute-start | bytes 98312 | tf_op jit(solution)/shard_map/ppermute | solution.py:166
  36.1 13.0 %copy-start = (bf16[240,512]{1,0:T(8,128)(2,1)S(1)}, bf16[240,512]{1,0:T(8,128)(2,1)}, u32[]{:S(2)}) copy-start(bf16[240,512]{1,0:T(8,128)(2,1)} %get-tuple-element.21.q_ref) | copy-start | bytes 737284
  36.1 10.1 %collective-permute-start.5 = (bf16[64,1024]{1,0:T(8,128)(2,1)S(1)}, bf16[64,1024]{1,0:T(8,128)(2,1)S(1)}, u32[]{:S(2)}, u32[]{:S(2)}) collective-permute-start(bf16[64,1024]{1,0:T(8,128)(2,1)S(1)} %pack.1.own_ref), channel_id=1, source_target_pairs={{0,4},{2,6},{4,0},{6,2},{8,12},{10,14},{12,8},{14,10},{16,20},{18,... | collective-permute-start | bytes 393224 | tf_op jit(solution)/shard_map/ppermute | solution.py:166
  40.9 8.2 %collective-permute-start.8 = (bf16[64,1024]{1,0:T(8,128)(2,1)S(1)}, bf16[64,1024]{1,0:T(8,128)(2,1)S(1)}, u32[]{:S(2)}, u32[]{:S(2)}) collective-permute-start(bf16[64,1024]{1,0:T(8,128)(2,1)S(1)} %collective-permute-done.3.after3_ref.kv3a_ref), channel_id=1, source_target_pairs={{0,2},{2,0},{4,6},{6,4},{8,10},{10,8},{12,14},{14,12},{16,18},{18,... | collective-permute-start | bytes 393224 | tf_op jit(solution)/shard_map/ppermute | solution.py:166
  42.9 7.9 %collective-permute-start.7 = (bf16[64,1024]{1,0:T(8,128)(2,1)S(1)}, bf16[64,1024]{1,0:T(8,128)(2,1)S(1)}, u32[]{:S(2)}, u32[]{:S(2)}) collective-permute-start(bf16[64,1024]{1,0:T(8,128)(2,1)S(1)} %pack.1.own_ref), channel_id=1, source_target_pairs={{0,2},{2,0},{4,6},{6,4},{8,10},{10,8},{12,14},{14,12},{16,18},{18,... | collective-permute-start | bytes 393224 | tf_op jit(solution)/shard_map/ppermute | solution.py:166
  46.2 7.2 %collective-permute-start.6 = (bf16[64,1024]{1,0:T(8,128)(2,1)S(1)}, bf16[64,1024]{1,0:T(8,128)(2,1)S(1)}, u32[]{:S(2)}, u32[]{:S(2)}) collective-permute-start(bf16[64,1024]{1,0:T(8,128)(2,1)S(1)} %collective-permute-done.5.two_ref), channel_id=1, source_target_pairs={{0,2},{2,0},{4,6},{6,4},{8,10},{10,8},{12,14},{14,12},{16,18},{18,... | collective-permute-start | bytes 393224 | tf_op jit(solution)/shard_map/ppermute | solution.py:166
  49.1 4.3 %copy-start.1 = (bf16[512,1024]{1,0:T(8,128)(2,1)S(1)}, bf16[512,1024]{1,0:T(8,128)(2,1)}, u32[]{:S(2)}) copy-start(bf16[512,1024]{1,0:T(8,128)(2,1)} %w_ref.1) | copy-start | bytes 3145732
  54.8 6.5 %collective-permute-start.9 = (bf16[256,512]{1,0:T(8,128)(2,1)S(1)}, bf16[256,512]{1,0:T(8,128)(2,1)S(1)}, u32[]{:S(2)}, u32[]{:S(2)}) collective-permute-start(bf16[256,512]{1,0:T(8,128)(2,1)S(1)} %get-tuple-element.36), channel_id=1, source_target_pairs={{0,1},{1,0},{2,3},{3,2},{4,5},{5,4},{6,7},{7,6},{8,9},{9,8},{10,11... | collective-permute-start | bytes 786440 | tf_op jit(solution)/shard_map/ppermute | solution.py:236

commit v3 on v2

--- a/solution.py
+++ b/solution.py
@@ -87,10 +87,10 @@
     q_ref[...] = jnp.dot(means, q_in[...], preferred_element_type=jnp.float32).astype(jnp.bfloat16)
 
 
-def pack_kernel(kv4_ref, near5_ref, far5_ref, after3_ref, after2_ref, own_ref):
-    own_ref[0:32, :] = kv4_ref[...]
-    own_ref[32:48, :] = near5_ref[...]
-    own_ref[48:64, :] = far5_ref[...]
+def pack_kernel(kv4_ref, near5_ref, far5_ref, out_ref):
+    out_ref[0:32, :] = kv4_ref[...]
+    out_ref[32:48, :] = near5_ref[...]
+    out_ref[48:64, :] = far5_ref[...]
 
 
 def near_kernel(q_ref, k_ref, v_ref, top_ref, total_ref, sum_ref):
@@ -128,13 +128,13 @@
     for pair in range(4):
         cols = slice(pair * LANES, (pair + 1) * LANES)
         vcols = slice(width + pair * LANES, width + (pair + 1) * LANES)
-        key = jnp.concatenate([part[0:64, cols] for part in parts], axis=0)
-        value = jnp.concatenate([part[0:64, vcols] for part in parts], axis=0)
+        key = jnp.concatenate([part[:, cols] for part in parts], axis=0)
+        value = jnp.concatenate([part[:, vcols] for part in parts], axis=0)
         top_ref[:, cols], total_ref[:, cols], sum_ref[:, cols] = attend_pair(q_ref[192:240, cols], key, value, True)
 
 
 def last_kernel(
-    q_ref, part_ref, far_top, far_total, far_sum, top_ref, total_ref, sum_ref, w_ref, mine_ref, send_ref, *scratch
+    q_ref, part_ref, far_top, far_total, far_sum, top_ref, total_ref, sum_ref, w_ref, attention_ref, send_ref, *scratch
 ):
     core = lax.axis_index("head")
     width = q_ref.shape[1]
@@ -150,15 +150,20 @@
         near = merge((top_ref[:, cols], total_ref[:, cols], sum_ref[:, cols]), far, 8.0)
         pieces.append((near[2] / near[1]).astype(jnp.bfloat16))
     attention = jnp.concatenate(pieces, axis=1)
+    attention_ref[...] = attention
     half = w_ref.shape[1] // 2
     away = pl.multiple_of((1 - core) * half, half)
-    home = pl.multiple_of(core * half, half)
     send_ref[...] = jnp.dot(attention, w_ref[:, pl.ds(away, half)], preferred_element_type=jnp.float32).astype(
         jnp.bfloat16
     )
-    mine_ref[...] = jnp.dot(attention, w_ref[:, pl.ds(home, half)], preferred_element_type=jnp.float32).astype(
-        jnp.bfloat16
-    )
+
+
+def mine_kernel(attention_ref, w_ref, mine_ref):
+    half = w_ref.shape[1] // 2
+    home = pl.multiple_of(lax.axis_index("head") * half, half)
+    mine_ref[...] = jnp.dot(
+        attention_ref[...], w_ref[:, pl.ds(home, half)], preferred_element_type=jnp.float32
+    ).astype(jnp.bfloat16)
 
 
 def moved(block, partner):
@@ -174,7 +179,8 @@
     return 11 - place if place // 4 in (0, 2) else 19 - place
 
 
-def call(kernel, name, outs, scratch=(), flops=0, moved_bytes=1_000_000, exps=0, limit=VMEM_LIMIT, **more):
+def call(kernel, name, outs, scratch=(), flops=0, moved_bytes=1_000_000, exps=0, in_specs=None, limit=VMEM_LIMIT):
+    given = {} if in_specs is None else {"in_specs": in_specs}
     return pl.pallas_call(
         kernel,
         out_shape=outs,
@@ -182,7 +188,7 @@
         compiler_params=params(limit),
         cost_estimate=pl.CostEstimate(flops=flops, bytes_accessed=moved_bytes, transcendentals=exps),
         name=name,
-        **more,
+        **given,
     )
 
 
@@ -208,13 +214,7 @@
     near = call(near_kernel, "near", fields, flops=8 * 256 * 256 * 64 * 4, exps=8 * 256 * 256)(
         queries, key_rows, value_rows
     )
-    whole, anywhere = pl.BlockSpec(memory_space=pltpu.VMEM), pl.BlockSpec(memory_space=pl.ANY)
-    own = call(
-        pack_kernel,
-        "pack",
-        shape((64, 2 * width), bf16),
-        in_specs=(whole, whole, whole, anywhere, anywhere),
-    )(far4, near5, far5, kv3a, kv2_got)
+    own = call(pack_kernel, "pack", shape((64, 2 * width), bf16))(far4, near5, far5)
     two = moved(own, flip(2))
     one = moved(own, flip(1))
     kv3b = moved(kv3a, flip(1))
@@ -225,7 +225,7 @@
     far = call(partial_kernel, "partial", (shape((48, width), f32),) * 3, flops=60_000_000, exps=8 * 48 * 192)(
         coarse_q, own, one, two
     )
-    mine, send = call(
+    attention, send = call(
         last_kernel,
         "last",
         (shape((rows, width), bf16),) * 2,
@@ -234,6 +234,7 @@
         exps=8 * 256 * 100,
     )(coarse_q, three, *far, *near, out_weight)
     fetched = lax.ppermute(send, "head", [(0, 1), (1, 0)])
+    mine = call(mine_kernel, "mine", shape((rows, width), bf16), flops=2 * 256 * 512 * 512)(attention, out_weight)
     return (mine.astype(f32) + fetched.astype(f32)).astype(bf16)
 
 

time: 62.4 us -> 57.4 us (0.920)
  waiting for transfers between devices: 9.59 us -> 3.83 us
    ppermute x9, waiting for transfers between devices: 8.45 us -> 3 us  [moved(): lax.ppermute(block, 'seq', [(i, i - i % RING + partner(i % RING)) for i i...]
    ppermute x9, starting transfers between devices: 38.7 us -> 39.4 us  [moved(): lax.ppermute(block, 'seq', [(i, i - i % RING + partner(i % RING)) for i i...]
  transfers between devices with their start and end apart: 10 -> 10, of which waited for: 4 -> 4; matrix products, arithmetic and copies ran while one was open for 0% -> 0% of each run, Pallas kernels for 6% -> 7%
where the time goes in v3:
time: 57.4 us; the launch traced here: 57 us
  starting transfers between devices  44.7 us (78%)
  Pallas kernels  7.52 us (13%)
  waiting for transfers between devices  3.83 us (7%)
  other arithmetic  0.77 us (1%)
    ppermute x9, starting transfers between devices, moved(): lax.ppermute(block, 'seq', [(i, i - i % RING + partner(i % RING)) for i i...  39.4 us
    ppermute x1, starting transfers between devices, body(): fetched = lax.ppermute(send, 'head', [(0, 1), (1, 0)])  5.24 us
    ppermute x9, waiting for transfers between devices, moved(): lax.ppermute(block, 'seq', [(i, i - i % RING + partner(i % RING)) for i i...  3 us
    pallas_call x1, Pallas kernels, body(): call(coarse_kernel, 'coarse', (shape((240, width), bf16),) + tuple((shape...  2.41 us
    pallas_call x1, Pallas kernels, body(): call(middle_kernel, 'middle', fields, [pltpu.VMEM((256, LANES), f32)], fl...  1.59 us
    pallas_call x1, Pallas kernels, body(): call(partial_kernel, 'partial', (shape((48, width), f32),) * 3, flops=600...  1.15 us
    pallas_call x1, Pallas kernels, body(): call(last_kernel, 'last', (shape((rows, width), bf16),) * 2, ([pltpu.VMEM...  1.15 us
  transfers between devices with their start and end apart: 10, of which 4 were waited for; matrix products, arithmetic and copies ran while one was open for 0% of the time, Pallas kernels for 7%

profile of v3, /device:TPU:1, one launch (start us, length us, event | category | flops | bytes accessed | tf_op | source)
XLA Modules:
  0.0 57.0 jit_solution(14481574960259644180)
XLA Ops:
  0.0 0.0 copy-start.3
  0.0 0.0 copy-start.4
  0.0 2.4 %coarse.1 = (bf16[240,512]{1,0:T(8,128)(2,1)}, bf16[128,1024]{1,0:T(8,128)(2,1)}, bf16[64,1024]{1,0:T(8,128)(2,1)}, bf16[32,1024]{1,0:T(8,128)(2,1)}, bf16[16,1024]{1,0:T(8,128)(2,1)}) custom-call(bf16[256,512]{1,0:T(8,128)(2,1)} %q_ref.1, bf16[256,512]{1,0:T(8,128)(2,1)} %k_ref.1, bf16[256,512]{1,0:T(8,128)(2,1)} %v_ref.1), custom_call_target="tpu_custom_call" | custom-call | flops 188743680 | bytes 1000000 | tf_op jit(solution)/shard_map/coarse/pallas_call | solution.py:200
  2.4 0.0 copy-start.2
  2.4 9.8 %collective-permute-start = (bf16[32,1024]{1,0:T(8,128)(2,1)}, bf16[32,1024]{1,0:T(8,128)(2,1)S(1)}, u32[]{:S(2)}, u32[]{:S(2)}) collective-permute-start(bf16[32,1024]{1,0:T(8,128)(2,1)} %get-tuple-element.22), channel_id=1, source_target_pairs={{0,8},{2,10},{4,12},{6,14},{8,0},{10,2},{12,4},{14,6},{16,24},{18,... | collective-permute-start | bytes 196616 | tf_op jit(solution)/shard_map/ppermute | solution.py:171
  12.2 9.3 %collective-permute-start.2 = (bf16[16,1024]{1,0:T(8,128)(2,1)}, bf16[16,1024]{1,0:T(8,128)(2,1)S(1)}, u32[]{:S(2)}, u32[]{:S(2)}) collective-permute-start(bf16[16,1024]{1,0:T(8,128)(2,1)} %get-tuple-element.23), channel_id=1, source_target_pairs={{0,22},{2,20},{4,18},{6,16},{8,30},{10,28},{12,26},{14,24},{16,6},... | collective-permute-start | bytes 98312 | tf_op jit(solution)/shard_map/ppermute | solution.py:171
  21.5 1.9 %collective-permute-start.1 = (bf16[16,1024]{1,0:T(8,128)(2,1)}, bf16[16,1024]{1,0:T(8,128)(2,1)S(1)}, u32[]{:S(2)}, u32[]{:S(2)}) collective-permute-start(bf16[16,1024]{1,0:T(8,128)(2,1)} %get-tuple-element.23), channel_id=1, source_target_pairs={{0,24},{2,26},{4,28},{6,30},{8,16},{10,18},{12,20},{14,22},{16,8},... | collective-permute-start | bytes 98312 | tf_op jit(solution)/shard_map/ppermute | solution.py:171
  23.5 4.0 %collective-permute-start.7 = (bf16[64,1024]{1,0:T(8,128)(2,1)}, bf16[64,1024]{1,0:T(8,128)(2,1)S(1)}, u32[]{:S(2)}, u32[]{:S(2)}) collective-permute-start(bf16[64,1024]{1,0:T(8,128)(2,1)} %get-tuple-element.28), channel_id=1, source_target_pairs={{0,4},{2,6},{4,0},{6,2},{8,12},{10,14},{12,8},{14,10},{16,20},{18,... | collective-permute-start | bytes 393224 | tf_op jit(solution)/shard_map/ppermute | solution.py:171
  27.4 1.9 %collective-permute-start.6 = (bf16[128,1024]{1,0:T(8,128)(2,1)}, bf16[128,1024]{1,0:T(8,128)(2,1)S(1)}, u32[]{:S(2)}, u32[]{:S(2)}) collective-permute-start(bf16[128,1024]{1,0:T(8,128)(2,1)} %get-tuple-element.27), channel_id=1, source_target_pairs={{0,2},{2,0},{4,6},{6,4},{8,10},{10,8},{12,14},{14,12},{16,18},{18,... | collective-permute-start | bytes 786440 | tf_op jit(solution)/shard_map/ppermute | solution.py:171
  29.4 0.0 collective-permute-done.2.far5_ref
  29.4 1.0 %collective-permute-done.1.near5_ref = bf16[16,1024]{1,0:T(8,128)(2,1)S(1)} collective-permute-done((bf16[16,1024]{1,0:T(8,128)(2,1)}, bf16[16,1024]{1,0:T(8,128)(2,1)S(1)}, u32[]{:S(2)}, u32[]{:S(2)}) %collective-permute-start.1) | collective-permute-done | bytes 32800 | tf_op jit(solution)/shard_map/ppermute | solution.py:171
  30.4 0.0 collective-permute-done.kv4_ref
  30.4 0.0 copy-start.1
  30.5 4.8 %collective-permute-start.3 = (bf16[64,1024]{1,0:T(8,128)(2,1)S(1)}, bf16[64,1024]{1,0:T(8,128)(2,1)S(1)}, u32[]{:S(2)}, u32[]{:S(2)}) collective-permute-start(bf16[64,1024]{1,0:T(8,128)(2,1)S(1)} %pack.1.own_ref), channel_id=1, source_target_pairs={{0,4},{2,6},{4,0},{6,2},{8,12},{10,14},{12,8},{14,10},{16,20},{18,... | collective-permute-start | bytes 393224 | tf_op jit(solution)/shard_map/ppermute | solution.py:171
  35.2 1.9 %collective-permute-start.5 = (bf16[64,1024]{1,0:T(8,128)(2,1)S(1)}, bf16[64,1024]{1,0:T(8,128)(2,1)S(1)}, u32[]{:S(2)}, u32[]{:S(2)}) collective-permute-start(bf16[64,1024]{1,0:T(8,128)(2,1)S(1)} %pack.1.own_ref), channel_id=1, source_target_pairs={{0,2},{2,0},{4,6},{6,4},{8,10},{10,8},{12,14},{14,12},{16,18},{18,... | collective-permute-start | bytes 393224 | tf_op jit(solution)/shard_map/ppermute | solution.py:171
  37.2 0.0 collective-permute-done.7.kv3a_ref
  37.2 3.4 %collective-permute-start.8 = (bf16[64,1024]{1,0:T(8,128)(2,1)S(1)}, bf16[64,1024]{1,0:T(8,128)(2,1)S(1)}, u32[]{:S(2)}, u32[]{:S(2)}) collective-permute-start(bf16[64,1024]{1,0:T(8,128)(2,1)S(1)} %collective-permute-done.7.kv3a_ref), channel_id=1, source_target_pairs={{0,2},{2,0},{4,6},{6,4},{8,10},{10,8},{12,14},{14,12},{16,18},{18,... | collective-permute-start | bytes 393224 | tf_op jit(solution)/shard_map/ppermute | solution.py:171
  40.5 0.0 collective-permute-done.3.two_ref
  40.6 2.5 %collective-permute-start.4 = (bf16[64,1024]{1,0:T(8,128)(2,1)S(1)}, bf16[64,1024]{1,0:T(8,128)(2,1)S(1)}, u32[]{:S(2)}, u32[]{:S(2)}) collective-permute-start(bf16[64,1024]{1,0:T(8,128)(2,1)S(1)} %collective-permute-done.3.two_ref), channel_id=1, source_target_pairs={{0,2},{2,0},{4,6},{6,4},{8,10},{10,8},{12,14},{14,12},{16,18},{18,... | collective-permute-start | bytes 393224 | tf_op jit(solution)/shard_map/ppermute | solution.py:171
  43.1 0.0 copy-done.3
  43.1 0.0 copy-done.4
  43.1 0.0 copy-done.2
  43.1 0.9 %near.1 = (f32[256,512]{1,0:T(8,128)S(1)}, f32[256,512]{1,0:T(8,128)S(1)}, f32[256,512]{1,0:T(8,128)S(1)}) custom-call(bf16[256,512]{1,0:T(8,128)(2,1)S(1)} %copy-done.2, bf16[256,512]{1,0:T(8,128)(2,1)S(1)} %copy-done.3, bf16[256,512]{1,0:T(8,128)(2,1)S(1)} %copy-done.4), custom_call_target="tpu_custom_call" | custom-call | flops 134217728 | bytes 1000000 | tf_op jit(solution)/shard_map/near/pallas_call | solution.py:214
  44.0 0.0 collective-permute-done.5.one_ref
  44.0 0.0 copy-done.1
  44.0 1.2 %partial.1 = (f32[48,512]{1,0:T(8,128)S(1)}, f32[48,512]{1,0:T(8,128)S(1)}, f32[48,512]{1,0:T(8,128)S(1)}) custom-call(bf16[240,512]{1,0:T(8,128)(2,1)S(1)} %copy-done.1, bf16[64,1024]{1,0:T(8,128)(2,1)S(1)} %pack.1.own_ref, bf16[64,1024]{1,0:T(8,128)(2,1)S(1)} %collective-permute-done.5.one_ref, bf16[64,1024]{1,0:T(8,128)(2,1)S(1)} %collective-permute-done.3.two_ref), custom_call_target="tpu_custom_call" | custom-call | flops 60000000 | bytes 1000000 | tf_op jit(solution)/shard_map/partial/pallas_call | solution.py:225
  45.2 0.7 %collective-permute-done.8.kv3b_ref = bf16[64,1024]{1,0:T(8,128)(2,1)S(1)} collective-permute-done((bf16[64,1024]{1,0:T(8,128)(2,1)S(1)}, bf16[64,1024]{1,0:T(8,128)(2,1)S(1)}, u32[]{:S(2)}, u32[]{:S(2)}) %collective-permute-start.8) | collective-permute-done | bytes 131104 | tf_op jit(solution)/shard_map/ppermute | solution.py:171
  45.9 0.0 collective-permute-done.6.kv2_ref
  45.9 0.0 copy-start
  45.9 1.6 %middle.1 = (f32[256,512]{1,0:T(8,128)S(1)}, f32[256,512]{1,0:T(8,128)S(1)}, f32[256,512]{1,0:T(8,128)S(1)}) custom-call(bf16[240,512]{1,0:T(8,128)(2,1)S(1)} %copy-done.1, bf16[128,1024]{1,0:T(8,128)(2,1)S(1)} %collective-permute-done.6.kv2_ref, bf16[64,1024]{1,0:T(8,128)(2,1)S(1)} %collective-permute-done.7.kv3a_ref, ...), custom_call_target="tpu_custom_call" | custom-call | flops 300000000 | bytes 1000000 | tf_op jit(solution)/shard_map/middle/pallas_call | solution.py:222
  47.5 1.2 %collective-permute-done.4.part_ref = bf16[64,1024]{1,0:T(8,128)(2,1)S(1)} collective-permute-done((bf16[64,1024]{1,0:T(8,128)(2,1)S(1)}, bf16[64,1024]{1,0:T(8,128)(2,1)S(1)}, u32[]{:S(2)}, u32[]{:S(2)}) %collective-permute-start.4) | collective-permute-done | bytes 131104 | tf_op jit(solution)/shard_map/ppermute | solution.py:171
  48.7 0.0 copy-done
  48.7 1.2 %last.1 = (bf16[256,512]{1,0:T(8,128)(2,1)S(1)}, bf16[256,512]{1,0:T(8,128)(2,1)S(1)}) custom-call(bf16[240,512]{1,0:T(8,128)(2,1)S(1)} %copy-done.1, bf16[64,1024]{1,0:T(8,128)(2,1)S(1)} %collective-permute-done.4.part_ref, f32[48,512]{1,0:T(8,128)S(1)} %get-tuple-element.24.far_top, f32[48,512]{1,0:T(8,128)S(1)} %get-tuple-element.25.far_total, ...), custom_call_target="tpu_custom_call" | custom-call | flops 600000000 | bytes 1000000 | tf_op jit(solution)/shard_map/last/pallas_call | solution.py:228
  49.9 5.2 %collective-permute-start.9 = (bf16[256,512]{1,0:T(8,128)(2,1)S(1)}, bf16[256,512]{1,0:T(8,128)(2,1)S(1)}, u32[]{:S(2)}, u32[]{:S(2)}) collective-permute-start(bf16[256,512]{1,0:T(8,128)(2,1)S(1)} %get-tuple-element.36), channel_id=1, source_target_pairs={{0,1},{1,0},{2,3},{3,2},{4,5},{5,4},{6,7},{7,6},{8,9},{9,8},{10,11... | collective-permute-start | bytes 786440 | tf_op jit(solution)/shard_map/ppermute | solution.py:236
  55.1 0.3 mine.1
  55.4 0.8 %collective-permute-done.9 = bf16[256,512]{1,0:T(8,128)(2,1)S(1)} collective-permute-done((bf16[256,512]{1,0:T(8,128)(2,1)S(1)}, bf16[256,512]{1,0:T(8,128)(2,1)S(1)}, u32[]{:S(2)}, u32[]{:S(2)}) %collective-permute-start.9) | collective-permute-done | bytes 262176 | tf_op jit(solution)/shard_map/ppermute | solution.py:236
  56.3 0.8 %add_convert_fusion = bf16[256,512]{1,0:T(8,128)(2,1)} fusion(bf16[256,512]{1,0:T(8,128)(2,1)S(1)} %collective-permute-done.9, bf16[256,512]{1,0:T(8,128)(2,1)S(1)} %mine.1), kind=kLoop, calls=%fused_computation | loop fusion | flops 524288 | bytes 786432 | tf_op jit(solution)/shard_map/convert_element_type | solution.py:238
  (1 shorter events, 0.0 us)
Async XLA Ops:
  0.0 43.1 %copy-start.3 = (bf16[256,512]{1,0:T(8,128)(2,1)S(1)}, bf16[256,512]{1,0:T(8,128)(2,1)}, u32[]{:S(2)}) copy-start(bf16[256,512]{1,0:T(8,128)(2,1)} %k_ref.1) | copy-start | bytes 786436
  0.0 43.1 %copy-start.4 = (bf16[256,512]{1,0:T(8,128)(2,1)S(1)}, bf16[256,512]{1,0:T(8,128)(2,1)}, u32[]{:S(2)}) copy-start(bf16[256,512]{1,0:T(8,128)(2,1)} %v_ref.1) | copy-start | bytes 786436
  2.4 40.7 %copy-start.2 = (bf16[256,512]{1,0:T(8,128)(2,1)S(1)}, bf16[256,512]{1,0:T(8,128)(2,1)}, u32[]{:S(2)}) copy-start(bf16[256,512]{1,0:T(8,128)(2,1)} %q_ref.1) | copy-start | bytes 786436
  2.4 28.0 %collective-permute-start = (bf16[32,1024]{1,0:T(8,128)(2,1)}, bf16[32,1024]{1,0:T(8,128)(2,1)S(1)}, u32[]{:S(2)}, u32[]{:S(2)}) collective-permute-start(bf16[32,1024]{1,0:T(8,128)(2,1)} %get-tuple-element.22), channel_id=1, source_target_pairs={{0,8},{2,10},{4,12},{6,14},{8,0},{10,2},{12,4},{14,6},{16,24},{18,... | collective-permute-start | bytes 196616 | tf_op jit(solution)/shard_map/ppermute | solution.py:171
  12.2 17.1 %collective-permute-start.2 = (bf16[16,1024]{1,0:T(8,128)(2,1)}, bf16[16,1024]{1,0:T(8,128)(2,1)S(1)}, u32[]{:S(2)}, u32[]{:S(2)}) collective-permute-start(bf16[16,1024]{1,0:T(8,128)(2,1)} %get-tuple-element.23), channel_id=1, source_target_pairs={{0,22},{2,20},{4,18},{6,16},{8,30},{10,28},{12,26},{14,24},{16,6},... | collective-permute-start | bytes 98312 | tf_op jit(solution)/shard_map/ppermute | solution.py:171
  21.5 8.9 %collective-permute-start.1 = (bf16[16,1024]{1,0:T(8,128)(2,1)}, bf16[16,1024]{1,0:T(8,128)(2,1)S(1)}, u32[]{:S(2)}, u32[]{:S(2)}) collective-permute-start(bf16[16,1024]{1,0:T(8,128)(2,1)} %get-tuple-element.23), channel_id=1, source_target_pairs={{0,24},{2,26},{4,28},{6,30},{8,16},{10,18},{12,20},{14,22},{16,8},... | collective-permute-start | bytes 98312 | tf_op jit(solution)/shard_map/ppermute | solution.py:171
  23.5 13.7 %collective-permute-start.7 = (bf16[64,1024]{1,0:T(8,128)(2,1)}, bf16[64,1024]{1,0:T(8,128)(2,1)S(1)}, u32[]{:S(2)}, u32[]{:S(2)}) collective-permute-start(bf16[64,1024]{1,0:T(8,128)(2,1)} %get-tuple-element.28), channel_id=1, source_target_pairs={{0,4},{2,6},{4,0},{6,2},{8,12},{10,14},{12,8},{14,10},{16,20},{18,... | collective-permute-start | bytes 393224 | tf_op jit(solution)/shard_map/ppermute | solution.py:171
  27.4 18.5 %collective-permute-start.6 = (bf16[128,1024]{1,0:T(8,128)(2,1)}, bf16[128,1024]{1,0:T(8,128)(2,1)S(1)}, u32[]{:S(2)}, u32[]{:S(2)}) collective-permute-start(bf16[128,1024]{1,0:T(8,128)(2,1)} %get-tuple-element.27), channel_id=1, source_target_pairs={{0,2},{2,0},{4,6},{6,4},{8,10},{10,8},{12,14},{14,12},{16,18},{18,... | collective-permute-start | bytes 786440 | tf_op jit(solution)/shard_map/ppermute | solution.py:171
  30.4 13.6 %copy-start.1 = (bf16[240,512]{1,0:T(8,128)(2,1)S(1)}, bf16[240,512]{1,0:T(8,128)(2,1)}, u32[]{:S(2)}) copy-start(bf16[240,512]{1,0:T(8,128)(2,1)} %get-tuple-element.21.q_ref) | copy-start | bytes 737284
  30.5 10.1 %collective-permute-start.3 = (bf16[64,1024]{1,0:T(8,128)(2,1)S(1)}, bf16[64,1024]{1,0:T(8,128)(2,1)S(1)}, u32[]{:S(2)}, u32[]{:S(2)}) collective-permute-start(bf16[64,1024]{1,0:T(8,128)(2,1)S(1)} %pack.1.own_ref), channel_id=1, source_target_pairs={{0,4},{2,6},{4,0},{6,2},{8,12},{10,14},{12,8},{14,10},{16,20},{18,... | collective-permute-start | bytes 393224 | tf_op jit(solution)/shard_map/ppermute | solution.py:171
  35.2 8.8 %collective-permute-start.5 = (bf16[64,1024]{1,0:T(8,128)(2,1)S(1)}, bf16[64,1024]{1,0:T(8,128)(2,1)S(1)}, u32[]{:S(2)}, u32[]{:S(2)}) collective-permute-start(bf16[64,1024]{1,0:T(8,128)(2,1)S(1)} %pack.1.own_ref), channel_id=1, source_target_pairs={{0,2},{2,0},{4,6},{6,4},{8,10},{10,8},{12,14},{14,12},{16,18},{18,... | collective-permute-start | bytes 393224 | tf_op jit(solution)/shard_map/ppermute | solution.py:171
  37.2 8.7 %collective-permute-start.8 = (bf16[64,1024]{1,0:T(8,128)(2,1)S(1)}, bf16[64,1024]{1,0:T(8,128)(2,1)S(1)}, u32[]{:S(2)}, u32[]{:S(2)}) collective-permute-start(bf16[64,1024]{1,0:T(8,128)(2,1)S(1)} %collective-permute-done.7.kv3a_ref), channel_id=1, source_target_pairs={{0,2},{2,0},{4,6},{6,4},{8,10},{10,8},{12,14},{14,12},{16,18},{18,... | collective-permute-start | bytes 393224 | tf_op jit(solution)/shard_map/ppermute | solution.py:171
  40.6 8.2 %collective-permute-start.4 = (bf16[64,1024]{1,0:T(8,128)(2,1)S(1)}, bf16[64,1024]{1,0:T(8,128)(2,1)S(1)}, u32[]{:S(2)}, u32[]{:S(2)}) collective-permute-start(bf16[64,1024]{1,0:T(8,128)(2,1)S(1)} %collective-permute-done.3.two_ref), channel_id=1, source_target_pairs={{0,2},{2,0},{4,6},{6,4},{8,10},{10,8},{12,14},{14,12},{16,18},{18,... | collective-permute-start | bytes 393224 | tf_op jit(solution)/shard_map/ppermute | solution.py:171
  45.9 2.8 %copy-start = (bf16[512,1024]{1,0:T(8,128)(2,1)S(1)}, bf16[512,1024]{1,0:T(8,128)(2,1)}, u32[]{:S(2)}) copy-start(bf16[512,1024]{1,0:T(8,128)(2,1)} %w_ref.3) | copy-start | bytes 3145732
  49.9 6.4 %collective-permute-start.9 = (bf16[256,512]{1,0:T(8,128)(2,1)S(1)}, bf16[256,512]{1,0:T(8,128)(2,1)S(1)}, u32[]{:S(2)}, u32[]{:S(2)}) collective-permute-start(bf16[256,512]{1,0:T(8,128)(2,1)S(1)} %get-tuple-element.36), channel_id=1, source_target_pairs={{0,1},{1,0},{2,3},{3,2},{4,5},{5,4},{6,7},{7,6},{8,9},{9,8},{10,11... | collective-permute-start | bytes 786440 | tf_op jit(solution)/shard_map/ppermute | solution.py:236

commit v4 on v3

--- a/solution.py
+++ b/solution.py
@@ -66,15 +66,15 @@
     return jnp.where((col >> shift) == row, 1.0 / (1 << shift), 0.0).astype(jnp.bfloat16)
 
 
-def coarse_kernel(q_hbm, k_hbm, v_hbm, q_ref, kv2_ref, kv3_ref, kv4_ref, kv5_ref, q_in, k_in, v_in, sems):
+def coarse_kernel(k_hbm, v_hbm, kv2_ref, kv3_ref, kv4_ref, kv5_ref, k_in, v_in, sems):
     copies = [
         pltpu.make_async_copy(hbm, vmem, sems.at[turn])
-        for turn, (hbm, vmem) in enumerate(((k_hbm, k_in), (v_hbm, v_in), (q_hbm, q_in)))
+        for turn, (hbm, vmem) in enumerate(((k_hbm, k_in), (v_hbm, v_in)))
     ]
     for copy in copies:
         copy.start()
     means = jnp.concatenate([mean_matrix(256 >> shift, shift) for shift in (1, 2, 3, 4)], axis=0)
-    width = q_in.shape[1]
+    width = k_in.shape[1]
     for turn, field in enumerate((k_in, v_in)):
         copies[turn].wait()
         means_of = jnp.dot(means, field[...], preferred_element_type=jnp.float32).astype(jnp.bfloat16)
@@ -83,8 +83,11 @@
         kv3_ref[:, cols] = means_of[128:192]
         kv4_ref[:, cols] = means_of[192:224]
         kv5_ref[:, cols] = means_of[224:240]
-    copies[2].wait()
-    q_ref[...] = jnp.dot(means, q_in[...], preferred_element_type=jnp.float32).astype(jnp.bfloat16)
+
+
+def query_kernel(q_ref, coarse_ref):
+    means = jnp.concatenate([mean_matrix(256 >> shift, shift) for shift in (1, 2, 3, 4)], axis=0)
+    coarse_ref[...] = jnp.dot(means, q_ref[...], preferred_element_type=jnp.float32).astype(jnp.bfloat16)
 
 
 def pack_kernel(kv4_ref, near5_ref, far5_ref, out_ref):
@@ -93,6 +96,11 @@
     out_ref[48:64, :] = far5_ref[...]
 
 
+def pack_near_kernel(own_ref, kv3_ref, out_ref):
+    out_ref[0:64, :] = own_ref[...]
+    out_ref[64:128, :] = kv3_ref[...]
+
+
 def near_kernel(q_ref, k_ref, v_ref, top_ref, total_ref, sum_ref):
     for pair in range(4):
         cols = slice(pair * LANES, (pair + 1) * LANES)
@@ -103,15 +111,15 @@
 
 
 def middle_kernel(
-    q_ref, kv2_ref, kv3a_ref, kv3b_ref, top_in, total_in, sum_in, top_ref, total_ref, sum_ref, scratch_ref
+    q_ref, kv2_ref, kv3a_ref, one_ref, top_in, total_in, sum_in, top_ref, total_ref, sum_ref, scratch_ref
 ):
     width = q_ref.shape[1]
     for pair in range(4):
         cols = slice(pair * LANES, (pair + 1) * LANES)
         vcols = slice(width + pair * LANES, width + (pair + 1) * LANES)
         level2 = attend_pair(q_ref[:128, cols], kv2_ref[:, cols], kv2_ref[:, vcols])
-        key3 = jnp.concatenate((kv3a_ref[:, cols], kv3b_ref[:, cols]), axis=0)
-        value3 = jnp.concatenate((kv3a_ref[:, vcols], kv3b_ref[:, vcols]), axis=0)
+        key3 = jnp.concatenate((kv3a_ref[:, cols], one_ref[64:128, cols]), axis=0)
+        value3 = jnp.concatenate((kv3a_ref[:, vcols], one_ref[64:128, vcols]), axis=0)
         level3 = attend_pair(q_ref[128:192, cols], key3, value3)
         double = spread(scratch_ref, 64, 2)
         level2 = merge(level2, [double(part) for part in level3], 2.0)
@@ -128,8 +136,8 @@
     for pair in range(4):
         cols = slice(pair * LANES, (pair + 1) * LANES)
         vcols = slice(width + pair * LANES, width + (pair + 1) * LANES)
-        key = jnp.concatenate([part[:, cols] for part in parts], axis=0)
-        value = jnp.concatenate([part[:, vcols] for part in parts], axis=0)
+        key = jnp.concatenate([part[0:64, cols] for part in parts], axis=0)
+        value = jnp.concatenate([part[0:64, vcols] for part in parts], axis=0)
         top_ref[:, cols], total_ref[:, cols], sum_ref[:, cols] = attend_pair(q_ref[192:240, cols], key, value, True)
 
 
@@ -197,15 +205,16 @@
     f32, bf16 = jnp.float32, jnp.bfloat16
     shape = jax.ShapeDtypeStruct
     fields = (shape((rows, width), f32),) * 3
-    coarse_q, kv2, kv3, kv4, kv5 = call(
+    kv2, kv3, kv4, kv5 = call(
         coarse_kernel,
         "coarse",
-        (shape((240, width), bf16),) + tuple(shape((size, 2 * width), bf16) for size in (128, 64, 32, 16)),
-        [pltpu.VMEM((rows, width), bf16)] * 3 + [pltpu.SemaphoreType.DMA((3,))],
-        flops=2 * 240 * 256 * 1536,
-        in_specs=[pl.BlockSpec(memory_space=pltpu.HBM)] * 3,
+        tuple(shape((size, 2 * width), bf16) for size in (128, 64, 32, 16)),
+        [pltpu.VMEM((rows, width), bf16)] * 2 + [pltpu.SemaphoreType.DMA((2,))],
+        flops=2 * 240 * 256 * 1024,
+        in_specs=[pl.BlockSpec(memory_space=pltpu.HBM)] * 2,
         limit=63 * 1024 * 1024,
-    )(queries, key_rows, value_rows)
+    )(key_rows, value_rows)
+    coarse_q = call(query_kernel, "queries", shape((240, width), bf16), flops=2 * 240 * 256 * 512)(queries)
     far4 = moved(kv4, flip(4))
     near5 = moved(kv5, flip(12))
     far5 = moved(kv5, far_partner)
@@ -216,12 +225,12 @@
     )
     own = call(pack_kernel, "pack", shape((64, 2 * width), bf16))(far4, near5, far5)
     two = moved(own, flip(2))
-    one = moved(own, flip(1))
-    kv3b = moved(kv3a, flip(1))
+    both = call(pack_near_kernel, "pack_near", shape((128, 2 * width), bf16))(own, kv3a)
+    one = moved(both, flip(1))
     three = moved(two, flip(1))
     near = call(
         middle_kernel, "middle", fields, [pltpu.VMEM((256, LANES), f32)], flops=300_000_000, exps=8 * 256 * 200
-    )(coarse_q, kv2_got, kv3a, kv3b, *near)
+    )(coarse_q, kv2_got, kv3a, one, *near)
     far = call(partial_kernel, "partial", (shape((48, width), f32),) * 3, flops=60_000_000, exps=8 * 48 * 192)(
         coarse_q, own, one, two
     )

time: 57.4 us -> 66.6 us (1.16)
  waiting for transfers between devices: 3.83 us -> 12.6 us
    ppermute x9 -> x8, waiting for transfers between devices: 3 us -> 11.8 us  [moved(): lax.ppermute(block, 'seq', [(i, i - i % RING + partner(i % RING)) for i i...]
    ppermute x1, starting transfers between devices: 5.24 us -> 6.04 us  [body(): fetched = lax.ppermute(send, 'head', [(0, 1), (1, 0)])]
    ppermute x9 -> x8, starting transfers between devices: 39.4 us -> 39.1 us  [moved(): lax.ppermute(block, 'seq', [(i, i - i % RING + partner(i % RING)) for i i...]
    pallas_call x1 -> x3, Pallas kernels: 2.41 us -> 2.39 us  [the longest x1 2.15 us: body(): call(coarse_kernel, 'coarse', tuple((shape((size, 2 * width), bf16) for s...]
  transfers between devices with their start and end apart: 10 -> 9, of which waited for: 4 -> 4; matrix products, arithmetic and copies ran while one was open for 0% -> 0% of each run, Pallas kernels for 7% -> 6%
where the time goes in v4:
time: 66.6 us; the launch traced here: 66.2 us
  starting transfers between devices  45.1 us (68%)
  waiting for transfers between devices  12.6 us (19%)
  Pallas kernels  7.5 us (11%)
  other arithmetic  0.77 us (1%)
    ppermute x8, starting transfers between devices, moved(): lax.ppermute(block, 'seq', [(i, i - i % RING + partner(i % RING)) for i i...  39.1 us
    ppermute x8, waiting for transfers between devices, moved(): lax.ppermute(block, 'seq', [(i, i - i % RING + partner(i % RING)) for i i...  11.8 us
    ppermute x1, starting transfers between devices, body(): fetched = lax.ppermute(send, 'head', [(0, 1), (1, 0)])  6.04 us
    pallas_call x1, Pallas kernels, body(): call(coarse_kernel, 'coarse', tuple((shape((size, 2 * width), bf16) for s...  2.15 us
    pallas_call x1, Pallas kernels, body(): call(middle_kernel, 'middle', fields, [pltpu.VMEM((256, LANES), f32)], fl...  1.59 us
  transfers between devices with their start and end apart: 9, of which 4 were waited for; matrix products, arithmetic and copies ran while one was open for 0% of the time, Pallas kernels for 6%

profile of v4, /device:TPU:1, one launch (start us, length us, event | category | flops | bytes accessed | tf_op | source)
XLA Modules:
  0.0 66.2 jit_solution(10844450168931731895)
XLA Ops:
  0.0 2.1 %coarse.1 = (bf16[128,1024]{1,0:T(8,128)(2,1)}, bf16[64,1024]{1,0:T(8,128)(2,1)}, bf16[32,1024]{1,0:T(8,128)(2,1)}, bf16[16,1024]{1,0:T(8,128)(2,1)}) custom-call(bf16[256,512]{1,0:T(8,128)(2,1)} %k_ref.1, bf16[256,512]{1,0:T(8,128)(2,1)} %v_ref.1), custom_call_target="tpu_custom_call" | custom-call | flops 125829120 | bytes 1000000 | tf_op jit(solution)/shard_map/coarse/pallas_call | solution.py:208
  2.2 5.7 %collective-permute-start.5 = (bf16[64,1024]{1,0:T(8,128)(2,1)}, bf16[64,1024]{1,0:T(8,128)(2,1)S(1)}, u32[]{:S(2)}, u32[]{:S(2)}) collective-permute-start(bf16[64,1024]{1,0:T(8,128)(2,1)} %get-tuple-element.22), channel_id=1, source_target_pairs={{0,4},{2,6},{4,0},{6,2},{8,12},{10,14},{12,8},{14,10},{16,20},{18,... | collective-permute-start | bytes 393224 | tf_op jit(solution)/shard_map/ppermute | solution.py:179
  7.9 8.8 %collective-permute-start = (bf16[32,1024]{1,0:T(8,128)(2,1)}, bf16[32,1024]{1,0:T(8,128)(2,1)S(1)}, u32[]{:S(2)}, u32[]{:S(2)}) collective-permute-start(bf16[32,1024]{1,0:T(8,128)(2,1)} %get-tuple-element.20), channel_id=1, source_target_pairs={{0,8},{2,10},{4,12},{6,14},{8,0},{10,2},{12,4},{14,6},{16,24},{18,... | collective-permute-start | bytes 196616 | tf_op jit(solution)/shard_map/ppermute | solution.py:179
  16.7 7.5 %collective-permute-start.2 = (bf16[16,1024]{1,0:T(8,128)(2,1)}, bf16[16,1024]{1,0:T(8,128)(2,1)S(1)}, u32[]{:S(2)}, u32[]{:S(2)}) collective-permute-start(bf16[16,1024]{1,0:T(8,128)(2,1)} %get-tuple-element.21), channel_id=1, source_target_pairs={{0,22},{2,20},{4,18},{6,16},{8,30},{10,28},{12,26},{14,24},{16,6},... | collective-permute-start | bytes 98312 | tf_op jit(solution)/shard_map/ppermute | solution.py:179
  24.2 1.9 %collective-permute-start.1 = (bf16[16,1024]{1,0:T(8,128)(2,1)}, bf16[16,1024]{1,0:T(8,128)(2,1)S(1)}, u32[]{:S(2)}, u32[]{:S(2)}) collective-permute-start(bf16[16,1024]{1,0:T(8,128)(2,1)} %get-tuple-element.21), channel_id=1, source_target_pairs={{0,24},{2,26},{4,28},{6,30},{8,16},{10,18},{12,20},{14,22},{16,8},... | collective-permute-start | bytes 98312 | tf_op jit(solution)/shard_map/ppermute | solution.py:179
  26.1 1.8 %collective-permute-done.2.far5_ref = bf16[16,1024]{1,0:T(8,128)(2,1)S(1)} collective-permute-done((bf16[16,1024]{1,0:T(8,128)(2,1)}, bf16[16,1024]{1,0:T(8,128)(2,1)S(1)}, u32[]{:S(2)}, u32[]{:S(2)}) %collective-permute-start.2) | collective-permute-done | bytes 32800 | tf_op jit(solution)/shard_map/ppermute | solution.py:179
  27.9 5.1 %collective-permute-done.1.near5_ref = bf16[16,1024]{1,0:T(8,128)(2,1)S(1)} collective-permute-done((bf16[16,1024]{1,0:T(8,128)(2,1)}, bf16[16,1024]{1,0:T(8,128)(2,1)S(1)}, u32[]{:S(2)}, u32[]{:S(2)}) %collective-permute-start.1) | collective-permute-done | bytes 32800 | tf_op jit(solution)/shard_map/ppermute | solution.py:179
  33.0 0.0 collective-permute-done.kv4_ref
  33.0 0.0 copy-start.4
  33.0 0.0 copy-start.1
  33.0 0.0 collective-permute-done.5.kv3_ref.kv3a_ref
  33.1 0.0 copy-start.3
  33.1 0.0 copy-start.2
  33.1 3.7 %collective-permute-start.6 = (bf16[128,1024]{1,0:T(8,128)(2,1)S(1)}, bf16[128,1024]{1,0:T(8,128)(2,1)S(1)}, u32[]{:S(2)}, u32[]{:S(2)}) collective-permute-start(bf16[128,1024]{1,0:T(8,128)(2,1)S(1)} %pack_near.1), channel_id=1, source_target_pairs={{0,2},{2,0},{4,6},{6,4},{8,10},{10,8},{12,14},{14,12},{16,18},{18,... | collective-permute-start | bytes 786440 | tf_op jit(solution)/shard_map/ppermute | solution.py:179
  36.8 0.0 copy-done.4
  36.8 1.9 %collective-permute-start.7 = (bf16[128,1024]{1,0:T(8,128)(2,1)S(1)}, bf16[128,1024]{1,0:T(8,128)(2,1)S(1)}, u32[]{:S(2)}, u32[]{:S(2)}) collective-permute-start(bf16[128,1024]{1,0:T(8,128)(2,1)S(1)} %copy-done.4), channel_id=1, source_target_pairs={{0,2},{2,0},{4,6},{6,4},{8,10},{10,8},{12,14},{14,12},{16,18},{18,... | collective-permute-start | bytes 786440 | tf_op jit(solution)/shard_map/ppermute | solution.py:179
  38.7 4.5 %collective-permute-start.3 = (bf16[64,1024]{1,0:T(8,128)(2,1)S(1)}, bf16[64,1024]{1,0:T(8,128)(2,1)S(1)}, u32[]{:S(2)}, u32[]{:S(2)}) collective-permute-start(bf16[64,1024]{1,0:T(8,128)(2,1)S(1)} %pack.1.own_ref), channel_id=1, source_target_pairs={{0,4},{2,6},{4,0},{6,2},{8,12},{10,14},{12,8},{14,10},{16,20},{18,... | collective-permute-start | bytes 393224 | tf_op jit(solution)/shard_map/ppermute | solution.py:179
  43.3 4.9 %collective-permute-done.3.two_ref = bf16[64,1024]{1,0:T(8,128)(2,1)S(1)} collective-permute-done((bf16[64,1024]{1,0:T(8,128)(2,1)S(1)}, bf16[64,1024]{1,0:T(8,128)(2,1)S(1)}, u32[]{:S(2)}, u32[]{:S(2)}) %collective-permute-start.3) | collective-permute-done | bytes 131104 | tf_op jit(solution)/shard_map/ppermute | solution.py:179
  48.1 5.0 %collective-permute-start.4 = (bf16[64,1024]{1,0:T(8,128)(2,1)S(1)}, bf16[64,1024]{1,0:T(8,128)(2,1)S(1)}, u32[]{:S(2)}, u32[]{:S(2)}) collective-permute-start(bf16[64,1024]{1,0:T(8,128)(2,1)S(1)} %collective-permute-done.3.two_ref), channel_id=1, source_target_pairs={{0,2},{2,0},{4,6},{6,4},{8,10},{10,8},{12,14},{14,12},{16,18},{18,... | collective-permute-start | bytes 393224 | tf_op jit(solution)/shard_map/ppermute | solution.py:179
  53.2 0.0 copy-done.1
  53.2 0.2 queries.1.q_ref
  53.4 0.0 copy-done.3
  53.4 0.0 copy-done.2
  53.4 0.9 %near.1 = (f32[256,512]{1,0:T(8,128)S(1)}, f32[256,512]{1,0:T(8,128)S(1)}, f32[256,512]{1,0:T(8,128)S(1)}) custom-call(bf16[256,512]{1,0:T(8,128)(2,1)S(1)} %copy-done.1, bf16[256,512]{1,0:T(8,128)(2,1)S(1)} %copy-done.2, bf16[256,512]{1,0:T(8,128)(2,1)S(1)} %copy-done.3), custom_call_target="tpu_custom_call" | custom-call | flops 134217728 | bytes 1000000 | tf_op jit(solution)/shard_map/near/pallas_call | solution.py:223
  54.3 0.0 collective-permute-done.6.one_ref
  54.3 1.2 %partial.1 = (f32[48,512]{1,0:T(8,128)S(1)}, f32[48,512]{1,0:T(8,128)S(1)}, f32[48,512]{1,0:T(8,128)S(1)}) custom-call(bf16[240,512]{1,0:T(8,128)(2,1)S(1)} %queries.1.q_ref, bf16[64,1024]{1,0:T(8,128)(2,1)S(1)} %pack.1.own_ref, bf16[128,1024]{1,0:T(8,128)(2,1)S(1)} %collective-permute-done.6.one_ref, bf16[64,1024]{1,0:T(8,128)(2,1)S(1)} %collective-permute-done.3.two_ref), custom_call_target="tpu_custom_call" | custom-call | flops 60000000 | bytes 1000000 | tf_op jit(solution)/shard_map/partial/pallas_call | solution.py:234
  55.5 0.0 collective-permute-done.7.kv2_ref
  55.5 0.0 copy-start
  55.5 1.6 %middle.1 = (f32[256,512]{1,0:T(8,128)S(1)}, f32[256,512]{1,0:T(8,128)S(1)}, f32[256,512]{1,0:T(8,128)S(1)}) custom-call(bf16[240,512]{1,0:T(8,128)(2,1)S(1)} %queries.1.q_ref, bf16[128,1024]{1,0:T(8,128)(2,1)S(1)} %collective-permute-done.7.kv2_ref, bf16[64,1024]{1,0:T(8,128)(2,1)S(1)} %collective-permute-done.5.kv3_ref.kv3a_ref, ...), custom_call_target="tpu_custom_call" | custom-call | flops 300000000 | bytes 1000000 | tf_op jit(solution)/shard_map/middle/pallas_call | solution.py:231
  57.1 0.0 collective-permute-done.4.part_ref
  57.1 0.0 copy-done
  57.1 1.2 %last.1 = (bf16[256,512]{1,0:T(8,128)(2,1)S(1)}, bf16[256,512]{1,0:T(8,128)(2,1)S(1)}) custom-call(bf16[240,512]{1,0:T(8,128)(2,1)S(1)} %queries.1.q_ref, bf16[64,1024]{1,0:T(8,128)(2,1)S(1)} %collective-permute-done.4.part_ref, f32[48,512]{1,0:T(8,128)S(1)} %get-tuple-element.23.far_top, f32[48,512]{1,0:T(8,128)S(1)} %get-tuple-element.24.far_total, ...), custom_call_target="tpu_custom_call" | custom-call | flops 600000000 | bytes 1000000 | tf_op jit(solution)/shard_map/last/pallas_call | solution.py:237
  58.3 6.0 %collective-permute-start.8 = (bf16[256,512]{1,0:T(8,128)(2,1)S(1)}, bf16[256,512]{1,0:T(8,128)(2,1)S(1)}, u32[]{:S(2)}, u32[]{:S(2)}) collective-permute-start(bf16[256,512]{1,0:T(8,128)(2,1)S(1)} %get-tuple-element.34), channel_id=1, source_target_pairs={{0,1},{1,0},{2,3},{3,2},{4,5},{5,4},{6,7},{7,6},{8,9},{9,8},{10,11... | collective-permute-start | bytes 786440 | tf_op jit(solution)/shard_map/ppermute | solution.py:245
  64.3 0.3 mine.1
  64.6 0.8 %collective-permute-done.8 = bf16[256,512]{1,0:T(8,128)(2,1)S(1)} collective-permute-done((bf16[256,512]{1,0:T(8,128)(2,1)S(1)}, bf16[256,512]{1,0:T(8,128)(2,1)S(1)}, u32[]{:S(2)}, u32[]{:S(2)}) %collective-permute-start.8) | collective-permute-done | bytes 262176 | tf_op jit(solution)/shard_map/ppermute | solution.py:245
  65.5 0.8 %add_convert_fusion = bf16[256,512]{1,0:T(8,128)(2,1)} fusion(bf16[256,512]{1,0:T(8,128)(2,1)S(1)} %collective-permute-done.8, bf16[256,512]{1,0:T(8,128)(2,1)S(1)} %mine.1), kind=kLoop, calls=%fused_computation | loop fusion | flops 524288 | bytes 786432 | tf_op jit(solution)/shard_map/convert_element_type | solution.py:247
  (2 shorter events, 0.0 us)
Async XLA Ops:
  2.2 30.9 %collective-permute-start.5 = (bf16[64,1024]{1,0:T(8,128)(2,1)}, bf16[64,1024]{1,0:T(8,128)(2,1)S(1)}, u32[]{:S(2)}, u32[]{:S(2)}) collective-permute-start(bf16[64,1024]{1,0:T(8,128)(2,1)} %get-tuple-element.22), channel_id=1, source_target_pairs={{0,4},{2,6},{4,0},{6,2},{8,12},{10,14},{12,8},{14,10},{16,20},{18,... | collective-permute-start | bytes 393224 | tf_op jit(solution)/shard_map/ppermute | solution.py:179
  7.9 25.1 %collective-permute-start = (bf16[32,1024]{1,0:T(8,128)(2,1)}, bf16[32,1024]{1,0:T(8,128)(2,1)S(1)}, u32[]{:S(2)}, u32[]{:S(2)}) collective-permute-start(bf16[32,1024]{1,0:T(8,128)(2,1)} %get-tuple-element.20), channel_id=1, source_target_pairs={{0,8},{2,10},{4,12},{6,14},{8,0},{10,2},{12,4},{14,6},{16,24},{18,... | collective-permute-start | bytes 196616 | tf_op jit(solution)/shard_map/ppermute | solution.py:179
  16.7 11.2 %collective-permute-start.2 = (bf16[16,1024]{1,0:T(8,128)(2,1)}, bf16[16,1024]{1,0:T(8,128)(2,1)S(1)}, u32[]{:S(2)}, u32[]{:S(2)}) collective-permute-start(bf16[16,1024]{1,0:T(8,128)(2,1)} %get-tuple-element.21), channel_id=1, source_target_pairs={{0,22},{2,20},{4,18},{6,16},{8,30},{10,28},{12,26},{14,24},{16,6},... | collective-permute-start | bytes 98312 | tf_op jit(solution)/shard_map/ppermute | solution.py:179
  24.2 8.8 %collective-permute-start.1 = (bf16[16,1024]{1,0:T(8,128)(2,1)}, bf16[16,1024]{1,0:T(8,128)(2,1)S(1)}, u32[]{:S(2)}, u32[]{:S(2)}) collective-permute-start(bf16[16,1024]{1,0:T(8,128)(2,1)} %get-tuple-element.21), channel_id=1, source_target_pairs={{0,24},{2,26},{4,28},{6,30},{8,16},{10,18},{12,20},{14,22},{16,8},... | collective-permute-start | bytes 98312 | tf_op jit(solution)/shard_map/ppermute | solution.py:179
  33.0 3.8 %copy-start.4 = (bf16[128,1024]{1,0:T(8,128)(2,1)S(1)}, bf16[128,1024]{1,0:T(8,128)(2,1)}, u32[]{:S(2)}) copy-start(bf16[128,1024]{1,0:T(8,128)(2,1)} %get-tuple-element.26) | copy-start | bytes 786436
  33.0 20.1 %copy-start.1 = (bf16[256,512]{1,0:T(8,128)(2,1)S(1)}, bf16[256,512]{1,0:T(8,128)(2,1)}, u32[]{:S(2)}) copy-start(bf16[256,512]{1,0:T(8,128)(2,1)} %q_ref.3) | copy-start | bytes 786436
  33.1 20.3 %copy-start.3 = (bf16[256,512]{1,0:T(8,128)(2,1)S(1)}, bf16[256,512]{1,0:T(8,128)(2,1)}, u32[]{:S(2)}) copy-start(bf16[256,512]{1,0:T(8,128)(2,1)} %v_ref.1) | copy-start | bytes 786436
  33.1 20.3 %copy-start.2 = (bf16[256,512]{1,0:T(8,128)(2,1)S(1)}, bf16[256,512]{1,0:T(8,128)(2,1)}, u32[]{:S(2)}) copy-start(bf16[256,512]{1,0:T(8,128)(2,1)} %k_ref.1) | copy-start | bytes 786436
  33.1 21.2 %collective-permute-start.6 = (bf16[128,1024]{1,0:T(8,128)(2,1)S(1)}, bf16[128,1024]{1,0:T(8,128)(2,1)S(1)}, u32[]{:S(2)}, u32[]{:S(2)}) collective-permute-start(bf16[128,1024]{1,0:T(8,128)(2,1)S(1)} %pack_near.1), channel_id=1, source_target_pairs={{0,2},{2,0},{4,6},{6,4},{8,10},{10,8},{12,14},{14,12},{16,18},{18,... | collective-permute-start | bytes 786440 | tf_op jit(solution)/shard_map/ppermute | solution.py:179
  36.8 18.7 %collective-permute-start.7 = (bf16[128,1024]{1,0:T(8,128)(2,1)S(1)}, bf16[128,1024]{1,0:T(8,128)(2,1)S(1)}, u32[]{:S(2)}, u32[]{:S(2)}) collective-permute-start(bf16[128,1024]{1,0:T(8,128)(2,1)S(1)} %copy-done.4), channel_id=1, source_target_pairs={{0,2},{2,0},{4,6},{6,4},{8,10},{10,8},{12,14},{14,12},{16,18},{18,... | collective-permute-start | bytes 786440 | tf_op jit(solution)/shard_map/ppermute | solution.py:179
  38.7 9.4 %collective-permute-start.3 = (bf16[64,1024]{1,0:T(8,128)(2,1)S(1)}, bf16[64,1024]{1,0:T(8,128)(2,1)S(1)}, u32[]{:S(2)}, u32[]{:S(2)}) collective-permute-start(bf16[64,1024]{1,0:T(8,128)(2,1)S(1)} %pack.1.own_ref), channel_id=1, source_target_pairs={{0,4},{2,6},{4,0},{6,2},{8,12},{10,14},{12,8},{14,10},{16,20},{18,... | collective-permute-start | bytes 393224 | tf_op jit(solution)/shard_map/ppermute | solution.py:179
  48.1 9.0 %collective-permute-start.4 = (bf16[64,1024]{1,0:T(8,128)(2,1)S(1)}, bf16[64,1024]{1,0:T(8,128)(2,1)S(1)}, u32[]{:S(2)}, u32[]{:S(2)}) collective-permute-start(bf16[64,1024]{1,0:T(8,128)(2,1)S(1)} %collective-permute-done.3.two_ref), channel_id=1, source_target_pairs={{0,2},{2,0},{4,6},{6,4},{8,10},{10,8},{12,14},{14,12},{16,18},{18,... | collective-permute-start | bytes 393224 | tf_op jit(solution)/shard_map/ppermute | solution.py:179
  55.5 1.6 %copy-start = (bf16[512,1024]{1,0:T(8,128)(2,1)S(1)}, bf16[512,1024]{1,0:T(8,128)(2,1)}, u32[]{:S(2)}) copy-start(bf16[512,1024]{1,0:T(8,128)(2,1)} %w_ref.3) | copy-start | bytes 3145732
  58.3 7.2 %collective-permute-start.8 = (bf16[256,512]{1,0:T(8,128)(2,1)S(1)}, bf16[256,512]{1,0:T(8,128)(2,1)S(1)}, u32[]{:S(2)}, u32[]{:S(2)}) collective-permute-start(bf16[256,512]{1,0:T(8,128)(2,1)S(1)} %get-tuple-element.34), channel_id=1, source_target_pairs={{0,1},{1,0},{2,3},{3,2},{4,5},{5,4},{6,7},{7,6},{8,9},{9,8},{10,11... | collective-permute-start | bytes 786440 | tf_op jit(solution)/shard_map/ppermute | solution.py:245

commit v5 on v3

--- a/solution.py
+++ b/solution.py
@@ -66,25 +66,38 @@
     return jnp.where((col >> shift) == row, 1.0 / (1 << shift), 0.0).astype(jnp.bfloat16)
 
 
-def coarse_kernel(q_hbm, k_hbm, v_hbm, q_ref, kv2_ref, kv3_ref, kv4_ref, kv5_ref, q_in, k_in, v_in, sems):
-    copies = [
-        pltpu.make_async_copy(hbm, vmem, sems.at[turn])
-        for turn, (hbm, vmem) in enumerate(((k_hbm, k_in), (v_hbm, v_in), (q_hbm, q_in)))
-    ]
-    for copy in copies:
-        copy.start()
+def coarse_kernel(k_hbm, v_hbm, *rest):
+    outs, held, (k_in, v_in, in_sems, out_sems) = rest[:4], rest[4:8], rest[8:]
+    rows, width = k_in.shape
+    half = rows // 2
+    loads = []
+    for turn, (hbm, vmem) in enumerate(((k_hbm, k_in), (v_hbm, v_in))):
+        for part in range(2):
+            place = pl.ds(part * half, half)
+            loads.append(pltpu.make_async_copy(hbm.at[place], vmem.at[place], in_sems.at[2 * turn + part]))
+    for load in loads:
+        load.start()
     means = jnp.concatenate([mean_matrix(256 >> shift, shift) for shift in (1, 2, 3, 4)], axis=0)
-    width = q_in.shape[1]
+    stores = []
     for turn, field in enumerate((k_in, v_in)):
-        copies[turn].wait()
+        loads[2 * turn].wait()
+        loads[2 * turn + 1].wait()
         means_of = jnp.dot(means, field[...], preferred_element_type=jnp.float32).astype(jnp.bfloat16)
-        cols = slice(turn * width, (turn + 1) * width)
-        kv2_ref[:, cols] = means_of[:128]
-        kv3_ref[:, cols] = means_of[128:192]
-        kv4_ref[:, cols] = means_of[192:224]
-        kv5_ref[:, cols] = means_of[224:240]
-    copies[2].wait()
-    q_ref[...] = jnp.dot(means, q_in[...], preferred_element_type=jnp.float32).astype(jnp.bfloat16)
+        cols = pl.ds(turn * width, width)
+        for level, (first, size) in enumerate(((0, 128), (128, 64), (192, 32), (224, 16))):
+            held[level][:, cols] = means_of[first : first + size]
+            store = pltpu.make_async_copy(
+                held[level].at[:, cols], outs[level].at[:, cols], out_sems.at[4 * turn + level]
+            )
+            store.start()
+            stores.append(store)
+    for store in stores:
+        store.wait()
+
+
+def query_kernel(q_ref, coarse_ref):
+    means = jnp.concatenate([mean_matrix(256 >> shift, shift) for shift in (1, 2, 3, 4)], axis=0)
+    coarse_ref[...] = jnp.dot(means, q_ref[...], preferred_element_type=jnp.float32).astype(jnp.bfloat16)
 
 
 def pack_kernel(kv4_ref, near5_ref, far5_ref, out_ref):
@@ -179,8 +192,7 @@
     return 11 - place if place // 4 in (0, 2) else 19 - place
 
 
-def call(kernel, name, outs, scratch=(), flops=0, moved_bytes=1_000_000, exps=0, in_specs=None, limit=VMEM_LIMIT):
-    given = {} if in_specs is None else {"in_specs": in_specs}
+def call(kernel, name, outs, scratch=(), flops=0, moved_bytes=1_000_000, exps=0, limit=VMEM_LIMIT, **given):
     return pl.pallas_call(
         kernel,
         out_shape=outs,
@@ -197,15 +209,21 @@
     f32, bf16 = jnp.float32, jnp.bfloat16
     shape = jax.ShapeDtypeStruct
     fields = (shape((rows, width), f32),) * 3
-    coarse_q, kv2, kv3, kv4, kv5 = call(
+    sizes = (128, 64, 32, 16)
+    hbm = pl.BlockSpec(memory_space=pltpu.HBM)
+    kv2, kv3, kv4, kv5 = call(
         coarse_kernel,
         "coarse",
-        (shape((240, width), bf16),) + tuple(shape((size, 2 * width), bf16) for size in (128, 64, 32, 16)),
-        [pltpu.VMEM((rows, width), bf16)] * 3 + [pltpu.SemaphoreType.DMA((3,))],
-        flops=2 * 240 * 256 * 1536,
-        in_specs=[pl.BlockSpec(memory_space=pltpu.HBM)] * 3,
+        tuple(shape((size, 2 * width), bf16) for size in sizes),
+        [pltpu.VMEM((size, 2 * width), bf16) for size in sizes]
+        + [pltpu.VMEM((rows, width), bf16)] * 2
+        + [pltpu.SemaphoreType.DMA((4,)), pltpu.SemaphoreType.DMA((8,))],
+        flops=2 * 240 * 256 * 1024,
+        in_specs=(hbm, hbm),
+        out_specs=(hbm,) * 4,
         limit=63 * 1024 * 1024,
-    )(queries, key_rows, value_rows)
+    )(key_rows, value_rows)
+    coarse_q = call(query_kernel, "queries", shape((240, width), bf16), flops=2 * 240 * 256 * 512)(queries)
     far4 = moved(kv4, flip(4))
     near5 = moved(kv5, flip(12))
     far5 = moved(kv5, far_partner)

time: 57.4 us -> 57.2 us (level)
    pallas_call x1 -> x2, Pallas kernels: 2.41 us -> 2.45 us  [the longest x1 2.24 us: body(): call(coarse_kernel, 'coarse', tuple((shape((size, 2 * width), bf16) for s...]
where the time goes in v5:
time: 57.2 us; the launch traced here: 56.8 us
  starting transfers between devices  44.7 us (78%)
  Pallas kernels  7.56 us (13%)
  waiting for transfers between devices  3.62 us (6%)
  other arithmetic  0.77 us (1%)
    ppermute x9, starting transfers between devices, moved(): lax.ppermute(block, 'seq', [(i, i - i % RING + partner(i % RING)) for i i...  39.4 us
    ppermute x1, starting transfers between devices, body(): fetched = lax.ppermute(send, 'head', [(0, 1), (1, 0)])  5.22 us
    ppermute x9, waiting for transfers between devices, moved(): lax.ppermute(block, 'seq', [(i, i - i % RING + partner(i % RING)) for i i...  2.79 us
    pallas_call x1, Pallas kernels, body(): call(coarse_kernel, 'coarse', tuple((shape((size, 2 * width), bf16) for s...  2.24 us
    pallas_call x1, Pallas kernels, body(): call(middle_kernel, 'middle', fields, [pltpu.VMEM((256, LANES), f32)], fl...  1.58 us
    pallas_call x1, Pallas kernels, body(): call(partial_kernel, 'partial', (shape((48, width), f32),) * 3, flops=600...  1.15 us
    pallas_call x1, Pallas kernels, body(): call(last_kernel, 'last', (shape((rows, width), bf16),) * 2, ([pltpu.VMEM...  1.15 us
  transfers between devices with their start and end apart: 10, of which 4 were waited for; matrix products, arithmetic and copies ran while one was open for 0% of the time, Pallas kernels for 7%

profile of v5, /device:TPU:1, one launch (start us, length us, event | category | flops | bytes accessed | tf_op | source)
XLA Modules:
  0.0 56.8 jit_solution(17527281604714455267)
XLA Ops:
  0.0 0.0 copy-start.3
  0.0 2.2 %coarse.1 = (bf16[128,1024]{1,0:T(8,128)(2,1)}, bf16[64,1024]{1,0:T(8,128)(2,1)}, bf16[32,1024]{1,0:T(8,128)(2,1)}, bf16[16,1024]{1,0:T(8,128)(2,1)}) custom-call(bf16[256,512]{1,0:T(8,128)(2,1)} %k_ref.1, bf16[256,512]{1,0:T(8,128)(2,1)} %v_ref.1), custom_call_target="tpu_custom_call" | custom-call | flops 125829120 | bytes 1000000 | tf_op jit(solution)/shard_map/coarse/pallas_call | solution.py:214
  2.2 0.0 copy-start.1
  2.3 9.8 %collective-permute-start = (bf16[32,1024]{1,0:T(8,128)(2,1)}, bf16[32,1024]{1,0:T(8,128)(2,1)S(1)}, u32[]{:S(2)}, u32[]{:S(2)}) collective-permute-start(bf16[32,1024]{1,0:T(8,128)(2,1)} %get-tuple-element.20), channel_id=1, source_target_pairs={{0,8},{2,10},{4,12},{6,14},{8,0},{10,2},{12,4},{14,6},{16,24},{18,... | collective-permute-start | bytes 196616 | tf_op jit(solution)/shard_map/ppermute | solution.py:184
  12.0 9.3 %collective-permute-start.2 = (bf16[16,1024]{1,0:T(8,128)(2,1)}, bf16[16,1024]{1,0:T(8,128)(2,1)S(1)}, u32[]{:S(2)}, u32[]{:S(2)}) collective-permute-start(bf16[16,1024]{1,0:T(8,128)(2,1)} %get-tuple-element.21), channel_id=1, source_target_pairs={{0,22},{2,20},{4,18},{6,16},{8,30},{10,28},{12,26},{14,24},{16,6},... | collective-permute-start | bytes 98312 | tf_op jit(solution)/shard_map/ppermute | solution.py:184
  21.4 1.9 %collective-permute-start.1 = (bf16[16,1024]{1,0:T(8,128)(2,1)}, bf16[16,1024]{1,0:T(8,128)(2,1)S(1)}, u32[]{:S(2)}, u32[]{:S(2)}) collective-permute-start(bf16[16,1024]{1,0:T(8,128)(2,1)} %get-tuple-element.21), channel_id=1, source_target_pairs={{0,24},{2,26},{4,28},{6,30},{8,16},{10,18},{12,20},{14,22},{16,8},... | collective-permute-start | bytes 98312 | tf_op jit(solution)/shard_map/ppermute | solution.py:184
  23.3 4.0 %collective-permute-start.7 = (bf16[64,1024]{1,0:T(8,128)(2,1)}, bf16[64,1024]{1,0:T(8,128)(2,1)S(1)}, u32[]{:S(2)}, u32[]{:S(2)}) collective-permute-start(bf16[64,1024]{1,0:T(8,128)(2,1)} %get-tuple-element.26), channel_id=1, source_target_pairs={{0,4},{2,6},{4,0},{6,2},{8,12},{10,14},{12,8},{14,10},{16,20},{18,... | collective-permute-start | bytes 393224 | tf_op jit(solution)/shard_map/ppermute | solution.py:184
  27.3 1.9 %collective-permute-start.6 = (bf16[128,1024]{1,0:T(8,128)(2,1)}, bf16[128,1024]{1,0:T(8,128)(2,1)S(1)}, u32[]{:S(2)}, u32[]{:S(2)}) collective-permute-start(bf16[128,1024]{1,0:T(8,128)(2,1)} %get-tuple-element.25), channel_id=1, source_target_pairs={{0,2},{2,0},{4,6},{6,4},{8,10},{10,8},{12,14},{14,12},{16,18},{18,... | collective-permute-start | bytes 786440 | tf_op jit(solution)/shard_map/ppermute | solution.py:184
  29.2 0.0 collective-permute-done.2.far5_ref
  29.2 1.0 %collective-permute-done.1.near5_ref = bf16[16,1024]{1,0:T(8,128)(2,1)S(1)} collective-permute-done((bf16[16,1024]{1,0:T(8,128)(2,1)}, bf16[16,1024]{1,0:T(8,128)(2,1)S(1)}, u32[]{:S(2)}, u32[]{:S(2)}) %collective-permute-start.1) | collective-permute-done | bytes 32800 | tf_op jit(solution)/shard_map/ppermute | solution.py:184
  30.2 0.0 collective-permute-done.kv4_ref
  30.3 0.0 copy-start.2
  30.3 4.8 %collective-permute-start.3 = (bf16[64,1024]{1,0:T(8,128)(2,1)S(1)}, bf16[64,1024]{1,0:T(8,128)(2,1)S(1)}, u32[]{:S(2)}, u32[]{:S(2)}) collective-permute-start(bf16[64,1024]{1,0:T(8,128)(2,1)S(1)} %pack.1.own_ref), channel_id=1, source_target_pairs={{0,4},{2,6},{4,0},{6,2},{8,12},{10,14},{12,8},{14,10},{16,20},{18,... | collective-permute-start | bytes 393224 | tf_op jit(solution)/shard_map/ppermute | solution.py:184
  35.1 1.9 %collective-permute-start.5 = (bf16[64,1024]{1,0:T(8,128)(2,1)S(1)}, bf16[64,1024]{1,0:T(8,128)(2,1)S(1)}, u32[]{:S(2)}, u32[]{:S(2)}) collective-permute-start(bf16[64,1024]{1,0:T(8,128)(2,1)S(1)} %pack.1.own_ref), channel_id=1, source_target_pairs={{0,2},{2,0},{4,6},{6,4},{8,10},{10,8},{12,14},{14,12},{16,18},{18,... | collective-permute-start | bytes 393224 | tf_op jit(solution)/shard_map/ppermute | solution.py:184
  37.0 0.0 collective-permute-done.7.kv3a_ref
  37.0 3.4 %collective-permute-start.8 = (bf16[64,1024]{1,0:T(8,128)(2,1)S(1)}, bf16[64,1024]{1,0:T(8,128)(2,1)S(1)}, u32[]{:S(2)}, u32[]{:S(2)}) collective-permute-start(bf16[64,1024]{1,0:T(8,128)(2,1)S(1)} %collective-permute-done.7.kv3a_ref), channel_id=1, source_target_pairs={{0,2},{2,0},{4,6},{6,4},{8,10},{10,8},{12,14},{14,12},{16,18},{18,... | collective-permute-start | bytes 393224 | tf_op jit(solution)/shard_map/ppermute | solution.py:184
  40.4 0.0 collective-permute-done.3.two_ref
  40.4 2.5 %collective-permute-start.4 = (bf16[64,1024]{1,0:T(8,128)(2,1)S(1)}, bf16[64,1024]{1,0:T(8,128)(2,1)S(1)}, u32[]{:S(2)}, u32[]{:S(2)}) collective-permute-start(bf16[64,1024]{1,0:T(8,128)(2,1)S(1)} %collective-permute-done.3.two_ref), channel_id=1, source_target_pairs={{0,2},{2,0},{4,6},{6,4},{8,10},{10,8},{12,14},{14,12},{16,18},{18,... | collective-permute-start | bytes 393224 | tf_op jit(solution)/shard_map/ppermute | solution.py:184
  42.9 0.0 copy-done.1
  42.9 0.2 queries.1.q_ref
  43.1 0.0 copy-done.3
  43.1 0.0 copy-done.2
  43.1 0.9 %near.1 = (f32[256,512]{1,0:T(8,128)S(1)}, f32[256,512]{1,0:T(8,128)S(1)}, f32[256,512]{1,0:T(8,128)S(1)}) custom-call(bf16[256,512]{1,0:T(8,128)(2,1)S(1)} %copy-done.1, bf16[256,512]{1,0:T(8,128)(2,1)S(1)} %copy-done.2, bf16[256,512]{1,0:T(8,128)(2,1)S(1)} %copy-done.3), custom_call_target="tpu_custom_call" | custom-call | flops 134217728 | bytes 1000000 | tf_op jit(solution)/shard_map/near/pallas_call | solution.py:232
  44.0 0.0 collective-permute-done.5.one_ref
  44.0 1.2 %partial.1 = (f32[48,512]{1,0:T(8,128)S(1)}, f32[48,512]{1,0:T(8,128)S(1)}, f32[48,512]{1,0:T(8,128)S(1)}) custom-call(bf16[240,512]{1,0:T(8,128)(2,1)S(1)} %queries.1.q_ref, bf16[64,1024]{1,0:T(8,128)(2,1)S(1)} %pack.1.own_ref, bf16[64,1024]{1,0:T(8,128)(2,1)S(1)} %collective-permute-done.5.one_ref, bf16[64,1024]{1,0:T(8,128)(2,1)S(1)} %collective-permute-done.3.two_ref), custom_call_target="tpu_custom_call" | custom-call | flops 60000000 | bytes 1000000 | tf_op jit(solution)/shard_map/partial/pallas_call | solution.py:243
  45.2 0.5 collective-permute-done.8.kv3b_ref
  45.7 0.0 collective-permute-done.6.kv2_ref
  45.7 0.0 copy-start
  45.7 1.6 %middle.1 = (f32[256,512]{1,0:T(8,128)S(1)}, f32[256,512]{1,0:T(8,128)S(1)}, f32[256,512]{1,0:T(8,128)S(1)}) custom-call(bf16[240,512]{1,0:T(8,128)(2,1)S(1)} %queries.1.q_ref, bf16[128,1024]{1,0:T(8,128)(2,1)S(1)} %collective-permute-done.6.kv2_ref, bf16[64,1024]{1,0:T(8,128)(2,1)S(1)} %collective-permute-done.7.kv3a_ref, ...), custom_call_target="tpu_custom_call" | custom-call | flops 300000000 | bytes 1000000 | tf_op jit(solution)/shard_map/middle/pallas_call | solution.py:240
  47.3 1.2 %collective-permute-done.4.part_ref = bf16[64,1024]{1,0:T(8,128)(2,1)S(1)} collective-permute-done((bf16[64,1024]{1,0:T(8,128)(2,1)S(1)}, bf16[64,1024]{1,0:T(8,128)(2,1)S(1)}, u32[]{:S(2)}, u32[]{:S(2)}) %collective-permute-start.4) | collective-permute-done | bytes 131104 | tf_op jit(solution)/shard_map/ppermute | solution.py:184
  48.5 0.0 copy-done
  48.5 1.2 %last.1 = (bf16[256,512]{1,0:T(8,128)(2,1)S(1)}, bf16[256,512]{1,0:T(8,128)(2,1)S(1)}) custom-call(bf16[240,512]{1,0:T(8,128)(2,1)S(1)} %queries.1.q_ref, bf16[64,1024]{1,0:T(8,128)(2,1)S(1)} %collective-permute-done.4.part_ref, f32[48,512]{1,0:T(8,128)S(1)} %get-tuple-element.22.far_top, f32[48,512]{1,0:T(8,128)S(1)} %get-tuple-element.23.far_total, ...), custom_call_target="tpu_custom_call" | custom-call | flops 600000000 | bytes 1000000 | tf_op jit(solution)/shard_map/last/pallas_call | solution.py:246
  49.7 5.2 %collective-permute-start.9 = (bf16[256,512]{1,0:T(8,128)(2,1)S(1)}, bf16[256,512]{1,0:T(8,128)(2,1)S(1)}, u32[]{:S(2)}, u32[]{:S(2)}) collective-permute-start(bf16[256,512]{1,0:T(8,128)(2,1)S(1)} %get-tuple-element.34), channel_id=1, source_target_pairs={{0,1},{1,0},{2,3},{3,2},{4,5},{5,4},{6,7},{7,6},{8,9},{9,8},{10,11... | collective-permute-start | bytes 786440 | tf_op jit(solution)/shard_map/ppermute | solution.py:254
  54.9 0.3 mine.1
  55.2 0.8 %collective-permute-done.9 = bf16[256,512]{1,0:T(8,128)(2,1)S(1)} collective-permute-done((bf16[256,512]{1,0:T(8,128)(2,1)S(1)}, bf16[256,512]{1,0:T(8,128)(2,1)S(1)}, u32[]{:S(2)}, u32[]{:S(2)}) %collective-permute-start.9) | collective-permute-done | bytes 262176 | tf_op jit(solution)/shard_map/ppermute | solution.py:254
  56.1 0.8 %add_convert_fusion = bf16[256,512]{1,0:T(8,128)(2,1)} fusion(bf16[256,512]{1,0:T(8,128)(2,1)S(1)} %collective-permute-done.9, bf16[256,512]{1,0:T(8,128)(2,1)S(1)} %mine.1), kind=kLoop, calls=%fused_computation | loop fusion | flops 524288 | bytes 786432 | tf_op jit(solution)/shard_map/convert_element_type | solution.py:256
  (1 shorter events, 0.0 us)
Async XLA Ops:
  0.0 43.1 %copy-start.3 = (bf16[256,512]{1,0:T(8,128)(2,1)S(1)}, bf16[256,512]{1,0:T(8,128)(2,1)}, u32[]{:S(2)}) copy-start(bf16[256,512]{1,0:T(8,128)(2,1)} %v_ref.1) | copy-start | bytes 786436
  2.2 40.6 %copy-start.1 = (bf16[256,512]{1,0:T(8,128)(2,1)S(1)}, bf16[256,512]{1,0:T(8,128)(2,1)}, u32[]{:S(2)}) copy-start(bf16[256,512]{1,0:T(8,128)(2,1)} %q_ref.3) | copy-start | bytes 786436
  2.3 28.0 %collective-permute-start = (bf16[32,1024]{1,0:T(8,128)(2,1)}, bf16[32,1024]{1,0:T(8,128)(2,1)S(1)}, u32[]{:S(2)}, u32[]{:S(2)}) collective-permute-start(bf16[32,1024]{1,0:T(8,128)(2,1)} %get-tuple-element.20), channel_id=1, source_target_pairs={{0,8},{2,10},{4,12},{6,14},{8,0},{10,2},{12,4},{14,6},{16,24},{18,... | collective-permute-start | bytes 196616 | tf_op jit(solution)/shard_map/ppermute | solution.py:184
  12.0 17.1 %collective-permute-start.2 = (bf16[16,1024]{1,0:T(8,128)(2,1)}, bf16[16,1024]{1,0:T(8,128)(2,1)S(1)}, u32[]{:S(2)}, u32[]{:S(2)}) collective-permute-start(bf16[16,1024]{1,0:T(8,128)(2,1)} %get-tuple-element.21), channel_id=1, source_target_pairs={{0,22},{2,20},{4,18},{6,16},{8,30},{10,28},{12,26},{14,24},{16,6},... | collective-permute-start | bytes 98312 | tf_op jit(solution)/shard_map/ppermute | solution.py:184
  21.4 8.9 %collective-permute-start.1 = (bf16[16,1024]{1,0:T(8,128)(2,1)}, bf16[16,1024]{1,0:T(8,128)(2,1)S(1)}, u32[]{:S(2)}, u32[]{:S(2)}) collective-permute-start(bf16[16,1024]{1,0:T(8,128)(2,1)} %get-tuple-element.21), channel_id=1, source_target_pairs={{0,24},{2,26},{4,28},{6,30},{8,16},{10,18},{12,20},{14,22},{16,8},... | collective-permute-start | bytes 98312 | tf_op jit(solution)/shard_map/ppermute | solution.py:184
  23.3 13.7 %collective-permute-start.7 = (bf16[64,1024]{1,0:T(8,128)(2,1)}, bf16[64,1024]{1,0:T(8,128)(2,1)S(1)}, u32[]{:S(2)}, u32[]{:S(2)}) collective-permute-start(bf16[64,1024]{1,0:T(8,128)(2,1)} %get-tuple-element.26), channel_id=1, source_target_pairs={{0,4},{2,6},{4,0},{6,2},{8,12},{10,14},{12,8},{14,10},{16,20},{18,... | collective-permute-start | bytes 393224 | tf_op jit(solution)/shard_map/ppermute | solution.py:184
  27.3 18.5 %collective-permute-start.6 = (bf16[128,1024]{1,0:T(8,128)(2,1)}, bf16[128,1024]{1,0:T(8,128)(2,1)S(1)}, u32[]{:S(2)}, u32[]{:S(2)}) collective-permute-start(bf16[128,1024]{1,0:T(8,128)(2,1)} %get-tuple-element.25), channel_id=1, source_target_pairs={{0,2},{2,0},{4,6},{6,4},{8,10},{10,8},{12,14},{14,12},{16,18},{18,... | collective-permute-start | bytes 786440 | tf_op jit(solution)/shard_map/ppermute | solution.py:184
  30.3 12.9 %copy-start.2 = (bf16[256,512]{1,0:T(8,128)(2,1)S(1)}, bf16[256,512]{1,0:T(8,128)(2,1)}, u32[]{:S(2)}) copy-start(bf16[256,512]{1,0:T(8,128)(2,1)} %k_ref.1) | copy-start | bytes 786436
  30.3 10.1 %collective-permute-start.3 = (bf16[64,1024]{1,0:T(8,128)(2,1)S(1)}, bf16[64,1024]{1,0:T(8,128)(2,1)S(1)}, u32[]{:S(2)}, u32[]{:S(2)}) collective-permute-start(bf16[64,1024]{1,0:T(8,128)(2,1)S(1)} %pack.1.own_ref), channel_id=1, source_target_pairs={{0,4},{2,6},{4,0},{6,2},{8,12},{10,14},{12,8},{14,10},{16,20},{18,... | collective-permute-start | bytes 393224 | tf_op jit(solution)/shard_map/ppermute | solution.py:184
  35.1 9.0 %collective-permute-start.5 = (bf16[64,1024]{1,0:T(8,128)(2,1)S(1)}, bf16[64,1024]{1,0:T(8,128)(2,1)S(1)}, u32[]{:S(2)}, u32[]{:S(2)}) collective-permute-start(bf16[64,1024]{1,0:T(8,128)(2,1)S(1)} %pack.1.own_ref), channel_id=1, source_target_pairs={{0,2},{2,0},{4,6},{6,4},{8,10},{10,8},{12,14},{14,12},{16,18},{18,... | collective-permute-start | bytes 393224 | tf_op jit(solution)/shard_map/ppermute | solution.py:184
  37.0 8.7 %collective-permute-start.8 = (bf16[64,1024]{1,0:T(8,128)(2,1)S(1)}, bf16[64,1024]{1,0:T(8,128)(2,1)S(1)}, u32[]{:S(2)}, u32[]{:S(2)}) collective-permute-start(bf16[64,1024]{1,0:T(8,128)(2,1)S(1)} %collective-permute-done.7.kv3a_ref), channel_id=1, source_target_pairs={{0,2},{2,0},{4,6},{6,4},{8,10},{10,8},{12,14},{14,12},{16,18},{18,... | collective-permute-start | bytes 393224 | tf_op jit(solution)/shard_map/ppermute | solution.py:184
  40.4 8.2 %collective-permute-start.4 = (bf16[64,1024]{1,0:T(8,128)(2,1)S(1)}, bf16[64,1024]{1,0:T(8,128)(2,1)S(1)}, u32[]{:S(2)}, u32[]{:S(2)}) collective-permute-start(bf16[64,1024]{1,0:T(8,128)(2,1)S(1)} %collective-permute-done.3.two_ref), channel_id=1, source_target_pairs={{0,2},{2,0},{4,6},{6,4},{8,10},{10,8},{12,14},{14,12},{16,18},{18,... | collective-permute-start | bytes 393224 | tf_op jit(solution)/shard_map/ppermute | solution.py:184
  45.7 2.8 %copy-start = (bf16[512,1024]{1,0:T(8,128)(2,1)S(1)}, bf16[512,1024]{1,0:T(8,128)(2,1)}, u32[]{:S(2)}) copy-start(bf16[512,1024]{1,0:T(8,128)(2,1)} %w_ref.3) | copy-start | bytes 3145732
  49.7 6.4 %collective-permute-start.9 = (bf16[256,512]{1,0:T(8,128)(2,1)S(1)}, bf16[256,512]{1,0:T(8,128)(2,1)S(1)}, u32[]{:S(2)}, u32[]{:S(2)}) collective-permute-start(bf16[256,512]{1,0:T(8,128)(2,1)S(1)} %get-tuple-element.34), channel_id=1, source_target_pairs={{0,1},{1,0},{2,3},{3,2},{4,5},{5,4},{6,7},{7,6},{8,9},{9,8},{10,11... | collective-permute-start | bytes 786440 | tf_op jit(solution)/shard_map/ppermute | solution.py:254

commit v6 on v3

--- a/solution.py
+++ b/solution.py
@@ -87,7 +87,7 @@
     q_ref[...] = jnp.dot(means, q_in[...], preferred_element_type=jnp.float32).astype(jnp.bfloat16)
 
 
-def pack_kernel(kv4_ref, near5_ref, far5_ref, out_ref):
+def pack_kernel(kv4_ref, near5_ref, far5_ref, after_ref, out_ref):
     out_ref[0:32, :] = kv4_ref[...]
     out_ref[32:48, :] = near5_ref[...]
     out_ref[48:64, :] = far5_ref[...]
@@ -214,7 +214,10 @@
     near = call(near_kernel, "near", fields, flops=8 * 256 * 256 * 64 * 4, exps=8 * 256 * 256)(
         queries, key_rows, value_rows
     )
-    own = call(pack_kernel, "pack", shape((64, 2 * width), bf16))(far4, near5, far5)
+    whole, anywhere = pl.BlockSpec(memory_space=pltpu.VMEM), pl.BlockSpec(memory_space=pl.ANY)
+    own = call(
+        pack_kernel, "pack", shape((64, 2 * width), bf16), in_specs=(whole, whole, whole, anywhere)
+    )(far4, near5, far5, near[0])
     two = moved(own, flip(2))
     one = moved(own, flip(1))
     kv3b = moved(kv3a, flip(1))

time: 57.4 us -> 57.3 us (level)
  no operation moved by 1% of the time
where the time goes in v6:
time: 57.3 us; the launch traced here: 56.9 us
  starting transfers between devices  44.6 us (78%)
  Pallas kernels  7.52 us (13%)
  waiting for transfers between devices  3.77 us (7%)
  other arithmetic  0.77 us (1%)
    ppermute x9, starting transfers between devices, moved(): lax.ppermute(block, 'seq', [(i, i - i % RING + partner(i % RING)) for i i...  39.4 us
    ppermute x1, starting transfers between devices, body(): fetched = lax.ppermute(send, 'head', [(0, 1), (1, 0)])  5.22 us
    ppermute x9, waiting for transfers between devices, moved(): lax.ppermute(block, 'seq', [(i, i - i % RING + partner(i % RING)) for i i...  2.95 us
    pallas_call x1, Pallas kernels, body(): call(coarse_kernel, 'coarse', (shape((240, width), bf16),) + tuple((shape...  2.41 us
    pallas_call x1, Pallas kernels, body(): call(middle_kernel, 'middle', fields, [pltpu.VMEM((256, LANES), f32)], fl...  1.58 us
    pallas_call x1, Pallas kernels, body(): call(partial_kernel, 'partial', (shape((48, width), f32),) * 3, flops=600...  1.15 us
    pallas_call x1, Pallas kernels, body(): call(last_kernel, 'last', (shape((rows, width), bf16),) * 2, ([pltpu.VMEM...  1.15 us
  transfers between devices with their start and end apart: 10, of which 4 were waited for; matrix products, arithmetic and copies ran while one was open for 0% of the time, Pallas kernels for 7%

profile of v6, /device:TPU:1, one launch (start us, length us, event | category | flops | bytes accessed | tf_op | source)
XLA Modules:
  0.0 56.9 jit_solution(15326351730484000726)
XLA Ops:
  0.0 0.0 copy-start.4
  0.0 0.0 copy-start.3
  0.0 0.0 copy-start.2
  0.0 2.4 %coarse.1 = (bf16[240,512]{1,0:T(8,128)(2,1)}, bf16[128,1024]{1,0:T(8,128)(2,1)}, bf16[64,1024]{1,0:T(8,128)(2,1)}, bf16[32,1024]{1,0:T(8,128)(2,1)}, bf16[16,1024]{1,0:T(8,128)(2,1)}) custom-call(bf16[256,512]{1,0:T(8,128)(2,1)} %q_ref.1, bf16[256,512]{1,0:T(8,128)(2,1)} %k_ref.1, bf16[256,512]{1,0:T(8,128)(2,1)} %v_ref.1), custom_call_target="tpu_custom_call" | custom-call | flops 188743680 | bytes 1000000 | tf_op jit(solution)/shard_map/coarse/pallas_call | solution.py:200
  2.4 9.6 %collective-permute-start = (bf16[32,1024]{1,0:T(8,128)(2,1)}, bf16[32,1024]{1,0:T(8,128)(2,1)S(1)}, u32[]{:S(2)}, u32[]{:S(2)}) collective-permute-start(bf16[32,1024]{1,0:T(8,128)(2,1)} %get-tuple-element.22), channel_id=1, source_target_pairs={{0,8},{2,10},{4,12},{6,14},{8,0},{10,2},{12,4},{14,6},{16,24},{18,... | collective-permute-start | bytes 196616 | tf_op jit(solution)/shard_map/ppermute | solution.py:171
  12.1 9.3 %collective-permute-start.2 = (bf16[16,1024]{1,0:T(8,128)(2,1)}, bf16[16,1024]{1,0:T(8,128)(2,1)S(1)}, u32[]{:S(2)}, u32[]{:S(2)}) collective-permute-start(bf16[16,1024]{1,0:T(8,128)(2,1)} %get-tuple-element.23), channel_id=1, source_target_pairs={{0,22},{2,20},{4,18},{6,16},{8,30},{10,28},{12,26},{14,24},{16,6},... | collective-permute-start | bytes 98312 | tf_op jit(solution)/shard_map/ppermute | solution.py:171
  21.4 1.9 %collective-permute-start.1 = (bf16[16,1024]{1,0:T(8,128)(2,1)}, bf16[16,1024]{1,0:T(8,128)(2,1)S(1)}, u32[]{:S(2)}, u32[]{:S(2)}) collective-permute-start(bf16[16,1024]{1,0:T(8,128)(2,1)} %get-tuple-element.23), channel_id=1, source_target_pairs={{0,24},{2,26},{4,28},{6,30},{8,16},{10,18},{12,20},{14,22},{16,8},... | collective-permute-start | bytes 98312 | tf_op jit(solution)/shard_map/ppermute | solution.py:171
  23.3 4.0 %collective-permute-start.7 = (bf16[64,1024]{1,0:T(8,128)(2,1)}, bf16[64,1024]{1,0:T(8,128)(2,1)S(1)}, u32[]{:S(2)}, u32[]{:S(2)}) collective-permute-start(bf16[64,1024]{1,0:T(8,128)(2,1)} %get-tuple-element.29), channel_id=1, source_target_pairs={{0,4},{2,6},{4,0},{6,2},{8,12},{10,14},{12,8},{14,10},{16,20},{18,... | collective-permute-start | bytes 393224 | tf_op jit(solution)/shard_map/ppermute | solution.py:171
  27.3 1.9 %collective-permute-start.6 = (bf16[128,1024]{1,0:T(8,128)(2,1)}, bf16[128,1024]{1,0:T(8,128)(2,1)S(1)}, u32[]{:S(2)}, u32[]{:S(2)}) collective-permute-start(bf16[128,1024]{1,0:T(8,128)(2,1)} %get-tuple-element.28), channel_id=1, source_target_pairs={{0,2},{2,0},{4,6},{6,4},{8,10},{10,8},{12,14},{14,12},{16,18},{18,... | collective-permute-start | bytes 786440 | tf_op jit(solution)/shard_map/ppermute | solution.py:171
  29.3 0.0 copy-done.4
  29.3 0.0 copy-done.3
  29.3 0.0 copy-done.2
  29.3 0.9 %near.1 = (f32[256,512]{1,0:T(8,128)S(1)}, f32[256,512]{1,0:T(8,128)S(1)}, f32[256,512]{1,0:T(8,128)S(1)}) custom-call(bf16[256,512]{1,0:T(8,128)(2,1)S(1)} %copy-done.2, bf16[256,512]{1,0:T(8,128)(2,1)S(1)} %copy-done.3, bf16[256,512]{1,0:T(8,128)(2,1)S(1)} %copy-done.4), custom_call_target="tpu_custom_call" | custom-call | flops 134217728 | bytes 1000000 | tf_op jit(solution)/shard_map/near/pallas_call | solution.py:214
  30.2 0.0 collective-permute-done.2.far5_ref
  30.2 0.0 collective-permute-done.1.near5_ref
  30.2 0.0 collective-permute-done.kv4_ref
  30.2 0.0 copy-start.1
  30.2 4.9 %collective-permute-start.3 = (bf16[64,1024]{1,0:T(8,128)(2,1)S(1)}, bf16[64,1024]{1,0:T(8,128)(2,1)S(1)}, u32[]{:S(2)}, u32[]{:S(2)}) collective-permute-start(bf16[64,1024]{1,0:T(8,128)(2,1)S(1)} %pack.1.own_ref), channel_id=1, source_target_pairs={{0,4},{2,6},{4,0},{6,2},{8,12},{10,14},{12,8},{14,10},{16,20},{18,... | collective-permute-start | bytes 393224 | tf_op jit(solution)/shard_map/ppermute | solution.py:171
  35.2 1.9 %collective-permute-start.5 = (bf16[64,1024]{1,0:T(8,128)(2,1)S(1)}, bf16[64,1024]{1,0:T(8,128)(2,1)S(1)}, u32[]{:S(2)}, u32[]{:S(2)}) collective-permute-start(bf16[64,1024]{1,0:T(8,128)(2,1)S(1)} %pack.1.own_ref), channel_id=1, source_target_pairs={{0,2},{2,0},{4,6},{6,4},{8,10},{10,8},{12,14},{14,12},{16,18},{18,... | collective-permute-start | bytes 393224 | tf_op jit(solution)/shard_map/ppermute | solution.py:171
  37.1 0.0 collective-permute-done.7.kv3a_ref
  37.1 3.4 %collective-permute-start.8 = (bf16[64,1024]{1,0:T(8,128)(2,1)S(1)}, bf16[64,1024]{1,0:T(8,128)(2,1)S(1)}, u32[]{:S(2)}, u32[]{:S(2)}) collective-permute-start(bf16[64,1024]{1,0:T(8,128)(2,1)S(1)} %collective-permute-done.7.kv3a_ref), channel_id=1, source_target_pairs={{0,2},{2,0},{4,6},{6,4},{8,10},{10,8},{12,14},{14,12},{16,18},{18,... | collective-permute-start | bytes 393224 | tf_op jit(solution)/shard_map/ppermute | solution.py:171
  40.5 0.0 collective-permute-done.3.two_ref
  40.5 2.4 %collective-permute-start.4 = (bf16[64,1024]{1,0:T(8,128)(2,1)S(1)}, bf16[64,1024]{1,0:T(8,128)(2,1)S(1)}, u32[]{:S(2)}, u32[]{:S(2)}) collective-permute-start(bf16[64,1024]{1,0:T(8,128)(2,1)S(1)} %collective-permute-done.3.two_ref), channel_id=1, source_target_pairs={{0,2},{2,0},{4,6},{6,4},{8,10},{10,8},{12,14},{14,12},{16,18},{18,... | collective-permute-start | bytes 393224 | tf_op jit(solution)/shard_map/ppermute | solution.py:171
  42.9 0.4 collective-permute-done.5.one_ref
  43.3 0.0 copy-done.1
  43.4 1.2 %partial.1 = (f32[48,512]{1,0:T(8,128)S(1)}, f32[48,512]{1,0:T(8,128)S(1)}, f32[48,512]{1,0:T(8,128)S(1)}) custom-call(bf16[240,512]{1,0:T(8,128)(2,1)S(1)} %copy-done.1, bf16[64,1024]{1,0:T(8,128)(2,1)S(1)} %pack.1.own_ref, bf16[64,1024]{1,0:T(8,128)(2,1)S(1)} %collective-permute-done.5.one_ref, bf16[64,1024]{1,0:T(8,128)(2,1)S(1)} %collective-permute-done.3.two_ref), custom_call_target="tpu_custom_call" | custom-call | flops 60000000 | bytes 1000000 | tf_op jit(solution)/shard_map/partial/pallas_call | solution.py:228
  44.5 1.3 %collective-permute-done.8.kv3b_ref = bf16[64,1024]{1,0:T(8,128)(2,1)S(1)} collective-permute-done((bf16[64,1024]{1,0:T(8,128)(2,1)S(1)}, bf16[64,1024]{1,0:T(8,128)(2,1)S(1)}, u32[]{:S(2)}, u32[]{:S(2)}) %collective-permute-start.8) | collective-permute-done | bytes 131104 | tf_op jit(solution)/shard_map/ppermute | solution.py:171
  45.8 0.0 collective-permute-done.6.kv2_ref
  45.8 0.0 copy-start
  45.8 1.6 %middle.1 = (f32[256,512]{1,0:T(8,128)S(1)}, f32[256,512]{1,0:T(8,128)S(1)}, f32[256,512]{1,0:T(8,128)S(1)}) custom-call(bf16[240,512]{1,0:T(8,128)(2,1)S(1)} %copy-done.1, bf16[128,1024]{1,0:T(8,128)(2,1)S(1)} %collective-permute-done.6.kv2_ref, bf16[64,1024]{1,0:T(8,128)(2,1)S(1)} %collective-permute-done.7.kv3a_ref, ...), custom_call_target="tpu_custom_call" | custom-call | flops 300000000 | bytes 1000000 | tf_op jit(solution)/shard_map/middle/pallas_call | solution.py:225
  47.4 1.2 %collective-permute-done.4.part_ref = bf16[64,1024]{1,0:T(8,128)(2,1)S(1)} collective-permute-done((bf16[64,1024]{1,0:T(8,128)(2,1)S(1)}, bf16[64,1024]{1,0:T(8,128)(2,1)S(1)}, u32[]{:S(2)}, u32[]{:S(2)}) %collective-permute-start.4) | collective-permute-done | bytes 131104 | tf_op jit(solution)/shard_map/ppermute | solution.py:171
  48.6 0.0 copy-done
  48.6 1.2 %last.1 = (bf16[256,512]{1,0:T(8,128)(2,1)S(1)}, bf16[256,512]{1,0:T(8,128)(2,1)S(1)}) custom-call(bf16[240,512]{1,0:T(8,128)(2,1)S(1)} %copy-done.1, bf16[64,1024]{1,0:T(8,128)(2,1)S(1)} %collective-permute-done.4.part_ref, f32[48,512]{1,0:T(8,128)S(1)} %get-tuple-element.25.far_top, f32[48,512]{1,0:T(8,128)S(1)} %get-tuple-element.26.far_total, ...), custom_call_target="tpu_custom_call" | custom-call | flops 600000000 | bytes 1000000 | tf_op jit(solution)/shard_map/last/pallas_call | solution.py:231
  49.8 5.2 %collective-permute-start.9 = (bf16[256,512]{1,0:T(8,128)(2,1)S(1)}, bf16[256,512]{1,0:T(8,128)(2,1)S(1)}, u32[]{:S(2)}, u32[]{:S(2)}) collective-permute-start(bf16[256,512]{1,0:T(8,128)(2,1)S(1)} %get-tuple-element.36), channel_id=1, source_target_pairs={{0,1},{1,0},{2,3},{3,2},{4,5},{5,4},{6,7},{7,6},{8,9},{9,8},{10,11... | collective-permute-start | bytes 786440 | tf_op jit(solution)/shard_map/ppermute | solution.py:239
  55.0 0.3 mine.1
  55.3 0.8 %collective-permute-done.9 = bf16[256,512]{1,0:T(8,128)(2,1)S(1)} collective-permute-done((bf16[256,512]{1,0:T(8,128)(2,1)S(1)}, bf16[256,512]{1,0:T(8,128)(2,1)S(1)}, u32[]{:S(2)}, u32[]{:S(2)}) %collective-permute-start.9) | collective-permute-done | bytes 262176 | tf_op jit(solution)/shard_map/ppermute | solution.py:239
  56.1 0.8 %add_convert_fusion = bf16[256,512]{1,0:T(8,128)(2,1)} fusion(bf16[256,512]{1,0:T(8,128)(2,1)S(1)} %collective-permute-done.9, bf16[256,512]{1,0:T(8,128)(2,1)S(1)} %mine.1), kind=kLoop, calls=%fused_computation | loop fusion | flops 524288 | bytes 786432 | tf_op jit(solution)/shard_map/convert_element_type | solution.py:241
  (1 shorter events, 0.0 us)
Async XLA Ops:
  0.0 29.3 %copy-start.4 = (bf16[256,512]{1,0:T(8,128)(2,1)S(1)}, bf16[256,512]{1,0:T(8,128)(2,1)}, u32[]{:S(2)}) copy-start(bf16[256,512]{1,0:T(8,128)(2,1)} %v_ref.1) | copy-start | bytes 786436
  0.0 29.3 %copy-start.3 = (bf16[256,512]{1,0:T(8,128)(2,1)S(1)}, bf16[256,512]{1,0:T(8,128)(2,1)}, u32[]{:S(2)}) copy-start(bf16[256,512]{1,0:T(8,128)(2,1)} %k_ref.1) | copy-start | bytes 786436
  0.0 29.3 %copy-start.2 = (bf16[256,512]{1,0:T(8,128)(2,1)S(1)}, bf16[256,512]{1,0:T(8,128)(2,1)}, u32[]{:S(2)}) copy-start(bf16[256,512]{1,0:T(8,128)(2,1)} %q_ref.1) | copy-start | bytes 786436
  2.4 27.8 %collective-permute-start = (bf16[32,1024]{1,0:T(8,128)(2,1)}, bf16[32,1024]{1,0:T(8,128)(2,1)S(1)}, u32[]{:S(2)}, u32[]{:S(2)}) collective-permute-start(bf16[32,1024]{1,0:T(8,128)(2,1)} %get-tuple-element.22), channel_id=1, source_target_pairs={{0,8},{2,10},{4,12},{6,14},{8,0},{10,2},{12,4},{14,6},{16,24},{18,... | collective-permute-start | bytes 196616 | tf_op jit(solution)/shard_map/ppermute | solution.py:171
  12.1 18.1 %collective-permute-start.2 = (bf16[16,1024]{1,0:T(8,128)(2,1)}, bf16[16,1024]{1,0:T(8,128)(2,1)S(1)}, u32[]{:S(2)}, u32[]{:S(2)}) collective-permute-start(bf16[16,1024]{1,0:T(8,128)(2,1)} %get-tuple-element.23), channel_id=1, source_target_pairs={{0,22},{2,20},{4,18},{6,16},{8,30},{10,28},{12,26},{14,24},{16,6},... | collective-permute-start | bytes 98312 | tf_op jit(solution)/shard_map/ppermute | solution.py:171
  21.4 8.8 %collective-permute-start.1 = (bf16[16,1024]{1,0:T(8,128)(2,1)}, bf16[16,1024]{1,0:T(8,128)(2,1)S(1)}, u32[]{:S(2)}, u32[]{:S(2)}) collective-permute-start(bf16[16,1024]{1,0:T(8,128)(2,1)} %get-tuple-element.23), channel_id=1, source_target_pairs={{0,24},{2,26},{4,28},{6,30},{8,16},{10,18},{12,20},{14,22},{16,8},... | collective-permute-start | bytes 98312 | tf_op jit(solution)/shard_map/ppermute | solution.py:171
  23.3 13.8 %collective-permute-start.7 = (bf16[64,1024]{1,0:T(8,128)(2,1)}, bf16[64,1024]{1,0:T(8,128)(2,1)S(1)}, u32[]{:S(2)}, u32[]{:S(2)}) collective-permute-start(bf16[64,1024]{1,0:T(8,128)(2,1)} %get-tuple-element.29), channel_id=1, source_target_pairs={{0,4},{2,6},{4,0},{6,2},{8,12},{10,14},{12,8},{14,10},{16,20},{18,... | collective-permute-start | bytes 393224 | tf_op jit(solution)/shard_map/ppermute | solution.py:171
  27.3 18.5 %collective-permute-start.6 = (bf16[128,1024]{1,0:T(8,128)(2,1)}, bf16[128,1024]{1,0:T(8,128)(2,1)S(1)}, u32[]{:S(2)}, u32[]{:S(2)}) collective-permute-start(bf16[128,1024]{1,0:T(8,128)(2,1)} %get-tuple-element.28), channel_id=1, source_target_pairs={{0,2},{2,0},{4,6},{6,4},{8,10},{10,8},{12,14},{14,12},{16,18},{18,... | collective-permute-start | bytes 786440 | tf_op jit(solution)/shard_map/ppermute | solution.py:171
  30.2 13.1 %copy-start.1 = (bf16[240,512]{1,0:T(8,128)(2,1)S(1)}, bf16[240,512]{1,0:T(8,128)(2,1)}, u32[]{:S(2)}) copy-start(bf16[240,512]{1,0:T(8,128)(2,1)} %get-tuple-element.21.q_ref) | copy-start | bytes 737284
  30.2 10.3 %collective-permute-start.3 = (bf16[64,1024]{1,0:T(8,128)(2,1)S(1)}, bf16[64,1024]{1,0:T(8,128)(2,1)S(1)}, u32[]{:S(2)}, u32[]{:S(2)}) collective-permute-start(bf16[64,1024]{1,0:T(8,128)(2,1)S(1)} %pack.1.own_ref), channel_id=1, source_target_pairs={{0,4},{2,6},{4,0},{6,2},{8,12},{10,14},{12,8},{14,10},{16,20},{18,... | collective-permute-start | bytes 393224 | tf_op jit(solution)/shard_map/ppermute | solution.py:171
  35.2 8.1 %collective-permute-start.5 = (bf16[64,1024]{1,0:T(8,128)(2,1)S(1)}, bf16[64,1024]{1,0:T(8,128)(2,1)S(1)}, u32[]{:S(2)}, u32[]{:S(2)}) collective-permute-start(bf16[64,1024]{1,0:T(8,128)(2,1)S(1)} %pack.1.own_ref), channel_id=1, source_target_pairs={{0,2},{2,0},{4,6},{6,4},{8,10},{10,8},{12,14},{14,12},{16,18},{18,... | collective-permute-start | bytes 393224 | tf_op jit(solution)/shard_map/ppermute | solution.py:171
  37.1 8.7 %collective-permute-start.8 = (bf16[64,1024]{1,0:T(8,128)(2,1)S(1)}, bf16[64,1024]{1,0:T(8,128)(2,1)S(1)}, u32[]{:S(2)}, u32[]{:S(2)}) collective-permute-start(bf16[64,1024]{1,0:T(8,128)(2,1)S(1)} %collective-permute-done.7.kv3a_ref), channel_id=1, source_target_pairs={{0,2},{2,0},{4,6},{6,4},{8,10},{10,8},{12,14},{14,12},{16,18},{18,... | collective-permute-start | bytes 393224 | tf_op jit(solution)/shard_map/ppermute | solution.py:171
  40.5 8.1 %collective-permute-start.4 = (bf16[64,1024]{1,0:T(8,128)(2,1)S(1)}, bf16[64,1024]{1,0:T(8,128)(2,1)S(1)}, u32[]{:S(2)}, u32[]{:S(2)}) collective-permute-start(bf16[64,1024]{1,0:T(8,128)(2,1)S(1)} %collective-permute-done.3.two_ref), channel_id=1, source_target_pairs={{0,2},{2,0},{4,6},{6,4},{8,10},{10,8},{12,14},{14,12},{16,18},{18,... | collective-permute-start | bytes 393224 | tf_op jit(solution)/shard_map/ppermute | solution.py:171
  45.8 2.8 %copy-start = (bf16[512,1024]{1,0:T(8,128)(2,1)S(1)}, bf16[512,1024]{1,0:T(8,128)(2,1)}, u32[]{:S(2)}) copy-start(bf16[512,1024]{1,0:T(8,128)(2,1)} %w_ref.3) | copy-start | bytes 3145732
  49.8 6.4 %collective-permute-start.9 = (bf16[256,512]{1,0:T(8,128)(2,1)S(1)}, bf16[256,512]{1,0:T(8,128)(2,1)S(1)}, u32[]{:S(2)}, u32[]{:S(2)}) collective-permute-start(bf16[256,512]{1,0:T(8,128)(2,1)S(1)} %get-tuple-element.36), channel_id=1, source_target_pairs={{0,1},{1,0},{2,3},{3,2},{4,5},{5,4},{6,7},{7,6},{8,9},{9,8},{10,11... | collective-permute-start | bytes 786440 | tf_op jit(solution)/shard_map/ppermute | solution.py:239
